TPU v7x, 32 devices: a whole 2x2x4 slice. The times are simulated.
32 devices in a mesh: dp: 16 (over z, y, x), tensor: 2 (over core).
Axes of the slice: x: 2, y: 2, z: 4, core: 2. Of those that a mesh axis runs over, the one named last changes fastest.
Arguments:
- tokens: bfloat16 [50176, 768], P(('dp', 'tensor')), may hold values from -6 to 6
- cotangent: bfloat16 [50176, 768], P(('dp', 'tensor')), may hold values from -6 to 6
- attn_qkv: bfloat16 [1, 2, 768, 3, 768], P(None, None, 'dp', None, 'tensor'), may hold values from -0.21875 to 0.21875
- attn_out: bfloat16 [1, 2, 768, 768], P(None, None, 'tensor', 'dp'), may hold values from -0.875 to 0.875
- mlp_in: bfloat16 [1, 768, 3072], P(None, 'dp', 'tensor'), may hold values from -0.21875 to 0.21875
- mlp_out: bfloat16 [1, 3072, 768], P(None, 'tensor', 'dp'), may hold values from -0.109375 to 0.109375
- norm_gains: float32 [1, 3, 768], P(None, None, ('dp', 'tensor')), may hold values from 0.5 to 1.5
- biases: float32 [1, 10, 768], P(None, None, ('dp', 'tensor')), may hold values from -4 to 4
- hidden_bias: float32 [1, 3072], P(None, ('dp', 'tensor')), may hold values from -6 to 6
Outputs:
- output: bfloat16 [50176, 768], P(('dp', 'tensor'))
- grad_tokens: float32 [50176, 768], P(('dp', 'tensor'))
- grad_attn_qkv: float32 [1, 2, 768, 3, 768], P(None, None, 'dp', None, 'tensor')
- grad_attn_out: float32 [1, 2, 768, 768], P(None, None, 'tensor', 'dp')
- grad_mlp_in: float32 [1, 768, 3072], P(None, 'dp', 'tensor')
- grad_mlp_out: float32 [1, 3072, 768], P(None, 'tensor', 'dp')
- grad_norm_gains: float32 [1, 3, 768], P(None, None, ('dp', 'tensor'))
- grad_biases: float32 [1, 10, 768], P(None, None, ('dp', 'tensor'))
- grad_hidden_bias: float32 [1, 3072], P(None, ('dp', 'tensor'))
All inputs are finite; a program needn't handle non-finite values.
Results may differ from a plain program's by a relative error of at most 0.023.
Values may be sent and summed in bfloat16 or wider, within the bound.
A program may use at most 320 MiB of HBM per device.

v0:
```python
import jax
import jax.numpy as jnp
from jax import lax
from jax.sharding import PartitionSpec as P

HEAD = 64
FRAMES = 16
PATCHES = 196


EPSILON = 1e-06
SCORE_FORMS = (
    ("cfphe,cfqhe->cfhpq", "cfhpq,cfqhe->cfphe", "cfhpq,cfphe->cfqhe", -1),
    ("cfphe,cgphe->chfgp", "chfgp,cgphe->cfphe", "chfgp,cfphe->cgphe", -2),
)


def layer_norm(stream, gain_row, shift_row):
    row_mean = jnp.mean(stream, axis=-1, keepdims=True)
    centred = stream - row_mean
    variance = jnp.mean(centred * centred, axis=-1, keepdims=True)
    return centred * lax.rsqrt(variance + EPSILON) * gain_row + shift_row


def to_heads(row_block):
    clip_count = row_block.shape[0] // (FRAMES * PATCHES)
    return row_block.reshape(clip_count, FRAMES, PATCHES, row_block.shape[1] // HEAD, HEAD)


def gelu_exact(pre_act):
    return jax.nn.gelu(pre_act, approximate=False)


def gather_rows(normed_b):
    return lax.all_gather(normed_b, "tensor", axis=0, tiled=True)


def reduce_rows(partial_value):
    return lax.psum_scatter(
        partial_value.astype(jnp.bfloat16), "tensor", scatter_dimension=0, tiled=True
    ).astype(jnp.float32)


def gather_grads(upstream_b):
    return lax.all_gather(upstream_b, "tensor", axis=0, tiled=True)


def reduce_grads(partial_value):
    return lax.psum_scatter(
        partial_value.astype(jnp.bfloat16), "tensor", scatter_dimension=0, tiled=True
    ).astype(jnp.float32)


def fetch_weights(attn_qkv, attn_out, mlp_in, mlp_out, layer_index):
    return (
        lax.all_gather(attn_qkv[layer_index], "dp", axis=1, tiled=True),
        lax.all_gather(attn_out[layer_index], "dp", axis=2, tiled=True),
        lax.all_gather(mlp_in[layer_index], "dp", axis=0, tiled=True),
        lax.all_gather(mlp_out[layer_index], "dp", axis=1, tiled=True),
    )


def fetch_vectors(norm_gains, biases, hidden_bias, layer_index):
    return (
        lax.all_gather(norm_gains[layer_index], ("dp", "tensor"), axis=1, tiled=True),
        lax.all_gather(biases[layer_index], ("dp", "tensor"), axis=1, tiled=True),
        lax.all_gather(hidden_bias[layer_index], ("dp", "tensor"), axis=0, tiled=True),
    )


def own_cols(vector, col_width):
    return lax.dynamic_slice_in_dim(vector, lax.axis_index("tensor") * col_width, col_width, 0)


def place_cols(vector, full_width):
    zeros_full = jnp.zeros((full_width,), jnp.float32)
    return lax.dynamic_update_slice_in_dim(
        zeros_full, vector, lax.axis_index("tensor") * vector.shape[0], 0
    )


def attend_heads(queries, key_rows, values, sub_kind):
    score_form, out_form, _, soft_axis = SCORE_FORMS[sub_kind]
    scores = jnp.einsum(
        score_form, to_heads(queries), to_heads(key_rows), preferred_element_type=jnp.float32
    )
    attn_probs = jax.nn.softmax(scores * HEAD ** (-0.5), axis=soft_axis)
    mixture = jnp.einsum(
        out_form,
        attn_probs.astype(jnp.bfloat16),
        to_heads(values),
        preferred_element_type=jnp.float32,
    )
    return mixture.reshape(queries.shape)


def attend_back(queries, key_rows, values, grad_mix, sub_kind):
    score_form, out_form, value_form, soft_axis = SCORE_FORMS[sub_kind]
    head_query = to_heads(queries)
    head_key = to_heads(key_rows)
    head_value = to_heads(values)
    head_grad = to_heads(grad_mix)
    scores = jnp.einsum(score_form, head_query, head_key, preferred_element_type=jnp.float32)
    attn_probs = jax.nn.softmax(scores * HEAD ** (-0.5), axis=soft_axis)
    grad_probs = jnp.einsum(score_form, head_grad, head_value, preferred_element_type=jnp.float32)
    grad_value = jnp.einsum(
        value_form, attn_probs.astype(jnp.bfloat16), head_grad, preferred_element_type=jnp.float32
    )
    inner = jnp.sum(grad_probs * attn_probs, axis=soft_axis, keepdims=True)
    grad_scores = (attn_probs * (grad_probs - inner)).astype(jnp.bfloat16)
    grad_query = jnp.einsum(
        out_form, grad_scores, head_key, preferred_element_type=jnp.float32
    ) * HEAD ** (-0.5)
    grad_key = jnp.einsum(
        value_form, grad_scores, head_query, preferred_element_type=jnp.float32
    ) * HEAD ** (-0.5)
    return (
        grad_query.reshape(queries.shape).astype(jnp.bfloat16),
        grad_key.reshape(queries.shape).astype(jnp.bfloat16),
        grad_value.reshape(queries.shape).astype(jnp.bfloat16),
    )


def attention_forward(stream, sub_kind, weights, vectors):
    w_qkv = weights[0][sub_kind]
    w_out = weights[1][sub_kind]
    gain_all, bias_all, _ = vectors
    col_width = w_qkv.shape[2]
    row_base = 4 * sub_kind
    normed = layer_norm(stream, gain_all[sub_kind], bias_all[row_base])
    gathered = gather_rows(normed.astype(jnp.bfloat16))
    projected = jnp.einsum("rd,dkc->rkc", gathered, w_qkv, preferred_element_type=jnp.float32)
    queries = (projected[:, 0] + own_cols(bias_all[row_base + 1], col_width)).astype(jnp.bfloat16)
    key_rows = projected[:, 1].astype(jnp.bfloat16)
    values = (projected[:, 2] + own_cols(bias_all[row_base + 2], col_width)).astype(jnp.bfloat16)
    mixture = attend_heads(queries, key_rows, values, sub_kind).astype(jnp.bfloat16)
    summed = reduce_rows(jnp.dot(mixture, w_out, preferred_element_type=jnp.float32))
    return (
        stream + summed + bias_all[row_base + 3],
        (stream, gathered, queries, key_rows, values, mixture),
    )


def attention_backward(upstream, stored, sub_kind, weights, vectors):
    stream, gathered, queries, key_rows, values, mixture = stored
    w_qkv = weights[0][sub_kind]
    w_out = weights[1][sub_kind]
    gain_all, bias_all, _ = vectors
    row_base = 4 * sub_kind
    gathered_grad = gather_grads(upstream.astype(jnp.bfloat16))
    grad_out = jnp.einsum("rc,rd->cd", mixture, gathered_grad, preferred_element_type=jnp.float32)
    grad_mix = jnp.einsum(
        "rd,cd->rc", gathered_grad, w_out, preferred_element_type=jnp.float32
    ).astype(jnp.bfloat16)
    grad_query, grad_key, grad_value = attend_back(queries, key_rows, values, grad_mix, sub_kind)
    grad_proj = jnp.stack([grad_query, grad_key, grad_value], axis=1)
    grad_qkv = jnp.einsum("rd,rkc->dkc", gathered, grad_proj, preferred_element_type=jnp.float32)
    grad_heads = jnp.sum(grad_proj, axis=0, dtype=jnp.float32)
    grad_normed = reduce_grads(
        jnp.einsum("rkc,dkc->rd", grad_proj, w_qkv, preferred_element_type=jnp.float32)
    )
    _, pullback = jax.vjp(layer_norm, stream, gain_all[sub_kind], bias_all[row_base])
    grad_stream, grad_gain, grad_shift = pullback(grad_normed)
    full_width = bias_all.shape[1]
    small_grads = (
        grad_gain,
        grad_shift,
        place_cols(grad_heads[0], full_width),
        place_cols(grad_heads[2], full_width),
        jnp.sum(upstream, axis=0),
    )
    return (upstream + grad_stream, grad_qkv, grad_out, small_grads)


def mlp_forward(stream, weights, vectors):
    w_in = weights[2]
    w_down = weights[3]
    gain_all, bias_all, hidden_all = vectors
    normed = layer_norm(stream, gain_all[2], bias_all[8])
    gathered = gather_rows(normed.astype(jnp.bfloat16))
    pre_act = jnp.dot(gathered, w_in, preferred_element_type=jnp.float32) + own_cols(
        hidden_all, w_in.shape[1]
    )
    act_b = gelu_exact(pre_act).astype(jnp.bfloat16)
    summed = reduce_rows(jnp.dot(act_b, w_down, preferred_element_type=jnp.float32))
    return (stream + summed + bias_all[9], (stream, gathered, pre_act, act_b))


def mlp_backward(upstream, stored, weights, vectors):
    stream, gathered, pre_act, act_b = stored
    w_in = weights[2]
    w_down = weights[3]
    gain_all, bias_all, hidden_all = vectors
    gathered_grad = gather_grads(upstream.astype(jnp.bfloat16))
    grad_down = jnp.einsum("ru,rd->ud", act_b, gathered_grad, preferred_element_type=jnp.float32)
    grad_act = jnp.einsum("rd,ud->ru", gathered_grad, w_down, preferred_element_type=jnp.float32)
    grad_act = lax.optimization_barrier(grad_act.astype(jnp.bfloat16)).astype(jnp.float32)
    _, gelu_pull = jax.vjp(gelu_exact, pre_act)
    grad_pre = gelu_pull(grad_act)[0].astype(jnp.bfloat16)
    grad_in = jnp.einsum("rd,ru->du", gathered, grad_pre, preferred_element_type=jnp.float32)
    grad_units = jnp.sum(grad_pre, axis=0, dtype=jnp.float32)
    grad_normed = reduce_grads(
        jnp.einsum("ru,du->rd", grad_pre, w_in, preferred_element_type=jnp.float32)
    )
    _, pullback = jax.vjp(layer_norm, stream, gain_all[2], bias_all[8])
    grad_stream, grad_gain, grad_shift = pullback(grad_normed)
    small_grads = (
        grad_gain,
        grad_shift,
        place_cols(grad_units, hidden_all.shape[0]),
        jnp.sum(upstream, axis=0),
    )
    return (upstream + grad_stream, grad_in, grad_down, small_grads)


def layer_forward(stream, weights, vectors):
    stored = []
    for sub_kind in range(2):
        stream, kept_now = attention_forward(stream, sub_kind, weights, vectors)
        stored.append(kept_now)
    stream, kept_now = mlp_forward(stream, weights, vectors)
    stored.append(kept_now)
    return (stream, stored)


def layer_backward(upstream, stored, weights, vectors):
    upstream, grad_in, grad_down, small_mlp = mlp_backward(upstream, stored[2], weights, vectors)
    upstream, qkv_later, out_later, small_later = attention_backward(
        upstream, stored[1], 1, weights, vectors
    )
    upstream, qkv_first, out_first, small_first = attention_backward(
        upstream, stored[0], 0, weights, vectors
    )
    grad_qkv = jnp.stack([qkv_first, qkv_later])
    grad_out = jnp.stack([out_first, out_later])
    grad_gains = jnp.stack([small_first[0], small_later[0], small_mlp[0]])
    grad_biases = jnp.stack(
        [
            small_first[1],
            small_first[2],
            small_first[3],
            small_first[4],
            small_later[1],
            small_later[2],
            small_later[3],
            small_later[4],
            small_mlp[1],
            small_mlp[3],
        ]
    )
    return (
        upstream,
        (grad_qkv, grad_out, grad_in, grad_down),
        (grad_gains, grad_biases, small_mlp[2]),
    )


def shards(tokens, cotangent, attn_qkv, attn_out, mlp_in, mlp_out, norm_gains, biases, hidden_bias):
    layer_count = attn_qkv.shape[0]
    stream = tokens.astype(jnp.float32)
    fetched = []
    stored_all = []
    layer_index = 0
    weights = fetch_weights(attn_qkv, attn_out, mlp_in, mlp_out, layer_index)
    vectors = fetch_vectors(norm_gains, biases, hidden_bias, layer_index)
    inputs = [stream]
    fetched.append((weights, vectors))
    stream, stored_now = layer_forward(stream, weights, vectors)
    stored_all.append(stored_now)
    output = stream.astype(jnp.bfloat16)
    upstream = cotangent.astype(jnp.float32)
    matrix_grads = [None] * layer_count
    vector_grads = [None] * layer_count
    for layer_index in reversed(range(layer_count)):
        weights = fetch_weights(attn_qkv, attn_out, mlp_in, mlp_out, layer_index)
        vectors = fetch_vectors(norm_gains, biases, hidden_bias, layer_index)
        _, stored = layer_forward(inputs[layer_index], weights, vectors)
        upstream, layer_mats, layer_vecs = layer_backward(upstream, stored, weights, vectors)
        matrix_grads[layer_index] = layer_mats
        vector_grads[layer_index] = layer_vecs
    stacked_qkv = jnp.stack([member[0] for member in matrix_grads])
    stacked_out = jnp.stack([member[1] for member in matrix_grads])
    stacked_in = jnp.stack([member[2] for member in matrix_grads])
    stacked_down = jnp.stack([member[3] for member in matrix_grads])
    stacked_gains = jnp.stack([member[0] for member in vector_grads])
    stacked_biases = jnp.stack([member[1] for member in vector_grads])
    stacked_hidden = jnp.stack([member[2] for member in vector_grads])
    stacked_qkv, stacked_out, stacked_in, stacked_down = (
        lax.psum_scatter(stacked_qkv, "dp", scatter_dimension=2, tiled=True),
        lax.psum_scatter(stacked_out, "dp", scatter_dimension=3, tiled=True),
        lax.psum_scatter(stacked_in, "dp", scatter_dimension=1, tiled=True),
        lax.psum_scatter(stacked_down, "dp", scatter_dimension=2, tiled=True),
    )
    stacked_gains, stacked_biases, stacked_hidden = (
        lax.psum_scatter(stacked_gains, ("dp", "tensor"), scatter_dimension=2, tiled=True),
        lax.psum_scatter(stacked_biases, ("dp", "tensor"), scatter_dimension=2, tiled=True),
        lax.psum_scatter(stacked_hidden, ("dp", "tensor"), scatter_dimension=1, tiled=True),
    )
    return (
        output,
        upstream,
        stacked_qkv,
        stacked_out,
        stacked_in,
        stacked_down,
        stacked_gains,
        stacked_biases,
        stacked_hidden,
    )


def solution(mesh):
    placed = (
        P(("dp", "tensor"), None),
        P(("dp", "tensor"), None),
        P(None, None, "dp", None, "tensor"),
        P(None, None, "tensor", "dp"),
        P(None, "dp", "tensor"),
        P(None, "tensor", "dp"),
        P(None, None, ("dp", "tensor")),
        P(None, None, ("dp", "tensor")),
        P(None, ("dp", "tensor")),
    )
    return jax.shard_map(
        shards,
        mesh=mesh,
        in_specs=placed,
        out_specs=(
            P(("dp", "tensor"), None),
            P(("dp", "tensor"), None),
            P(None, None, "dp", None, "tensor"),
            P(None, None, "tensor", "dp"),
            P(None, "dp", "tensor"),
            P(None, "tensor", "dp"),
            P(None, None, ("dp", "tensor")),
            P(None, None, ("dp", "tensor")),
            P(None, ("dp", "tensor")),
        ),
        check_vma=False,
    )
```

profile of v0, /device:TPU:0, one launch (start us, length us, event | category | flops | bytes accessed | tf_op | source)
XLA Modules:
  0.0 1701.9 jit_solution(394512087602113452)
XLA Ops:
  8.2 44.3 %all-gather.1 = f32[1,10,768]{1,0,2:T(1,128)S(1)} all-gather(f32[1,10,24]{1,0,2:T(1,128)S(1)} %copy.143), channel_id=3, replica_groups=mesh['dp'=16,'tensor'=2] {'dp','tensor'}, dimensions={2}, use_global_device_ids=true | all-gather | bytes 31680 | tf_op jit(solution)/shard_map/all_gather | solution.py:66
  52.4 16.1 fusion.123
  70.5 38.0 %all-gather = f32[1,3,768]{1,0,2:T(1,128)S(1)} all-gather(f32[1,3,24]{1,0,2:T(1,128)S(1)} %copy.142), channel_id=2, replica_groups=mesh['dp'=16,'tensor'=2] {'dp','tensor'}, dimensions={2}, use_global_device_ids=true | all-gather | bytes 9504 | tf_op jit(solution)/shard_map/all_gather | solution.py:65
  131.2 75.1 %all-gather.30.cloned.1.call-done = bf16[1,2,768,3,384]{4,2,3,1,0:T(8,128)(2,1)} async-done(((bf16[1,2,48,3,384]{4,2,3,1,0:T(8,128)(2,1)}), bf16[1,2,768,3,384]{4,2,3,1,0:T(8,128)(2,1)}) %all-gather.30.cloned.1.call-update) | async-done | bytes 3538960 | tf_op jit(solution)/shard_map/all_gather | solution.py:56
  206.4 11.8 fusion.57
  284.8 13.4 fusion.124
  330.5 11.4 reduce-scatter.14.cloned.1.call-done
  350.2 14.2 all-gather.20.cloned.1.call-done
  364.5 12.2 fusion.53
  424.3 11.4 convert_element_type.318
  530.5 11.8 reduce-scatter.16.cloned.1.call-done
  550.6 41.4 %all-reduce = f32[3072]{0:T(1024)S(1)} all-reduce(f32[3072]{0:T(1024)S(1)} %bitcast_dynamic-update-slice_fusion), channel_id=7, replica_groups=mesh['dp'=16,'tensor'=2] {'dp','tensor'}, use_global_device_ids=true, to_apply=%add | all-reduce | flops 3072 | bytes 24576
  592.1 16.5 all-gather.36.cloned.1.call-done
  608.6 15.1 all-gather.24.cloned.1.call-done
  623.7 12.4 convolution_convert_fusion
  636.2 53.9 %all-gather.34.cloned.1.call-done = bf16[1,768,1536]{2,1,0:T(8,128)(2,1)} async-done(((bf16[1,48,1536]{2,1,0:T(8,128)(2,1)}), bf16[1,768,1536]{2,1,0:T(8,128)(2,1)}) %all-gather.34.cloned.1.call-update) | async-done | bytes 2359312 | tf_op jit(solution)/shard_map/all_gather | solution.py:58
  690.0 15.4 all-gather.22.cloned.1.call-done
  705.4 57.2 %convert_reduce_fusion = (f32[1536]{0:T(1024)}, bf16[3136,1536]{1,0:T(8,128)(2,1)S(1)}, f32[3136,1536]{1,0:T(8,128)}, f32[3136,1536]{1,0:T(8,128)}) fusion(bf16[3136,1536]{1,0:T(8,128)(2,1)} %convolution_convert_fusion, f32[1536]{0:T(1024)S(1)} %dynamic-slice.9, bf16[3136,768]{1,0:T(8,128)(2,1)} %all-gather.22.cloned.1.call-done, ...), kind=kOutput, calls=%fused_computation.15 | convolution fusion | flops 7764834816 | bytes 64991232 | tf_op jit(solution)/shard_map/dot_general | solution.py:181
  776.4 15.7 multiply_convert_fusion.1
  912.9 13.0 fusion.18
  987.6 13.8 reduce-scatter.22.cloned.1.call-done
  1020.2 13.8 convolution_bitcast_fusion
  1034.0 12.4 copy.191
  1073.3 12.8 convert_bitcast_fusion.3
  1086.1 14.4 multiply_reduce_fusion
  1126.3 18.6 %multiply_convert_fusion = bf16[16,6,196,196]{2,3,1,0:T(8,128)(2,1)} fusion(f32[16,6,196,196]{2,3,1,0:T(8,128)} %get-tuple-element.105, f32[16,6,196]{2,1,0:T(8,128)S(1)} %get-tuple-element.104, f32[16,6,196,196]{2,3,1,0:T(8,128)} %get-tuple-element.98, f32[16,6,196]{2,1,0:T(8,128)S(1)} %copy-done.38), kind=kLoop, calls=%fused_computation.4 | loop fusion | flops 14751744 | bytes 37029888 | tf_op jit(solution)/shard_map/convert_element_type | solution.py:110
  1210.2 14.0 convolution_bitcast_fusion.1
  1235.3 11.4 fusion.103
  1262.1 118.4 %all-reduce.9.cloned.1.call-done = (f32[1,2,384,768]{2,1,0,3:T(2,128)}, f32[1,1536,768]{1,0,2:T(1,128)}) async-done(((f32[1,2,384,768]{2,1,0,3:T(2,128)}, f32[1,1536,768]{1,0,2:T(1,128)}), (f32[1,2,384,768]{2,1,0,3:T(2,128)}, f32[1,1536,768]{1,0,2:T(1,128)})) %all-reduce.9.cloned.1.call-update) | async-done | bytes 7077904
  1402.6 41.2 %all-reduce.5 = (f32[1,3,768]{2,0,1:T(1,128)S(1)}, f32[1,10,768]{2,0,1:T(1,128)S(1)}) all-reduce(f32[1,3,768]{2,0,1:T(1,128)S(1)} %stack.91, f32[1,10,768]{2,0,1:T(1,128)S(1)} %stack.97), channel_id=19, replica_groups=mesh['dp'=16,'tensor'=2] {'dp','tensor'}, use_global_device_ids=true, to_apply=%region_31.0.clone | all-reduce | flops 9984 | bytes 79872
  1450.7 87.7 %reduce-scatter.28.cloned.1.call-done = f32[1,48,1536]{2,1,0:T(8,128)} async-done(((f32[1,768,1536]{2,1,0:T(8,128)}), f32[1,48,1536]{2,1,0:T(8,128)}) %reduce-scatter.28.cloned.1.call-update) | async-done | bytes 294928 | tf_op jit(solution)/shard_map/reduce_scatter | solution.py:291
  1538.4 156.2 %reduce-scatter.26.cloned.1.call-done = f32[1,2,48,3,384]{4,2,3,1,0:T(8,128)} async-done(((f32[1,2,768,3,384]{4,2,3,1,0:T(8,128)}), f32[1,2,48,3,384]{4,2,3,1,0:T(8,128)}) %reduce-scatter.26.cloned.1.call-update) | async-done | bytes 442384 | tf_op jit(solution)/shard_map/reduce_scatter | solution.py:289
  (355 shorter events, 670.5 us)
Async XLA Ops:
  7.2 61.4 %copy-start = (bf16[1568,768]{1,0:T(8,128)(2,1)S(1)}, bf16[1568,768]{1,0:T(8,128)(2,1)}, u32[]{:S(2)}) copy-start(bf16[1568,768]{1,0:T(8,128)(2,1)} %param.9) | copy-start | bytes 7225348
  7.2 124.0 %all-gather.18.cloned.1.call-start = ((), (), s32[]{:S(2)}) async-start(), calls=%async_computation.9 | async-start | bytes 7225344 | tf_op jit(solution)/shard_map/all_gather | solution.py:35
  68.6 473.7 %copy-start.33 = (f32[768]{0:T(1024)}, f32[768]{0:T(1024)S(1)}, u32[]{:S(2)}) copy-start(f32[768]{0:T(1024)S(1)} %get-tuple-element.92) | copy-start | bytes 9220
  69.0 50.0 %copy-start.29 = (f32[1568]{0:T(1024)}, f32[1568]{0:T(1024)S(1)}, u32[]{:S(2)}) copy-start(f32[1568]{0:T(1024)S(1)} %broadcast_multiply_fusion.2) | copy-start | bytes 18820
  70.4 147.7 %copy-start.39 = (f32[1568]{0:T(1024)}, f32[1568]{0:T(1024)S(1)}, u32[]{:S(2)}) copy-start(f32[1568]{0:T(1024)S(1)} %fusion.109) | copy-start | bytes 18820
  116.2 229.7 %copy-start.47 = (f32[768]{0:T(1024)}, f32[768]{0:T(1024)S(1)}, u32[]{:S(2)}) copy-start(f32[768]{0:T(1024)S(1)} %get-tuple-element.65) | copy-start | bytes 9220
  119.0 87.4 %all-gather.30.cloned.1.call-start = ((), (), s32[]{:S(2)}) async-start(), calls=%async_computation.23 | async-start | bytes 3760128 | tf_op jit(solution)/shard_map/all_gather | solution.py:56
  119.8 203.9 %all-gather.32.cloned.1.call-start = ((), (), s32[]{:S(2)}) async-start(), calls=%async_computation.24 | async-start | bytes 1253376 | tf_op jit(solution)/shard_map/all_gather | solution.py:57
  120.5 221.4 %reduce-scatter.14.cloned.1.call-start = ((), (), s32[]{:S(2)}) async-start(), calls=%async_computation.10 | async-start | bytes 7225344 | tf_op jit(solution)/shard_map/reduce_scatter | solution.py:39
  330.4 34.0 %all-gather.20.cloned.1.call-start = ((), (), s32[]{:S(2)}) async-start(), calls=%async_computation.11 | async-start | bytes 7225344 | tf_op jit(solution)/shard_map/all_gather | solution.py:35
  348.6 193.7 %reduce-scatter.16.cloned.1.call-start = ((), (), s32[]{:S(2)}) async-start(), calls=%async_computation.12 | async-start | bytes 7225344 | tf_op jit(solution)/shard_map/reduce_scatter | solution.py:39
  528.2 80.4 %all-gather.36.cloned.1.call-start = ((), (), s32[]{:S(2)}) async-start(), calls=%async_computation.26 | async-start | bytes 2506752 | tf_op jit(solution)/shard_map/all_gather | solution.py:59
  529.0 94.7 %all-gather.24.cloned.1.call-start = ((), (), s32[]{:S(2)}) async-start(), calls=%async_computation.15 | async-start | bytes 7225344 | tf_op jit(solution)/shard_map/all_gather | solution.py:45
  529.7 160.3 %all-gather.34.cloned.1.call-start = ((), (), s32[]{:S(2)}) async-start(), calls=%async_computation.25 | async-start | bytes 2506752 | tf_op jit(solution)/shard_map/all_gather | solution.py:58
  530.5 174.9 %all-gather.22.cloned.1.call-start = ((), (), s32[]{:S(2)}) async-start(), calls=%async_computation.13 | async-start | bytes 7225344 | tf_op jit(solution)/shard_map/all_gather | solution.py:35
  550.4 255.4 %reduce-scatter.20.cloned.1.call-start = ((), (), s32[]{:S(2)}) async-start(), calls=%async_computation.16 | async-start | bytes 7225344 | tf_op jit(solution)/shard_map/reduce_scatter | solution.py:49
  705.4 60.8 %copy-start.72 = (bf16[1,768,1536]{2,1,0:T(8,128)(2,1)S(1)}, bf16[1,768,1536]{2,1,0:T(8,128)(2,1)}, u32[]{:S(2)}) copy-start(bf16[1,768,1536]{2,1,0:T(8,128)(2,1)} %all-gather.34.cloned.1.call-done) | copy-start | bytes 7077892
  776.3 43.3 %reduce-scatter.18.cloned.1.call-start = ((), (), s32[]{:S(2)}) async-start(), calls=%async_computation.14 | async-start | bytes 7225344 | tf_op jit(solution)/shard_map/reduce_scatter | solution.py:39
  776.4 19.4 %copy-start.71 = (bf16[1,1536,768]{1,2,0:T(8,128)(2,1)S(1)}, bf16[1,1536,768]{1,2,0:T(8,128)(2,1)}, u32[]{:S(2)}) copy-start(bf16[1,1536,768]{1,2,0:T(8,128)(2,1)} %all-gather.36.cloned.1.call-done) | copy-start | bytes 7077892
  805.7 53.0 %all-gather.26.cloned.1.call-start = ((), (), s32[]{:S(2)}) async-start(), calls=%async_computation.17 | async-start | bytes 7225344 | tf_op jit(solution)/shard_map/all_gather | solution.py:45
  830.8 170.6 %reduce-scatter.22.cloned.1.call-start = ((), (), s32[]{:S(2)}) async-start(), calls=%async_computation.18 | async-start | bytes 7225344 | tf_op jit(solution)/shard_map/reduce_scatter | solution.py:49
  987.3 66.8 %all-gather.28.cloned.1.call-start = ((), (), s32[]{:S(2)}) async-start(), calls=%async_computation.19 | async-start | bytes 7225344 | tf_op jit(solution)/shard_map/all_gather | solution.py:45
  1020.2 231.8 %reduce-scatter.30.cloned.1.call-start = ((), (), s32[]{:S(2)}) async-start(), calls=%async_computation.27 | async-start | bytes 1622016
  1048.1 332.3 %all-reduce.9.cloned.1.call-start = ((), (), s32[]{:S(2)}) async-start(), calls=%async_computation.28 | async-start | bytes 14155776
  1126.2 268.3 %reduce-scatter.24.cloned.1.call-start = ((), (), s32[]{:S(2)}) async-start(), calls=%async_computation.20 | async-start | bytes 7225344 | tf_op jit(solution)/shard_map/reduce_scatter | solution.py:49
  1210.1 328.3 %reduce-scatter.28.cloned.1.call-start = ((), (), s32[]{:S(2)}) async-start(), calls=%async_computation.22 | async-start | bytes 5013504 | tf_op jit(solution)/shard_map/reduce_scatter | solution.py:291
  1224.2 470.4 %reduce-scatter.26.cloned.1.call-start = ((), (), s32[]{:S(2)}) async-start(), calls=%async_computation.21 | async-start | bytes 7520256 | tf_op jit(solution)/shard_map/reduce_scatter | solution.py:289
  1257.5 137.0 %copy-start.2 = (bf16[1568,768]{1,0:T(8,128)(2,1)S(1)}, bf16[1568,768]{1,0:T(8,128)(2,1)}, u32[]{:S(2)}) copy-start(bf16[1568,768]{1,0:T(8,128)(2,1)} %param.9) | copy-start | bytes 7225348
  1257.5 137.0 %copy-start.30 = (f32[1568]{0:T(1024)S(1)}, f32[1568]{0:T(1024)}, u32[]{:S(2)}) copy-start(f32[1568]{0:T(1024)} %copy-done.29) | copy-start | bytes 18820
  1257.5 137.0 %copy-start.46 = (f32[768]{0:T(1024)S(1)}, f32[768]{0:T(1024)}, u32[]{:S(2)}) copy-start(f32[768]{0:T(1024)} %copy-done.45) | copy-start | bytes 9220
  1262.0 136.1 %copy-start.50 = (f32[1568]{0:T(1024)S(1)}, f32[1568]{0:T(1024)}, u32[]{:S(2)}) copy-start(f32[1568]{0:T(1024)} %copy-done.49) | copy-start | bytes 18820
  1262.0 136.1 %copy-start.40 = (f32[1568]{0:T(1024)S(1)}, f32[1568]{0:T(1024)}, u32[]{:S(2)}) copy-start(f32[1568]{0:T(1024)} %copy-done.39) | copy-start | bytes 18820
  (64 other events, 436.2 us)
Sparse Core Ops, SparseCore 0:
  119.1 12.0 all-gather.17
  133.9 72.4 all-gather.29
  209.1 54.6 all-gather.31
  330.5 11.2 reduce-scatter.13
  348.7 15.7 all-gather.19
  528.4 13.8 reduce-scatter.15
  545.1 63.4 all-gather.35
  610.2 13.5 all-gather.23
  626.5 63.4 all-gather.33
  692.0 13.3 all-gather.21
  776.4 13.7 reduce-scatter.19
  805.8 13.7 reduce-scatter.17
  831.0 15.8 all-gather.25
  987.4 13.9 reduce-scatter.21
  1020.3 15.7 all-gather.27
  1048.2 98.2 reduce-scatter.29
  1154.0 226.4 all-reduce.8
  1382.7 11.7 reduce-scatter.23
  1400.3 138.0 reduce-scatter.27
  1545.0 149.5 reduce-scatter.25
where the time goes:
time: 1710 us; the launch traced here: 1700 us
  waiting for transfers between devices  619 us (36%)
  local copies, waits for them, and re-layouts  425 us (25%)
  matrix products  330 us (19%)
  blocking collectives  165 us (10%)
  other arithmetic  145 us (8%)
    reduce_scatter x1, waiting for transfers between devices, shards(): lax.psum_scatter(stacked_qkv, 'dp', scatter_dimension=2, tiled=True)  156 us
    unnamed x22, waiting for transfers between devices  122 us
    reduce_scatter x1, waiting for transfers between devices, shards(): lax.psum_scatter(stacked_in, 'dp', scatter_dimension=1, tiled=True)  87.7 us
    unnamed x2, blocking collectives  82.7 us
    all_gather x1, waiting for transfers between devices, fetch_weights(): lax.all_gather(attn_qkv[layer_index], 'dp', axis=1, tiled=True)  75.1 us
    dot_general x1, matrix products, mlp_forward(): jnp.dot(gathered, w_in, preferred_element_type=jnp.float32)  57.2 us
    all_gather x1, waiting for transfers between devices, fetch_weights(): lax.all_gather(mlp_in[layer_index], 'dp', axis=0, tiled=True)  53.9 us
    convert_element_type x5, local copies, waits for them, and re-layouts, attention_forward(): key_rows = projected[:, 1].astype(jnp.bfloat16)  47.8 us
  transfers between devices with their start and end apart: 20, of which 15 were waited for; matrix products, arithmetic and copies ran while one was open for 27% of the time, Pallas kernels for 0%

commit v1 on v0

v1 whole, which is shorter than its diff:
```python
import functools
import jax
import jax.numpy as jnp
from jax import lax
from jax.experimental import pallas as pl
from jax.experimental.pallas import tpu as pltpu
from jax.sharding import PartitionSpec as P

HEAD = 64
FRAMES = 16
PATCHES = 196
PAD = 208
EPSILON = 1e-06
BF = jnp.bfloat16
F32 = jnp.float32
NN = (((1,), (0,)), ((), ()))
NT = (((1,), (1,)), ((), ()))
TN = (((0,), (0,)), ((), ()))
VMEM_BYTES = 60 * 1024 * 1024


def dot(a, b, dims):
    return lax.dot_general(a, b, dims, preferred_element_type=F32)


def norm_parts(x):
    mean = jnp.mean(x, axis=-1, keepdims=True)
    centred = x - mean
    var = jnp.mean(centred * centred, axis=-1, keepdims=True)
    rstd = lax.rsqrt(var + EPSILON)
    return centred * rstd, rstd


def norm_back(grad_normed, xhat, rstd, gain):
    scaled = grad_normed * gain
    first = jnp.mean(scaled, axis=-1, keepdims=True)
    second = jnp.mean(scaled * xhat, axis=-1, keepdims=True)
    return rstd * (scaled - first - xhat * second)


def split_halves(pair):
    lane = lax.broadcasted_iota(jnp.int32, pair.shape, 1)
    zero = jnp.zeros_like(pair)
    return jnp.where(lane < HEAD, pair, zero), jnp.where(lane < HEAD, zero, pair)


def project(normed, w_ref, vec_ref, row_base, cols):
    parts = []
    for g in range(2):
        w = w_ref[g, :, 0 : 3 * cols]
        qkv = dot(normed, w, NN)
        bq = vec_ref[row_base + 1 : row_base + 2, g * cols : (g + 1) * cols]
        bv = vec_ref[row_base + 2 : row_base + 3, g * cols : (g + 1) * cols]
        q = (qkv[:, :cols] + bq).astype(BF) * BF(0.125)
        k = qkv[:, cols : 2 * cols].astype(BF)
        v = (qkv[:, 2 * cols :] + bv).astype(BF)
        parts.append((q, k, v))
    return parts


def heads_forward(q, k, v, mask):
    exps, sums, outs = [], [], []
    for qh in split_halves(q):
        s = dot(qh, k, NT)
        s = jnp.where(mask, s, -1e30)
        top = jnp.max(s, axis=-1, keepdims=True)
        e = jnp.exp(s - top)
        recip = 1.0 / jnp.sum(e, axis=-1, keepdims=True)
        eb = e.astype(BF)
        outs.append(dot(eb, v, NN) * recip)
        exps.append(eb)
        sums.append(recip)
    lane = lax.broadcasted_iota(jnp.int32, q.shape, 1)
    return jnp.where(lane < HEAD, outs[0], outs[1]), exps, sums


def heads_backward(q, k, v, o, do, exps, recips):
    prod = do.astype(F32) * o.astype(F32)
    dq = dk = dv = None
    qs, ks, ps = split_halves(q), split_halves(k), split_halves(prod)
    dos = split_halves(do)
    for h in range(2):
        r = recips[h]
        delta = jnp.sum(ps[h], axis=-1, keepdims=True) * r
        dor = (dos[h].astype(F32) * r).astype(BF)
        dp = dot(dor, v, NT)
        e = exps[h]
        ds = (e.astype(F32) * (dp - delta)).astype(BF)
        dq_h = dot(ds, ks[h], NN)
        dk_h = dot(ds, qs[h], TN)
        dv_h = dot(e, dor, TN)
        dq = dq_h if dq is None else dq + dq_h
        dk = dk_h if dk is None else dk + dk_h
        dv = dv_h if dv is None else dv + dv_h
    return (dq * 0.125).astype(BF), dk.astype(BF), dv.astype(BF)


def spatial_mask():
    return lax.broadcasted_iota(jnp.int32, (PAD, PAD), 1) < PATCHES


def spatial_fwd_kernel(x_ref, w_ref, vec_ref, s_ref, qkv_ref, mix_ref, p_ref, r_ref):
    cols = w_ref.shape[2] // 4
    x = x_ref[0].astype(F32)
    xhat, _ = norm_parts(x)
    normed = (xhat * vec_ref[10:11, :] + vec_ref[0:1, :]).astype(BF)
    mask = spatial_mask()
    branch = vec_ref[3:4, :]
    lane = lax.broadcasted_iota(jnp.int32, (PAD, 128), 1)
    recips = jnp.zeros((PAD, 128), F32)
    for g, (q, k, v) in enumerate(project(normed, w_ref, vec_ref, 0, cols)):
        qkv_ref[0, g, :, 0:cols] = q
        qkv_ref[0, g, :, cols : 2 * cols] = k
        qkv_ref[0, g, :, 2 * cols : 3 * cols] = v
        mixes = []
        for j in range(cols // 128):
            sl = slice(128 * j, 128 * (j + 1))
            mix, exps, rec = heads_forward(q[:, sl], k[:, sl], v[:, sl], mask)
            mixes.append(mix.astype(BF))
            for h in range(2):
                head = (g * (cols // 128) + j) * 2 + h
                p_ref[0, head] = exps[h]
                recips = jnp.where(lane == head, rec[h], recips)
        mix = jnp.concatenate(mixes, axis=1)
        mix_ref[0, g] = mix
        branch = branch + dot(mix, w_ref[g, :, 3 * cols : 4 * cols], NT)
    r_ref[0] = recips
    s_ref[0] = x + branch


def spatial_fwd(x, weights, section, vec):
    frames = x.shape[0]
    D = x.shape[2]
    cols = D // 2
    heads = D // HEAD
    whole = lambda *shape: pl.BlockSpec(shape, lambda i: (0,) * len(shape))
    return pl.pallas_call(
        spatial_fwd_kernel,
        grid=(frames,),
        in_specs=[
            pl.BlockSpec((1, PAD, D), lambda i: (i, 0, 0)),
            pl.BlockSpec((2, D, 4 * cols), lambda i: (0, 0, section)),
            whole(*vec.shape),
        ],
        out_specs=[
            pl.BlockSpec((1, PAD, D), lambda i: (i, 0, 0)),
            pl.BlockSpec((1, 2, PAD, 3 * cols), lambda i: (i, 0, 0, 0)),
            pl.BlockSpec((1, 2, PAD, cols), lambda i: (i, 0, 0, 0)),
            pl.BlockSpec((1, heads, PAD, PAD), lambda i: (i, 0, 0, 0)),
            pl.BlockSpec((1, PAD, 128), lambda i: (i, 0, 0)),
        ],
        out_shape=[
            jax.ShapeDtypeStruct((frames, PAD, D), F32),
            jax.ShapeDtypeStruct((frames, 2, PAD, 3 * cols), BF),
            jax.ShapeDtypeStruct((frames, 2, PAD, cols), BF),
            jax.ShapeDtypeStruct((frames, heads, PAD, PAD), BF),
            jax.ShapeDtypeStruct((frames, PAD, 128), F32),
        ],
        name="spatial_fwd",
        compiler_params=pltpu.CompilerParams(vmem_limit_bytes=VMEM_BYTES),
    )(x, weights, vec)


def attn_back_common(x, ub, up, w_ref, vec_ref, row_base, gain_row, mix_of, qkv_of, exps_of, rec_of, gw_ref, gv_ref, cols, blocks):
    xhat, rstd = norm_parts(x)
    gain = vec_ref[gain_row : gain_row + 1, :]
    normed = (xhat * gain + vec_ref[row_base : row_base + 1, :]).astype(BF)
    dn = None
    gv_ref[3:4, :] += jnp.sum(up, axis=0, keepdims=True)
    rows = x.shape[0]
    step = rows // blocks
    for g in range(2):
        wo = w_ref[g, :, 3 * cols : 4 * cols]
        dmix = dot(ub, wo, NN).astype(BF)
        mix = mix_of(g)
        gw_ref[g, :, 3 * cols : 4 * cols] += dot(ub, mix, TN)
        parts = []
        for part in range(3):
            parts.append([[] for _ in range(blocks)])
        for b in range(blocks):
            rs = slice(step * b, step * (b + 1))
            for j in range(cols // 128):
                sl = slice(128 * j, 128 * (j + 1))
                q, k, v = qkv_of(g, j, rs)
                exps = [exps_of((g * (cols // 128) + j) * 2 + h, b) for h in range(2)]
                recs = [rec_of((g * (cols // 128) + j) * 2 + h, rs) for h in range(2)]
                trio = heads_backward(q, k, v, mix[rs, sl], dmix[rs, sl], exps, recs)
                for part in range(3):
                    parts[part][b].append(trio[part])
        cat = lambda rowsof: jnp.concatenate([jnp.concatenate(r, axis=1) for r in rowsof], axis=0)
        dq, dk, dv = cat(parts[0]), cat(parts[1]), cat(parts[2])
        span = slice(g * cols, (g + 1) * cols)
        gv_ref[1:2, span] += jnp.sum(dq.astype(F32), axis=0, keepdims=True)
        gv_ref[2:3, span] += jnp.sum(dv.astype(F32), axis=0, keepdims=True)
        dqkv = jnp.concatenate([dq, dk, dv], axis=1)
        gw_ref[g, :, 0 : 3 * cols] += dot(normed, dqkv, TN)
        term = dot(dqkv, w_ref[g, :, 0 : 3 * cols], NT)
        dn = term if dn is None else dn + term
    gv_ref[0:1, :] += jnp.sum(dn, axis=0, keepdims=True)
    gv_ref[4:5, :] += jnp.sum(dn * xhat, axis=0, keepdims=True)
    return up + norm_back(dn, xhat, rstd, gain)


def spatial_bwd_kernel(x_ref, up_ref, qkv_ref, mix_ref, p_ref, r_ref, w_ref, vec_ref, gx_ref, gb_ref, gv_ref, gw_ref):
    cols = w_ref.shape[2] // 4

    @pl.when(pl.program_id(0) == 0)
    def _():
        gw_ref[...] = jnp.zeros_like(gw_ref)
        gv_ref[...] = jnp.zeros_like(gv_ref)

    x = x_ref[0].astype(F32)
    up = up_ref[0]
    ub = up.astype(BF)
    gx_ref[0] = attn_back_common(
        x, ub, up, w_ref, vec_ref, 0, 10,
        lambda g: mix_ref[0, g],
        lambda g, j, rs: tuple(
            qkv_ref[0, g, :, cols * t + 128 * j : cols * t + 128 * (j + 1)] for t in range(3)
        ),
        lambda head, b: p_ref[0, head],
        lambda head, rs: r_ref[0, :, head : head + 1],
        gw_ref, gv_ref, cols, 1,
    )

    @pl.when(pl.program_id(0) == pl.num_programs(0) - 1)
    def _():
        gb_ref[...] = gw_ref[...].astype(BF)


def spatial_bwd(x, up, qkv, mix, p, r, weights, section, vec):
    frames = x.shape[0]
    D = x.shape[2]
    cols = D // 2
    heads = D // HEAD
    whole = lambda *shape: pl.BlockSpec(shape, lambda i: (0,) * len(shape))
    return pl.pallas_call(
        spatial_bwd_kernel,
        grid=(frames,),
        in_specs=[
            pl.BlockSpec((1, PAD, D), lambda i: (i, 0, 0)),
            pl.BlockSpec((1, PAD, D), lambda i: (i, 0, 0)),
            pl.BlockSpec((1, 2, PAD, 3 * cols), lambda i: (i, 0, 0, 0)),
            pl.BlockSpec((1, 2, PAD, cols), lambda i: (i, 0, 0, 0)),
            pl.BlockSpec((1, heads, PAD, PAD), lambda i: (i, 0, 0, 0)),
            pl.BlockSpec((1, PAD, 128), lambda i: (i, 0, 0)),
            pl.BlockSpec((2, D, 4 * cols), lambda i: (0, 0, section)),
            whole(*vec.shape),
        ],
        out_specs=[
            pl.BlockSpec((1, PAD, D), lambda i: (i, 0, 0)),
            whole(2, D, 4 * cols),
            whole(8, D),
        ],
        out_shape=[
            jax.ShapeDtypeStruct((frames, PAD, D), F32),
            jax.ShapeDtypeStruct((2, D, 4 * cols), BF),
            jax.ShapeDtypeStruct((8, D), F32),
        ],
        scratch_shapes=[pltpu.VMEM((2, D, 4 * cols), F32)],
        name="spatial_bwd",
        compiler_params=pltpu.CompilerParams(vmem_limit_bytes=VMEM_BYTES),
    )(x, up, qkv, mix, p, r, weights, vec)


GROUP = 8 * FRAMES
STEP_GROUPS = 2


def temporal_mask():
    a = lax.broadcasted_iota(jnp.int32, (GROUP, GROUP), 0)
    b = lax.broadcasted_iota(jnp.int32, (GROUP, GROUP), 1)
    return (a % 8) == (b % 8)


def live_rows(rows_per_step, rows):
    base = pl.program_id(0) * rows_per_step
    return base + lax.broadcasted_iota(jnp.int32, (rows_per_step, 1), 0) < rows


def temporal_fwd_kernel(rows, x_ref, w_ref, vec_ref, s_ref, qkv_ref, mix_ref, p_ref, r_ref):
    cols = w_ref.shape[2] // 4
    n = x_ref.shape[0]
    x = jnp.where(live_rows(n, rows), x_ref[...], 0.0)
    xhat, _ = norm_parts(x)
    normed = (xhat * vec_ref[11:12, :] + vec_ref[4:5, :]).astype(BF)
    mask = temporal_mask()
    branch = vec_ref[7:8, :]
    lane = lax.broadcasted_iota(jnp.int32, (GROUP, 128), 1)
    recips = [jnp.zeros((GROUP, 128), F32) for _ in range(n // GROUP)]
    for g, (q, k, v) in enumerate(project(normed, w_ref, vec_ref, 4, cols)):
        qkv_ref[g, :, 0:cols] = q
        qkv_ref[g, :, cols : 2 * cols] = k
        qkv_ref[g, :, 2 * cols : 3 * cols] = v
        blocks = []
        for b in range(n // GROUP):
            rs = slice(GROUP * b, GROUP * (b + 1))
            mixes = []
            for j in range(cols // 128):
                sl = slice(128 * j, 128 * (j + 1))
                mix, exps, rec = heads_forward(q[rs, sl], k[rs, sl], v[rs, sl], mask)
                mixes.append(mix.astype(BF))
                for h in range(2):
                    head = (g * (cols // 128) + j) * 2 + h
                    p_ref[head, rs] = exps[h]
                    recips[b] = jnp.where(lane == head, rec[h], recips[b])
            blocks.append(jnp.concatenate(mixes, axis=1))
        mix = jnp.concatenate(blocks, axis=0)
        mix_ref[g] = mix
        branch = branch + dot(mix, w_ref[g, :, 3 * cols : 4 * cols], NT)
    r_ref[...] = jnp.concatenate(recips, axis=0)
    s_ref[...] = x + branch


def temporal_fwd(x, weights, section, vec):
    rows, D = x.shape
    cols = D // 2
    heads = D // HEAD
    n = STEP_GROUPS * GROUP
    steps = -(-rows // n)
    padded = steps * n
    whole = lambda *shape: pl.BlockSpec(shape, lambda i: (0,) * len(shape))
    return pl.pallas_call(
        functools.partial(temporal_fwd_kernel, rows),
        grid=(steps,),
        in_specs=[
            pl.BlockSpec((n, D), lambda i: (i, 0)),
            pl.BlockSpec((2, D, 4 * cols), lambda i: (0, 0, section)),
            whole(*vec.shape),
        ],
        out_specs=[
            pl.BlockSpec((n, D), lambda i: (i, 0)),
            pl.BlockSpec((2, n, 3 * cols), lambda i: (0, i, 0)),
            pl.BlockSpec((2, n, cols), lambda i: (0, i, 0)),
            pl.BlockSpec((heads, n, GROUP), lambda i: (0, i, 0)),
            pl.BlockSpec((n, 128), lambda i: (i, 0)),
        ],
        out_shape=[
            jax.ShapeDtypeStruct((rows, D), F32),
            jax.ShapeDtypeStruct((2, padded, 3 * cols), BF),
            jax.ShapeDtypeStruct((2, padded, cols), BF),
            jax.ShapeDtypeStruct((heads, padded, GROUP), BF),
            jax.ShapeDtypeStruct((padded, 128), F32),
        ],
        name="temporal_fwd",
        compiler_params=pltpu.CompilerParams(vmem_limit_bytes=VMEM_BYTES),
    )(x, weights, vec)


def temporal_bwd_kernel(rows, x_ref, up_ref, qkv_ref, mix_ref, p_ref, r_ref, w_ref, vec_ref, gx_ref, gb_ref, gv_ref, gw_ref):
    cols = w_ref.shape[2] // 4
    n = x_ref.shape[0]

    @pl.when(pl.program_id(0) == 0)
    def _():
        gw_ref[...] = jnp.zeros_like(gw_ref)
        gv_ref[...] = jnp.zeros_like(gv_ref)

    live = live_rows(n, rows)
    x = jnp.where(live, x_ref[...], 0.0)
    up = jnp.where(live, up_ref[...], 0.0)
    ub = up.astype(BF)
    gx_ref[...] = attn_back_common(
        x, ub, up, w_ref, vec_ref, 4, 11,
        lambda g: mix_ref[g],
        lambda g, j, rs: tuple(
            qkv_ref[g, rs, cols * t + 128 * j : cols * t + 128 * (j + 1)] for t in range(3)
        ),
        lambda head, b: p_ref[head, GROUP * b : GROUP * (b + 1)],
        lambda head, rs: r_ref[rs, head : head + 1],
        gw_ref, gv_ref, cols, n // GROUP,
    )

    @pl.when(pl.program_id(0) == pl.num_programs(0) - 1)
    def _():
        gb_ref[...] = gw_ref[...].astype(BF)


def temporal_bwd(x, up, qkv, mix, p, r, weights, section, vec):
    rows, D = x.shape
    cols = D // 2
    heads = D // HEAD
    n = STEP_GROUPS * GROUP
    steps = -(-rows // n)
    whole = lambda *shape: pl.BlockSpec(shape, lambda i: (0,) * len(shape))
    return pl.pallas_call(
        functools.partial(temporal_bwd_kernel, rows),
        grid=(steps,),
        in_specs=[
            pl.BlockSpec((n, D), lambda i: (i, 0)),
            pl.BlockSpec((n, D), lambda i: (i, 0)),
            pl.BlockSpec((2, n, 3 * cols), lambda i: (0, i, 0)),
            pl.BlockSpec((2, n, cols), lambda i: (0, i, 0)),
            pl.BlockSpec((heads, n, GROUP), lambda i: (0, i, 0)),
            pl.BlockSpec((n, 128), lambda i: (i, 0)),
            pl.BlockSpec((2, D, 4 * cols), lambda i: (0, 0, section)),
            whole(*vec.shape),
        ],
        out_specs=[
            pl.BlockSpec((n, D), lambda i: (i, 0)),
            whole(2, D, 4 * cols),
            whole(8, D),
        ],
        out_shape=[
            jax.ShapeDtypeStruct((rows, D), F32),
            jax.ShapeDtypeStruct((2, D, 4 * cols), BF),
            jax.ShapeDtypeStruct((8, D), F32),
        ],
        scratch_shapes=[pltpu.VMEM((2, D, 4 * cols), F32)],
        name="temporal_bwd",
        compiler_params=pltpu.CompilerParams(vmem_limit_bytes=VMEM_BYTES),
    )(x, up, qkv, mix, p, r, weights, vec)


MLP_ROWS = 416
INV_SQRT2 = 0.7071067811865476
INV_SQRT2PI = 0.3989422804014327


def mlp_kernel(x_ref, cot_ref, wi_ref, wo_ref, vec_ref, hid_ref, out_ref, up_ref, gi_ref, go_ref, gv_ref, gh_ref, ai_ref, ao_ref):
    @pl.when(pl.program_id(0) == 0)
    def _():
        ai_ref[...] = jnp.zeros_like(ai_ref)
        ao_ref[...] = jnp.zeros_like(ao_ref)
        gv_ref[...] = jnp.zeros_like(gv_ref)
        gh_ref[...] = jnp.zeros_like(gh_ref)

    width = wi_ref.shape[2]
    x = x_ref[...]
    xhat, rstd = norm_parts(x)
    gain = vec_ref[12:13, :]
    normed = (xhat * gain + vec_ref[8:9, :]).astype(BF)
    ub = cot_ref[...]
    up = ub.astype(F32)
    gv_ref[3:4, :] += jnp.sum(up, axis=0, keepdims=True)
    branch = vec_ref[9:10, :]
    dn = None
    chunk = 768
    for g in range(2):
        for c in range(width // chunk):
            sl = slice(chunk * c, chunk * (c + 1))
            pre = dot(normed, wi_ref[g, :, sl], NN) + hid_ref[g : g + 1, sl]
            cdf = 0.5 + 0.5 * lax.erf(pre * INV_SQRT2)
            act = (pre * cdf).astype(BF)
            branch = branch + dot(act, wo_ref[g, :, sl], NT)
            ao_ref[g, :, sl] += dot(ub, act, TN)
            dact = dot(ub, wo_ref[g, :, sl], NN).astype(BF).astype(F32)
            slope = cdf + pre * (jnp.exp(pre * pre * -0.5) * INV_SQRT2PI)
            dpre32 = dact * slope
            dpre = dpre32.astype(BF)
            gh_ref[g : g + 1, sl] += jnp.sum(dpre.astype(F32), axis=0, keepdims=True)
            ai_ref[g, :, sl] += dot(normed, dpre, TN)
            term = dot(dpre, wi_ref[g, :, sl], NT)
            dn = term if dn is None else dn + term
    out_ref[...] = (x + branch).astype(BF)
    gv_ref[0:1, :] += jnp.sum(dn, axis=0, keepdims=True)
    gv_ref[4:5, :] += jnp.sum(dn * xhat, axis=0, keepdims=True)
    up_ref[...] = up + norm_back(dn, xhat, rstd, gain)

    @pl.when(pl.program_id(0) == pl.num_programs(0) - 1)
    def _():
        gi_ref[...] = ai_ref[...].astype(BF)
        go_ref[...] = ao_ref[...].astype(BF)


def mlp_both(x, cot, weights, section, vec, hidden):
    rows, D = x.shape
    width = hidden.shape[1]
    n = MLP_ROWS
    whole = lambda *shape: pl.BlockSpec(shape, lambda i: (0,) * len(shape))
    one = pl.Buffered(1)
    return pl.pallas_call(
        mlp_kernel,
        grid=(rows // n,),
        in_specs=[
            pl.BlockSpec((n, D), lambda i: (i, 0)),
            pl.BlockSpec((n, D), lambda i: (i, 0)),
            pl.BlockSpec((2, D, width), lambda i: (0, 0, section), pipeline_mode=one),
            pl.BlockSpec((2, D, width), lambda i: (0, 0, section + 1), pipeline_mode=one),
            whole(*vec.shape),
            whole(*hidden.shape),
        ],
        out_specs=[
            pl.BlockSpec((n, D), lambda i: (i, 0)),
            pl.BlockSpec((n, D), lambda i: (i, 0)),
            pl.BlockSpec((2, D, width), lambda i: (0, 0, 0)),
            pl.BlockSpec((2, D, width), lambda i: (0, 0, 0)),
            whole(8, D),
            whole(*hidden.shape),
        ],
        out_shape=[
            jax.ShapeDtypeStruct((rows, D), BF),
            jax.ShapeDtypeStruct((rows, D), F32),
            jax.ShapeDtypeStruct((2, D, width), BF),
            jax.ShapeDtypeStruct((2, D, width), BF),
            jax.ShapeDtypeStruct((8, D), F32),
            jax.ShapeDtypeStruct(hidden.shape, F32),
        ],
        scratch_shapes=[pltpu.VMEM((2, D, width), F32), pltpu.VMEM((2, D, width), F32)],
        name="mlp_both",
        compiler_params=pltpu.CompilerParams(vmem_limit_bytes=VMEM_BYTES),
    )(x, cot, weights, weights, vec, hidden)


def to_patch_groups(rows):
    frames, pad, D = rows.shape
    swapped = lax.all_to_all(
        rows.reshape(frames, 2, pad // 2, D), "tensor", split_axis=1, concat_axis=0, tiled=True
    )
    return (
        swapped.reshape(2 * frames, pad // 16, 8, D).transpose(1, 0, 2, 3).reshape(frames * pad, D)
    )


def to_frames(rows):
    total, D = rows.shape
    frames = total // PAD
    blocks = rows.reshape(PAD // 16, 2 * frames, 8, D).transpose(1, 0, 2, 3)
    swapped = lax.all_to_all(
        blocks.reshape(2 * frames, 1, PAD // 2, D), "tensor", split_axis=0, concat_axis=1, tiled=True
    )
    return swapped.reshape(frames, PAD, D)


def pad_frames(rows):
    D = rows.shape[1]
    return jnp.pad(rows.reshape(-1, PATCHES, D), ((0, 0), (0, PAD - PATCHES), (0, 0)))


def strip_frames(rows):
    D = rows.shape[2]
    return rows[:, :PATCHES].reshape(-1, D)


def shards(tokens, cotangent, attn_qkv, attn_out, mlp_in, mlp_out, norm_gains, biases, hidden_bias):
    D = tokens.shape[1]
    depth = mlp_in.shape[1]
    cols = attn_qkv.shape[4]
    units = mlp_in.shape[2]
    everyone = ("dp", "tensor")
    own = jnp.concatenate(
        [
            attn_qkv[0, 0].reshape(depth, 3 * cols),
            attn_out[0, 0].T,
            attn_qkv[0, 1].reshape(depth, 3 * cols),
            attn_out[0, 1].T,
            mlp_in[0],
            mlp_out[0].T,
        ],
        axis=1,
    )
    weights = lax.all_gather(own, ("tensor", "dp"), axis=0, tiled=True).reshape(2, D, own.shape[1])
    small = jnp.concatenate(
        [biases[0].reshape(-1), norm_gains[0].reshape(-1), hidden_bias[0].reshape(-1)]
    )
    small = lax.all_gather(small.reshape(1, -1), everyone, axis=0, tiled=True)
    devices = small.shape[0]
    share = D // devices
    vec = small[:, : 13 * share].reshape(devices, 13, share).transpose(1, 0, 2).reshape(13, D)
    hidden = small[:, 13 * share :].reshape(2, units)

    x = pad_frames(tokens)
    stream1, s_qkv, s_mix, s_p, s_r = spatial_fwd(x, weights, 0, vec)
    x1 = to_patch_groups(stream1)
    x2, t_qkv, t_mix, t_p, t_r = temporal_fwd(x1, weights, 1, vec)
    cot = to_patch_groups(pad_frames(cotangent))
    out_b, up2, g_in, g_down, gv_m, g_hidden = mlp_both(x2, cot, weights, 2, vec, hidden)
    output = strip_frames(to_frames(out_b))
    up1, g_t, gv_t = temporal_bwd(x1, up2, t_qkv, t_mix, t_p, t_r, weights, 1, vec)
    up1 = to_frames(up1)
    up0, g_s, gv_s = spatial_bwd(x, up1, s_qkv, s_mix, s_p, s_r, weights, 0, vec)
    grad_tokens = strip_frames(up0)

    def scatter(grad):
        return lax.psum_scatter(
            grad.reshape(2 * D, grad.shape[2]), ("tensor", "dp"), scatter_dimension=0, tiled=True
        ).astype(F32)

    g_in, g_down, g_t, g_s = scatter(g_in), scatter(g_down), scatter(g_t), scatter(g_s)
    grad_qkv = jnp.stack([g[:, : 3 * cols].reshape(depth, 3, cols) for g in (g_s, g_t)])[None]
    grad_out = jnp.stack([g[:, 3 * cols :].T for g in (g_s, g_t)])[None]
    vec_grad = jnp.concatenate([gv_s[0:4], gv_t[0:4], gv_m[0:1], gv_m[3:4], gv_s[4:5], gv_t[4:5], gv_m[4:5]])
    small_grad = jnp.concatenate(
        [
            vec_grad.reshape(13, devices, share).transpose(1, 0, 2).reshape(devices, 13 * share),
            g_hidden.reshape(devices, -1),
        ],
        axis=1,
    )
    small_grad = lax.psum_scatter(small_grad, everyone, scatter_dimension=0, tiled=True)[0]
    grad_biases = small_grad[: 10 * share].reshape(1, 10, share)
    grad_gains = small_grad[10 * share : 13 * share].reshape(1, 3, share)
    grad_hidden = small_grad[13 * share :].reshape(1, -1)
    return (
        output,
        grad_tokens,
        grad_qkv,
        grad_out,
        g_in[None],
        g_down.T[None],
        grad_gains,
        grad_biases,
        grad_hidden,
    )


def solution(mesh):
    placed = (
        P(("dp", "tensor"), None),
        P(("dp", "tensor"), None),
        P(None, None, "dp", None, "tensor"),
        P(None, None, "tensor", "dp"),
        P(None, "dp", "tensor"),
        P(None, "tensor", "dp"),
        P(None, None, ("dp", "tensor")),
        P(None, None, ("dp", "tensor")),
        P(None, ("dp", "tensor")),
    )
    return jax.shard_map(
        shards, mesh=mesh, in_specs=placed, out_specs=placed, check_vma=False
    )
```

time: 1710 us -> 828 us (0.48)
  local copies, waits for them, and re-layouts: 425 us -> 52.1 us
  matrix products: 330 us -> 0 us
  Pallas kernels: 0 us -> 279 us
  waiting for transfers between devices: 619 us -> 362 us
  other arithmetic: 145 us -> 6.21 us
  blocking collectives: 165 us -> 108 us
    dot_general x29 -> x0, matrix products: 316 us -> none  [the longest x1 57.2 us: mlp_forward(): jnp.dot(gathered, w_in, preferred_element_type=jnp.float32)]
    pallas_call x0 -> x5, Pallas kernels: none -> 279 us  [the longest x1 81.8 us: mlp_both(): pl.pallas_call(mlp_kernel, grid=(rows // n,), in_specs=[pl.BlockSpec((n,...]
    convert_element_type x26 -> x0, local copies, waits for them, and re-layouts: 207 us -> none  [the longest x5 47.8 us: attention_forward(): key_rows = projected[:, 1].astype(jnp.bfloat16)]
    all_gather x10 -> x1, waiting for transfers between devices: 198 us -> 64.7 us  [shards(): lax.all_gather(own, ('tensor', 'dp'), axis=0, tiled=True)]
    unnamed x22 -> x5, waiting for transfers between devices: 122 us -> 1.07 us
    all_gather x2 -> x0, blocking collectives: 82.2 us -> none  [the longest x1 44.3 us: fetch_vectors(): lax.all_gather(biases[layer_index], ('dp', 'tensor'), axis=1, tiled=True)]
    slice x11 -> x18, local copies, waits for them, and re-layouts: 76.3 us -> 9.53 us  [the longest x2 5.11 us: strip_frames(): return rows[:, :PATCHES].reshape(-1, D)]
    reduce_sum x16 -> x0, other arithmetic: 60.9 us -> none  [the longest x5 22.4 us: layer_norm(): return centred * lax.rsqrt(variance + EPSILON) * gain_row + shift_row]
  transfers between devices with their start and end apart: 20 -> 6, of which waited for: 15 -> 4; matrix products, arithmetic and copies ran while one was open for 27% -> 5% of each run, Pallas kernels for 0% -> 7%
where the time goes in v1:
time: 828 us; the launch traced here: 826 us
  waiting for transfers between devices  362 us (44%)
  Pallas kernels  279 us (34%)
  blocking collectives  108 us (13%)
  local copies, waits for them, and re-layouts  52.1 us (6%)
  between operations  14.4 us (2%)
    reduce_scatter x4, waiting for transfers between devices, scatter(): lax.psum_scatter(grad.reshape(2 * D, grad.shape[2]), ('tensor', 'dp'), sc...  296 us
    unnamed x2, blocking collectives  86.1 us
    pallas_call x1, Pallas kernels, mlp_both(): pl.pallas_call(mlp_kernel, grid=(rows // n,), in_specs=[pl.BlockSpec((n,...  81.8 us
    all_gather x1, waiting for transfers between devices, shards(): lax.all_gather(own, ('tensor', 'dp'), axis=0, tiled=True)  64.7 us
    pallas_call x1, Pallas kernels, spatial_bwd(): pl.pallas_call(spatial_bwd_kernel, grid=(frames,), in_specs=[pl.BlockSpec...  58.4 us
    pallas_call x1, Pallas kernels, temporal_bwd(): pl.pallas_call(functools.partial(temporal_bwd_kernel, rows), grid=(steps,...  58 us
    pallas_call x1, Pallas kernels, temporal_fwd(): pl.pallas_call(functools.partial(temporal_fwd_kernel, rows), grid=(steps,...  53.7 us
    pallas_call x1, Pallas kernels, spatial_fwd(): pl.pallas_call(spatial_fwd_kernel, grid=(frames,), in_specs=[pl.BlockSpec...  27.5 us
  transfers between devices with their start and end apart: 6, of which 4 were waited for; matrix products, arithmetic and copies ran while one was open for 5% of the time, Pallas kernels for 7%

profile of v1, /device:TPU:0, one launch (start us, length us, event | category | flops | bytes accessed | tf_op | source)
XLA Modules:
  0.0 825.5 jit_solution(11790033410524594796)
XLA Ops:
  7.2 1.0 fusion
  12.7 2.6 reshape.127
  15.5 1.6 copy.86
  17.1 3.8 all-to-all-start.1
  21.5 43.6 %all-reduce.2 = f32[13056]{0:T(1024)S(1)} all-reduce(f32[13056]{0:T(1024)S(1)} %maximum_dynamic-update-slice_fusion), channel_id=2, replica_groups=mesh['dp'=16,'tensor'=2] {'dp','tensor'}, use_global_device_ids=true, to_apply=%add.2 | all-reduce | flops 13056 | bytes 104448
  65.3 4.1 reshape.119
  69.4 3.4 pad.7.x_ref
  73.8 1.8 copy.87
  76.3 64.7 %all-gather.3.cloned.1.call-done = bf16[1536,6144]{1,0:T(8,128)(2,1)} async-done(((bf16[48,6144]{1,0:T(8,128)(2,1)}), bf16[1536,6144]{1,0:T(8,128)(2,1)}) %all-gather.3.cloned.1.call-update) | async-done | bytes 18874384 | tf_op jit(solution)/shard_map/all_gather | solution.py:552
  141.0 27.5 %spatial_fwd.1 = (f32[8,208,768]{2,1,0:T(8,128)}, bf16[8,2,208,1152]{3,2,1,0:T(8,128)(2,1)}, bf16[8,2,208,384]{3,2,1,0:T(8,128)(2,1)}, bf16[8,12,208,208]{3,2,1,0:T(8,128)(2,1)}, f32[8,208,128]{2,1,0:T(8,128)}) custom-call(bf16[8,208,768]{2,1,0:T(8,128)(2,1)} %pad.7.x_ref, bf16[2,768,6144]{2,1,0:T(8,128)(2,1)} %bitcast.94, f32[13,768]{1,0:T(8,128)} %reshape.123.vec_ref), custom_call_target="tpu_custom_call" | custom-call | tf_op jit(solution)/shard_map/spatial_fwd/pallas_call | solution.py:137
  168.5 2.8 copy.84
  171.3 7.8 all_to_all.60
  179.2 2.8 copy.85
  182.0 53.7 %temporal_fwd.1 = (f32[1664,768]{1,0:T(8,128)}, bf16[2,1792,1152]{2,1,0:T(8,128)(2,1)}, bf16[2,1792,384]{2,1,0:T(8,128)(2,1)}, bf16[12,1792,128]{2,1,0:T(8,128)(2,1)}, f32[1792,128]{1,0:T(8,128)}) custom-call(f32[1664,768]{1,0:T(8,128)} %bitcast.100, bf16[2,768,6144]{2,1,0:T(8,128)(2,1)} %bitcast.95, f32[13,768]{1,0:T(8,128)} %reshape.123.vec_ref), custom_call_target="tpu_custom_call" | custom-call | tf_op jit(solution)/shard_map/temporal_fwd/pallas_call | solution.py:323
  235.6 81.8 %mlp_both.1 = (bf16[1664,768]{1,0:T(8,128)(2,1)}, f32[1664,768]{1,0:T(8,128)}, bf16[2,768,1536]{2,1,0:T(8,128)(2,1)}, bf16[2,768,1536]{2,1,0:T(8,128)(2,1)}, f32[8,768]{1,0:T(8,128)}, /*index=5*/f32[2,1536]{1,0:T(2,128)}) custom-call(f32[1664,768]{1,0:T(8,128)} %get-tuple-element.32.x_ref, bf16[1664,768]{1,0:T(8,128)(2,1)} %bitcast.110, ...), custom_call_target="tpu_custom_call" | custom-call | tf_op jit(solution)/shard_map/mlp_both/pallas_call | solution.py:472
  317.4 58.0 %temporal_bwd.1 = (f32[1664,768]{1,0:T(8,128)}, bf16[2,768,1536]{2,1,0:T(8,128)(2,1)}, f32[8,768]{1,0:T(8,128)}) custom-call(f32[1664,768]{1,0:T(8,128)} %bitcast.101, f32[1664,768]{1,0:T(8,128)} %get-tuple-element.34.up_ref, bf16[2,1792,1152]{2,1,0:T(8,128)(2,1)} %get-tuple-element.35.qkv_ref, bf16[2,1792,384]{2,1,0:T(8,128)(2,1)} %get-tuple-element.36.mix_ref, ...), custom_call_target="tpu_custom_call" | custom-call | tf_op jit(solution)/shard_map/temporal_bwd/pallas_call | solution.py:386
  375.5 2.8 copy.106
  378.3 8.2 all_to_all.61
  386.5 2.7 copy.93
  389.2 58.4 %spatial_bwd.1 = (f32[8,208,768]{2,1,0:T(8,128)}, bf16[2,768,1536]{2,1,0:T(8,128)(2,1)}, f32[8,768]{1,0:T(8,128)}) custom-call(bf16[8,208,768]{2,1,0:T(8,128)(2,1)} %pad.7.x_ref, f32[8,208,768]{2,1,0:T(8,128)} %bitcast.102, bf16[8,2,208,1152]{3,2,1,0:T(8,128)(2,1)} %get-tuple-element.40.qkv_ref, bf16[8,2,208,384]{3,2,1,0:T(8,128)(2,1)} %get-tuple-element.41.mix_ref, ...), custom_call_target="tpu_custom_call" | custom-call | tf_op jit(solution)/shard_map/spatial_bwd/pallas_call | solution.py:237
  449.6 5.8 all_to_all.62
  455.8 2.1 reshape.135
  457.9 5.0 slice.76
  462.8 5.2 reshape.139
  469.4 42.5 %all-reduce.3 = f32[32,408]{0,1:T(8,128)S(1)} all-reduce(f32[32,408]{0,1:T(8,128)S(1)} %pad_maximum_fusion), channel_id=7, replica_groups=mesh['dp'=16,'tensor'=2] {'dp','tensor'}, use_global_device_ids=true, to_apply=%region_4.5.clone | all-reduce | flops 13056 | bytes 104448
  515.3 78.1 %reduce-scatter.6.cloned.1.call-done = bf16[48,1536]{1,0:T(8,128)(2,1)} async-done(((bf16[1536,1536]{1,0:T(8,128)(2,1)}), bf16[48,1536]{1,0:T(8,128)(2,1)}) %reduce-scatter.6.cloned.1.call-update) | async-done | bytes 147472 | tf_op jit(solution)/shard_map/reduce_scatter | solution.py:575
  595.3 0.9 convert_element_type.12
  596.3 0.9 convert_element_type.11
  597.9 106.9 %reduce-scatter.10.cloned.1.call-done = bf16[48,1536]{1,0:T(8,128)(2,1)} async-done(((bf16[1536,1536]{1,0:T(8,128)(2,1)}), bf16[48,1536]{1,0:T(8,128)(2,1)}) %reduce-scatter.10.cloned.1.call-update) | async-done | bytes 147472 | tf_op jit(solution)/shard_map/reduce_scatter | solution.py:575
  704.8 1.6 bitcast_convert_fusion
  706.5 110.7 %reduce-scatter.12.cloned.1.call-done = bf16[48,1536]{1,0:T(8,128)(2,1)} async-done(((bf16[1536,1536]{1,0:T(8,128)(2,1)}), bf16[48,1536]{1,0:T(8,128)(2,1)}) %reduce-scatter.12.cloned.1.call-update) | async-done | bytes 147472 | tf_op jit(solution)/shard_map/reduce_scatter | solution.py:575
  817.2 1.6 convert_bitcast_fusion
  (81 shorter events, 16.6 us)
Async XLA Ops:
  7.2 133.8 %all-gather.3.cloned.1.call-start = ((), (), s32[]{:S(2)}) async-start(), calls=%async_computation.8 | async-start | bytes 19464192 | tf_op jit(solution)/shard_map/all_gather | solution.py:552
  11.8 0.8 copy-start.1
  15.5 5.6 copy-start.6
  15.5 5.7 copy-start.5
  15.5 5.8 copy-start.7
  17.1 56.7 %all-to-all-start.1 = ((bf16[8,2,104,768]{3,2,0,1:T(8,128)(2,1)}), bf16[8,2,104,768]{3,2,0,1:T(8,128)(2,1)S(1)}, u32[]{:S(2)}, u32[]{:S(2)}) async-start(bf16[8,2,104,768]{3,2,0,1:T(8,128)(2,1)} %copy.86), calls=%async_computation.1 | async-start | bytes 5111808 | tf_op jit(solution)/shard_map/all_to_all | solution.py:507
  21.0 493.3 %reduce-scatter.8.cloned.1.call-start = ((), (), s32[]{:S(2)}) async-start(), calls=%async_computation.10 | async-start | bytes 4866048 | tf_op jit(solution)/shard_map/reduce_scatter | solution.py:575
  375.5 217.9 %reduce-scatter.6.cloned.1.call-start = ((), (), s32[]{:S(2)}) async-start(), calls=%async_computation.9 | async-start | bytes 4866048 | tf_op jit(solution)/shard_map/reduce_scatter | solution.py:575
  447.6 257.2 %reduce-scatter.10.cloned.1.call-start = ((), (), s32[]{:S(2)}) async-start(), calls=%async_computation.11 | async-start | bytes 4866048 | tf_op jit(solution)/shard_map/reduce_scatter | solution.py:575
  447.7 1.1 copy-start.4
  447.7 1.1 copy-start.3
  447.7 1.8 copy-start
  448.2 369.0 %reduce-scatter.12.cloned.1.call-start = ((), (), s32[]{:S(2)}) async-start(), calls=%async_computation.12 | async-start | bytes 4866048 | tf_op jit(solution)/shard_map/reduce_scatter | solution.py:575
  462.8 5.2 copy-start.2
Sparse Core Ops, SparseCore 0:
  12.8 128.1 all-gather.2
  375.6 105.2 reduce-scatter.7
  487.2 106.0 reduce-scatter.5
  598.7 106.0 reduce-scatter.9
  711.1 106.0 reduce-scatter.11

commit v2 on v1

--- a/solution.py
+++ b/solution.py
@@ -128,7 +128,7 @@
     s_ref[0] = x + branch
 
 
-def spatial_fwd(x, weights, section, vec):
+def spatial_fwd(x, weights, vec):
     frames = x.shape[0]
     D = x.shape[2]
     cols = D // 2
@@ -139,7 +139,7 @@
         grid=(frames,),
         in_specs=[
             pl.BlockSpec((1, PAD, D), lambda i: (i, 0, 0)),
-            pl.BlockSpec((2, D, 4 * cols), lambda i: (0, 0, section)),
+            pl.BlockSpec((2, D, 4 * cols), lambda i: (0, 0, 0)),
             whole(*vec.shape),
         ],
         out_specs=[
@@ -228,7 +228,7 @@
         gb_ref[...] = gw_ref[...].astype(BF)
 
 
-def spatial_bwd(x, up, qkv, mix, p, r, weights, section, vec):
+def spatial_bwd(x, up, qkv, mix, p, r, weights, vec):
     frames = x.shape[0]
     D = x.shape[2]
     cols = D // 2
@@ -244,7 +244,7 @@
             pl.BlockSpec((1, 2, PAD, cols), lambda i: (i, 0, 0, 0)),
             pl.BlockSpec((1, heads, PAD, PAD), lambda i: (i, 0, 0, 0)),
             pl.BlockSpec((1, PAD, 128), lambda i: (i, 0, 0)),
-            pl.BlockSpec((2, D, 4 * cols), lambda i: (0, 0, section)),
+            pl.BlockSpec((2, D, 4 * cols), lambda i: (0, 0, 0)),
             whole(*vec.shape),
         ],
         out_specs=[
@@ -312,7 +312,7 @@
     s_ref[...] = x + branch
 
 
-def temporal_fwd(x, weights, section, vec):
+def temporal_fwd(x, weights, vec):
     rows, D = x.shape
     cols = D // 2
     heads = D // HEAD
@@ -325,7 +325,7 @@
         grid=(steps,),
         in_specs=[
             pl.BlockSpec((n, D), lambda i: (i, 0)),
-            pl.BlockSpec((2, D, 4 * cols), lambda i: (0, 0, section)),
+            pl.BlockSpec((2, D, 4 * cols), lambda i: (0, 0, 0)),
             whole(*vec.shape),
         ],
         out_specs=[
@@ -376,7 +376,7 @@
         gb_ref[...] = gw_ref[...].astype(BF)
 
 
-def temporal_bwd(x, up, qkv, mix, p, r, weights, section, vec):
+def temporal_bwd(x, up, qkv, mix, p, r, weights, vec):
     rows, D = x.shape
     cols = D // 2
     heads = D // HEAD
@@ -393,7 +393,7 @@
             pl.BlockSpec((2, n, cols), lambda i: (0, i, 0)),
             pl.BlockSpec((heads, n, GROUP), lambda i: (0, i, 0)),
             pl.BlockSpec((n, 128), lambda i: (i, 0)),
-            pl.BlockSpec((2, D, 4 * cols), lambda i: (0, 0, section)),
+            pl.BlockSpec((2, D, 4 * cols), lambda i: (0, 0, 0)),
             whole(*vec.shape),
         ],
         out_specs=[
@@ -463,7 +463,7 @@
         go_ref[...] = ao_ref[...].astype(BF)
 
 
-def mlp_both(x, cot, weights, section, vec, hidden):
+def mlp_both(x, cot, w_in, w_down, vec, hidden):
     rows, D = x.shape
     width = hidden.shape[1]
     n = MLP_ROWS
@@ -475,8 +475,8 @@
         in_specs=[
             pl.BlockSpec((n, D), lambda i: (i, 0)),
             pl.BlockSpec((n, D), lambda i: (i, 0)),
-            pl.BlockSpec((2, D, width), lambda i: (0, 0, section), pipeline_mode=one),
-            pl.BlockSpec((2, D, width), lambda i: (0, 0, section + 1), pipeline_mode=one),
+            pl.BlockSpec((2, D, width), lambda i: (0, 0, 0), pipeline_mode=one),
+            pl.BlockSpec((2, D, width), lambda i: (0, 0, 0), pipeline_mode=one),
             whole(*vec.shape),
             whole(*hidden.shape),
         ],
@@ -499,7 +499,392 @@
         scratch_shapes=[pltpu.VMEM((2, D, width), F32), pltpu.VMEM((2, D, width), F32)],
         name="mlp_both",
         compiler_params=pltpu.CompilerParams(vmem_limit_bytes=VMEM_BYTES),
-    )(x, cot, weights, weights, vec, hidden)
+    )(x, cot, w_in, w_down, vec, hidden)
+
+
+MESH = pl.DeviceIdType.MESH
+
+
+class Place:
+    def __init__(self, lines):
+        self.lines = lines
+        self.dp = lax.axis_index("dp")
+        self.t = lax.axis_index("tensor")
+        self.z = self.dp // 4
+        self.y = (self.dp // 2) % 2
+        self.x = self.dp % 2
+        self.a = self.y * (1 - self.t) + self.x * self.t
+        self.b = self.x * (1 - self.t) + self.y * self.t
+        toward_y = self.dp + 2 - 4 * self.y
+        toward_x = self.dp + 1 - 2 * self.x
+        self.first = (toward_y * (1 - self.t) + toward_x * self.t, self.t)
+        self.second = (toward_x * (1 - self.t) + toward_y * self.t, self.t)
+        self.core = (self.dp, 1 - self.t)
+        self.up = (self.dp + 4, self.t)
+        self.down = (self.dp - 4, self.t)
+
+    def yx(self, a, b, t):
+        return a * (1 - t) + b * t, b * (1 - t) + a * t
+
+    def greet(self):
+        bar = pltpu.get_barrier_semaphore()
+        for who in (self.core, self.first, self.second):
+            pl.semaphore_signal(bar, inc=1, device_id=who, device_id_type=MESH)
+
+        @pl.when(self.z > 0)
+        def _():
+            pl.semaphore_signal(bar, inc=1, device_id=self.down, device_id_type=MESH)
+
+        @pl.when(self.z < self.lines - 1)
+        def _():
+            pl.semaphore_signal(bar, inc=1, device_id=self.up, device_id_type=MESH)
+
+        inner = (self.z > 0).astype(jnp.int32) + (self.z < self.lines - 1).astype(jnp.int32)
+        pl.semaphore_wait(bar, 3 + inner)
+
+
+def remote(src, dst, sems, i, who):
+    return pltpu.make_async_remote_copy(
+        src_ref=src, dst_ref=dst, send_sem=sems[0].at[i], recv_sem=sems[1].at[i],
+        device_id=who, device_id_type=MESH,
+    )
+
+
+class Reduce:
+    @staticmethod
+    def scratch(lines, rows, width, dtype):
+        block = (rows, width)
+        n = 4 + 2 * lines
+        return [
+            pltpu.VMEM((lines, 2, 2) + block, dtype),
+            pltpu.VMEM((lines, 2, 2) + block, dtype),
+            pltpu.VMEM((lines, 2) + block, dtype),
+            pltpu.VMEM((lines,) + block, dtype),
+            pltpu.VMEM((lines,) + block, dtype),
+            pltpu.VMEM((lines,) + block, dtype),
+            pltpu.SemaphoreType.DMA((n,)),
+            pltpu.SemaphoreType.DMA((n,)),
+            pltpu.SemaphoreType.DMA((4,)),
+        ]
+
+    n_scratch = 9
+
+    def __init__(self, place, g_ref, out_ref, scratch):
+        self.p = place
+        self.g, self.out = g_ref, out_ref
+        self.own, self.land0, self.land1, self.land2, self.from_down, self.from_up = scratch[:6]
+        self.sems = scratch[6:8]
+        self.local = scratch[8]
+        self.stages = 3 + place.lines
+
+    def _core(self):
+        p = self.p
+        copies = []
+        for a in range(2):
+            for b in range(2):
+                y, x = p.yx(a, b, 1 - p.t)
+                copies.append(
+                    remote(self.g.at[1 - p.t, :, y, x], self.land0.at[:, a, b], self.sems, 2 * a + b, p.core)
+                )
+        return copies
+
+    def _load(self):
+        p = self.p
+        copies = []
+        for a in range(2):
+            for b in range(2):
+                y, x = p.yx(a, b, p.t)
+                copies.append(
+                    pltpu.make_async_copy(self.g.at[p.t, :, y, x], self.own.at[:, a, b], self.local.at[2 * a + b])
+                )
+        return copies
+
+    def _first(self):
+        p = self.p
+        return remote(self.own.at[:, 1 - p.a], self.land1, self.sems, 4, p.first)
+
+    def _second(self):
+        p = self.p
+        return remote(self.own.at[:, p.a, 1 - p.b], self.land2, self.sems, 5, p.second)
+
+    def _up(self, slab, i):
+        return remote(self.from_down.at[slab], self.from_down.at[slab], self.sems, 6 + i, self.p.up)
+
+    def _down(self, slab, i):
+        return remote(self.from_up.at[slab], self.from_up.at[slab], self.sems, 6 + self.p.lines - 1 + i, self.p.down)
+
+    def stage(self, k):
+        p, n = self.p, self.p.lines
+        add = lambda u, v: (u.astype(F32) + v.astype(F32)).astype(self.own.dtype)
+        if k == 0:
+            for c in self._core():
+                c.start()
+            for c in self._load():
+                c.start()
+        elif k == 1:
+            for c in self._load():
+                c.wait()
+            for c in self._core():
+                c.wait()
+
+            def body(i, _):
+                self.own[i] = add(self.own[i], self.land0[i])
+                return _
+
+            lax.fori_loop(0, n, body, 0)
+            self._first().start()
+        elif k == 2:
+            self._first().wait()
+
+            def body(i, _):
+                self.own[i, p.a] = add(self.own[i, p.a], self.land1[i])
+                return _
+
+            lax.fori_loop(0, n, body, 0)
+            self._second().start()
+        elif k == 3:
+            self._second().wait()
+
+            def body(i, _):
+                total = add(self.own[i, p.a, p.b], self.land2[i])
+                self.own[i, p.a, p.b] = total
+                return _
+
+            lax.fori_loop(0, n, body, 0)
+            self._line(0)
+        elif k < 3 + n - 1:
+            self._line(k - 3)
+        else:
+            self._finish()
+
+    def _line(self, step):
+        p, n = self.p, self.p.lines
+        for z in range(n):
+            mine = lambda slab: self.own[slab, p.a, p.b]
+            @pl.when(p.z == z)
+            def _():
+                if z < n - 1:
+                    for d in range(z + 1, n):
+                        i = n - 1 - d
+                        if z + i == step:
+                            if z > 0:
+                                self._up_wait(d, i)
+                                self.from_down[d] = (
+                                    self.from_down[d].astype(F32) + mine(d).astype(F32)
+                                ).astype(self.own.dtype)
+                            else:
+                                self.from_down[d] = mine(d)
+                            self._up(d, i).start()
+                if z > 0:
+                    for d in range(0, z):
+                        i = d
+                        if (n - 1 - z) + i == step:
+                            if z < n - 1:
+                                self._down_wait(d, i)
+                                self.from_up[d] = (
+                                    self.from_up[d].astype(F32) + mine(d).astype(F32)
+                                ).astype(self.own.dtype)
+                            else:
+                                self.from_up[d] = mine(d)
+                            self._down(d, i).start()
+
+    def _up_wait(self, d, i):
+        self._up(d, i).wait_recv()
+
+    def _down_wait(self, d, i):
+        self._down(d, i).wait_recv()
+
+    def _finish(self):
+        p, n = self.p, self.p.lines
+        for z in range(n):
+            @pl.when(p.z == z)
+            def _():
+                total = self.own[z, p.a, p.b].astype(F32)
+                if z > 0:
+                    self._up_wait(z, n - 1 - z)
+                    total = total + self.from_down[z].astype(F32)
+                if z < n - 1:
+                    self._down_wait(z, z)
+                    total = total + self.from_up[z].astype(F32)
+                self.out[...] = total
+                for d in range(z + 1, n):
+                    self._up(d, n - 1 - d).wait_send()
+                for d in range(0, z):
+                    self._down(d, d).wait_send()
+
+
+def reduce_kernel(n, lines, *refs):
+    place = Place(lines)
+    place.greet()
+    g_refs, out_refs, scratch = refs[:n], refs[n : 2 * n], refs[2 * n :]
+    m = Reduce.n_scratch
+    jobs = [Reduce(place, g_refs[i], out_refs[i], scratch[i * m : (i + 1) * m]) for i in range(n)]
+    for step in range(jobs[0].stages + n - 1):
+        for i, job in enumerate(jobs):
+            if 0 <= step - i < job.stages:
+                job.stage(step - i)
+
+
+def reduce_all(grads, lines, collective_id):
+    n = len(grads)
+    shapes = []
+    for g in grads:
+        shapes += Reduce.scratch(lines, g.shape[4], g.shape[5], g.dtype)
+    return pl.pallas_call(
+        functools.partial(reduce_kernel, n, lines),
+        in_specs=[pl.BlockSpec(memory_space=pl.ANY)] * n,
+        out_specs=[pl.BlockSpec(memory_space=pltpu.VMEM)] * n,
+        out_shape=[jax.ShapeDtypeStruct(g.shape[4:], F32) for g in grads],
+        scratch_shapes=shapes,
+        name="reduce_all",
+        compiler_params=pltpu.CompilerParams(
+            collective_id=collective_id, has_side_effects=True, vmem_limit_bytes=60 * 1024 * 1024
+        ),
+    )(*grads)
+
+
+class Gather:
+    @staticmethod
+    def scratch(lines):
+        n = 2 * (lines - 1) + 5
+        return [pltpu.SemaphoreType.DMA((n,)), pltpu.SemaphoreType.DMA((n,)), pltpu.SemaphoreType.DMA((1,))]
+
+    n_scratch = 3
+
+    def __init__(self, place, own_ref, full_ref, scratch):
+        self.p, self.own, self.full = place, own_ref, full_ref
+        self.sems, self.local = scratch[:2], scratch[2]
+        self.hops = place.lines - 1
+        self.stages = self.hops + 4
+
+    def _slab(self, z):
+        p = self.p
+        return self.full.at[p.t, z, p.y, p.x]
+
+    def _up(self, k):
+        src = self.own if k == 0 else self._slab(self.p.z - k)
+        return remote(src, self._slab(self.p.z - k), self.sems, k, self.p.up)
+
+    def _down(self, k):
+        src = self.own if k == 0 else self._slab(self.p.z + k)
+        return remote(src, self._slab(self.p.z + k), self.sems, self.hops + k, self.p.down)
+
+    def _send_line(self, k):
+        p = self.p
+
+        @pl.when((p.z < self.hops) & (p.z >= k))
+        def _():
+            self._up(k).start()
+
+        @pl.when((p.z > 0) & (p.z + k <= self.hops))
+        def _():
+            self._down(k).start()
+
+    def _take_line(self, k):
+        p = self.p
+
+        @pl.when(p.z >= k + 1)
+        def _():
+            self._up(k).wait_recv()
+
+        @pl.when(p.z + k + 1 <= self.hops)
+        def _():
+            self._down(k).wait_recv()
+
+    def _column(self, i, who, y, x):
+        block = self.full.at[self.p.t, :, y, x]
+        return remote(block, block, self.sems, 2 * self.hops + i, who)
+
+    def _first(self):
+        return self._column(0, self.p.first, self.p.y, self.p.x)
+
+    def _plane(self, i, who, b):
+        p = self.p
+        block0 = self.full.at[p.t, :, :, b]
+        block1 = self.full.at[p.t, :, b, :]
+        return (
+            remote(block0, block0, self.sems, 2 * self.hops + i, who),
+            remote(block1, block1, self.sems, 2 * self.hops + i, who),
+        )
+
+    def _each(self, pair, act):
+        @pl.when(self.p.t == 0)
+        def _():
+            act(pair[0])
+
+        @pl.when(self.p.t == 1)
+        def _():
+            act(pair[1])
+
+    def _core(self, i):
+        p = self.p
+        if i == 0:
+            return self._column(2, p.core, p.y, p.x)
+        y, x = p.yx(1 - p.a, p.b, p.t)
+        return self._column(3, p.core, y, x)
+
+    def stage(self, k):
+        p = self.p
+        if k == 0:
+            pltpu.make_async_copy(self.own, self._slab(p.z), self.local.at[0]).start()
+            self._send_line(0)
+        elif k < self.hops:
+            self._take_line(k - 1)
+            self._send_line(k)
+        elif k == self.hops:
+            self._take_line(k - 1)
+            pltpu.make_async_copy(self.own, self._slab(p.z), self.local.at[0]).wait()
+            self._first().start()
+            self._core(0).start()
+        elif k == self.hops + 1:
+            self._first().wait_recv()
+            self._each(self._plane(1, p.second, p.b), lambda c: c.start())
+            self._core(1).start()
+        elif k == self.hops + 2:
+            self._each(self._plane(1, p.second, p.b), lambda c: c.wait_recv())
+            self._each(self._plane(4, p.core, 1 - p.b), lambda c: c.start())
+        else:
+            self._core(0).wait()
+            self._core(1).wait()
+            self._each(self._plane(4, p.core, 1 - p.b), lambda c: c.wait())
+            self._first().wait_send()
+            self._each(self._plane(1, p.second, p.b), lambda c: c.wait_send())
+            for k in range(self.hops):
+                @pl.when((p.z < self.hops) & (p.z >= k))
+                def _():
+                    self._up(k).wait_send()
+
+                @pl.when((p.z > 0) & (p.z + k <= self.hops))
+                def _():
+                    self._down(k).wait_send()
+
+
+def gather_kernel(n, lines, *refs):
+    place = Place(lines)
+    place.greet()
+    own_refs, full_refs, scratch = refs[:n], refs[n : 2 * n], refs[2 * n :]
+    m = Gather.n_scratch
+    jobs = [Gather(place, own_refs[i], full_refs[i], scratch[i * m : (i + 1) * m]) for i in range(n)]
+    for step in range(jobs[0].stages + n - 1):
+        for i, job in enumerate(jobs):
+            if 0 <= step - i < job.stages:
+                job.stage(step - i)
+
+
+def gather_all(owns, lines, collective_id):
+    n = len(owns)
+    scratch = []
+    for _ in owns:
+        scratch += Gather.scratch(lines)
+    return pl.pallas_call(
+        functools.partial(gather_kernel, n, lines),
+        in_specs=[pl.BlockSpec(memory_space=pl.ANY)] * n,
+        out_specs=[pl.BlockSpec(memory_space=pl.ANY)] * n,
+        out_shape=[jax.ShapeDtypeStruct((2, lines, 2, 2) + o.shape, o.dtype) for o in owns],
+        scratch_shapes=scratch,
+        name="gather_all",
+        compiler_params=pltpu.CompilerParams(collective_id=collective_id, has_side_effects=True),
+    )(*owns)
 
 
 def to_patch_groups(rows):
@@ -538,47 +923,44 @@
     cols = attn_qkv.shape[4]
     units = mlp_in.shape[2]
     everyone = ("dp", "tensor")
-    own = jnp.concatenate(
-        [
-            attn_qkv[0, 0].reshape(depth, 3 * cols),
-            attn_out[0, 0].T,
-            attn_qkv[0, 1].reshape(depth, 3 * cols),
-            attn_out[0, 1].T,
-            mlp_in[0],
-            mlp_out[0].T,
-        ],
-        axis=1,
-    )
-    weights = lax.all_gather(own, ("tensor", "dp"), axis=0, tiled=True).reshape(2, D, own.shape[1])
+    owns = [
+        jnp.concatenate([attn_qkv[0, s].reshape(depth, 3 * cols), attn_out[0, s].T], axis=1)
+        for s in range(2)
+    ]
+    owns += [mlp_in[0], mlp_out[0].T]
     small = jnp.concatenate(
         [biases[0].reshape(-1), norm_gains[0].reshape(-1), hidden_bias[0].reshape(-1)]
     )
-    small = lax.all_gather(small.reshape(1, -1), everyone, axis=0, tiled=True)
+    count = small.shape[0]
+    direct = depth % 16 == 0
+    if direct:
+        lines = D // depth // 4
+        tile = jnp.pad(small, (0, 1024 - count)).reshape(8, 128)
+        tile, *weights = gather_all([tile] + owns, lines, 1)
+        small = tile.reshape(2, D // depth, 1024).transpose(1, 0, 2).reshape(-1, 1024)[:, :count]
+        weights = [w.reshape(2, D, w.shape[5]) for w in weights]
+    else:
+        small = lax.all_gather(small.reshape(1, -1), everyone, axis=0, tiled=True)
+        weights = [
+            lax.all_gather(w, ("tensor", "dp"), axis=0, tiled=True).reshape(2, D, -1) for w in owns
+        ]
     devices = small.shape[0]
     share = D // devices
     vec = small[:, : 13 * share].reshape(devices, 13, share).transpose(1, 0, 2).reshape(13, D)
     hidden = small[:, 13 * share :].reshape(2, units)
 
     x = pad_frames(tokens)
-    stream1, s_qkv, s_mix, s_p, s_r = spatial_fwd(x, weights, 0, vec)
+    stream1, s_qkv, s_mix, s_p, s_r = spatial_fwd(x, weights[0], vec)
     x1 = to_patch_groups(stream1)
-    x2, t_qkv, t_mix, t_p, t_r = temporal_fwd(x1, weights, 1, vec)
+    x2, t_qkv, t_mix, t_p, t_r = temporal_fwd(x1, weights[1], vec)
     cot = to_patch_groups(pad_frames(cotangent))
-    out_b, up2, g_in, g_down, gv_m, g_hidden = mlp_both(x2, cot, weights, 2, vec, hidden)
+    out_b, up2, g_in, g_down, gv_m, g_hidden = mlp_both(x2, cot, weights[2], weights[3], vec, hidden)
     output = strip_frames(to_frames(out_b))
-    up1, g_t, gv_t = temporal_bwd(x1, up2, t_qkv, t_mix, t_p, t_r, weights, 1, vec)
+    up1, g_t, gv_t = temporal_bwd(x1, up2, t_qkv, t_mix, t_p, t_r, weights[1], vec)
     up1 = to_frames(up1)
-    up0, g_s, gv_s = spatial_bwd(x, up1, s_qkv, s_mix, s_p, s_r, weights, 0, vec)
+    up0, g_s, gv_s = spatial_bwd(x, up1, s_qkv, s_mix, s_p, s_r, weights[0], vec)
     grad_tokens = strip_frames(up0)
 
-    def scatter(grad):
-        return lax.psum_scatter(
-            grad.reshape(2 * D, grad.shape[2]), ("tensor", "dp"), scatter_dimension=0, tiled=True
-        ).astype(F32)
-
-    g_in, g_down, g_t, g_s = scatter(g_in), scatter(g_down), scatter(g_t), scatter(g_s)
-    grad_qkv = jnp.stack([g[:, : 3 * cols].reshape(depth, 3, cols) for g in (g_s, g_t)])[None]
-    grad_out = jnp.stack([g[:, 3 * cols :].T for g in (g_s, g_t)])[None]
     vec_grad = jnp.concatenate([gv_s[0:4], gv_t[0:4], gv_m[0:1], gv_m[3:4], gv_s[4:5], gv_t[4:5], gv_m[4:5]])
     small_grad = jnp.concatenate(
         [
@@ -587,7 +969,24 @@
         ],
         axis=1,
     )
-    small_grad = lax.psum_scatter(small_grad, everyone, scatter_dimension=0, tiled=True)[0]
+    grads = [g_s, g_t, g_in, g_down]
+    if direct:
+        tiles = jnp.pad(small_grad, ((0, 0), (0, 1024 - count))).reshape(-1, 2, 8, 128)
+        tiles = tiles.transpose(1, 0, 2, 3).reshape(2, lines, 2, 2, 8, 128)
+        grads = [g.reshape(2, lines, 2, 2, depth, g.shape[2]) for g in grads]
+        *grads, small_grad = reduce_all(grads + [tiles], lines, 2)
+        small_grad = small_grad.reshape(-1)[:count]
+    else:
+        grads = [
+            lax.psum_scatter(
+                g.reshape(2 * D, g.shape[2]), ("tensor", "dp"), scatter_dimension=0, tiled=True
+            ).astype(F32)
+            for g in grads
+        ]
+        small_grad = lax.psum_scatter(small_grad, everyone, scatter_dimension=0, tiled=True)[0]
+    g_s, g_t, g_in, g_down = grads
+    grad_qkv = jnp.stack([g[:, : 3 * cols].reshape(depth, 3, cols) for g in (g_s, g_t)])[None]
+    grad_out = jnp.stack([g[:, 3 * cols :].T for g in (g_s, g_t)])[None]
     grad_biases = small_grad[: 10 * share].reshape(1, 10, share)
     grad_gains = small_grad[10 * share : 13 * share].reshape(1, 3, share)
     grad_hidden = small_grad[13 * share :].reshape(1, -1)

time: 828 us -> 612 us (0.74)
  waiting for transfers between devices: 362 us -> 6.21 us
  Pallas kernels: 279 us -> 507 us
  blocking collectives: 108 us -> 0 us
  starting transfers between devices: 4.04 us -> 19.7 us
  local copies, waits for them, and re-layouts: 52.1 us -> 66.5 us
  between operations: 14.4 us -> 1.19 us
    reduce_scatter x4 -> x0, waiting for transfers between devices: 296 us -> none  [scatter(): lax.psum_scatter(grad.reshape(2 * D, grad.shape[2]), ('tensor', 'dp'), sc...]
    pallas_call x0 -> x2, Pallas kernels: none -> 230 us  [the longest x1 115 us: gather_all(): pl.pallas_call(functools.partial(gather_kernel, n, lines), in_specs=[pl.B...]
    unnamed x2 -> x0, blocking collectives: 86.1 us -> none
    all_gather x1 -> x0, waiting for transfers between devices: 64.7 us -> none  [shards(): lax.all_gather(own, ('tensor', 'dp'), axis=0, tiled=True)]
    all_to_all x3 -> x0, blocking collectives: 21.8 us -> none  [the longest x2 14 us: to_frames(): lax.all_to_all(blocks.reshape(2 * frames, 1, PAD // 2, D), 'tensor', spli...]
    all_to_all x0 -> x2, starting transfers between devices: none -> 10 us  [to_frames(): lax.all_to_all(blocks.reshape(2 * frames, 1, PAD // 2, D), 'tensor', spli...]
  transfers between devices with their start and end apart: 6 -> 4, of which waited for: 4 -> 2; matrix products, arithmetic and copies ran while one was open for 5% -> 8% of each run, Pallas kernels for 7% -> 52%
where the time goes in v2:
time: 612 us; the launch traced here: 603 us
  Pallas kernels  507 us (83%)
  local copies, waits for them, and re-layouts  66.5 us (11%)
  starting transfers between devices  19.7 us (3%)
  waiting for transfers between devices  6.21 us (1%)
    pallas_call x1, Pallas kernels, gather_all(): pl.pallas_call(functools.partial(gather_kernel, n, lines), in_specs=[pl.B...  115 us
    pallas_call x1, Pallas kernels, reduce_all(): pl.pallas_call(functools.partial(reduce_kernel, n, lines), in_specs=[pl.B...  115 us
    pallas_call x1, Pallas kernels, mlp_both(): pl.pallas_call(mlp_kernel, grid=(rows // n,), in_specs=[pl.BlockSpec((n,...  80.3 us
    pallas_call x1, Pallas kernels, spatial_bwd(): pl.pallas_call(spatial_bwd_kernel, grid=(frames,), in_specs=[pl.BlockSpec...  58.4 us
    pallas_call x1, Pallas kernels, temporal_bwd(): pl.pallas_call(functools.partial(temporal_bwd_kernel, rows), grid=(steps,...  58.1 us
    pallas_call x1, Pallas kernels, temporal_fwd(): pl.pallas_call(functools.partial(temporal_fwd_kernel, rows), grid=(steps,...  53.7 us
    pallas_call x1, Pallas kernels, spatial_fwd(): pl.pallas_call(spatial_fwd_kernel, grid=(frames,), in_specs=[pl.BlockSpec...  27.5 us
  transfers between devices with their start and end apart: 4, of which 2 were waited for; matrix products, arithmetic and copies ran while one was open for 8% of the time, Pallas kernels for 52%

profile of v2, /device:TPU:0, one launch (start us, length us, event | category | flops | bytes accessed | tf_op | source)
XLA Modules:
  0.0 603.3 jit_solution(15554178011933639007)
XLA Ops:
  0.6 2.6 reshape.150
  3.5 1.6 copy.68
  5.1 3.8 all-to-all-start.1
  10.9 114.8 %gather_all.1 = (f32[2,4,2,2,8,128]{5,4,3,2,1,0:T(8,128)}, bf16[2,4,2,2,48,1536]{5,4,3,2,1,0:T(8,128)(2,1)}, bf16[2,4,2,2,48,1536]{5,4,3,2,1,0:T(8,128)(2,1)}, b...) custom-call(f32[8,128]{1,0:T(8,128)} %fusion.1.refs_0_, ...), custom_call_target="tpu_custom_call" | custom-call | tf_op jit(solution)/shard_map/gather_all/pallas_call | solution.py:879
  125.7 0.9 reshape.142
  126.9 4.1 reshape.139
  131.0 3.4 pad.15.x_ref
  135.4 27.5 %spatial_fwd.1 = (f32[8,208,768]{2,1,0:T(8,128)}, bf16[8,2,208,1152]{3,2,1,0:T(8,128)(2,1)}, bf16[8,2,208,384]{3,2,1,0:T(8,128)(2,1)}, bf16[8,12,208,208]{3,2,1,0:T(8,128)(2,1)}, f32[8,208,128]{2,1,0:T(8,128)}) custom-call(bf16[8,208,768]{2,1,0:T(8,128)(2,1)} %pad.15.x_ref, bf16[2,768,1536]{2,1,0:T(8,128)(2,1)} %bitcast.111, f32[13,768]{1,0:T(8,128)} %reshape.145.vec_ref), custom_call_target="tpu_custom_call" | custom-call | tf_op jit(solution)/shard_map/spatial_fwd/pallas_call | solution.py:137
  162.8 5.1 copy.66
  168.0 5.9 all-to-all-start
  173.8 1.7 copy.69
  176.2 2.8 all-to-all-done
  179.0 5.2 copy.67
  184.2 53.7 %temporal_fwd.1 = (f32[1664,768]{1,0:T(8,128)}, bf16[2,1792,1152]{2,1,0:T(8,128)(2,1)}, bf16[2,1792,384]{2,1,0:T(8,128)(2,1)}, bf16[12,1792,128]{2,1,0:T(8,128)(2,1)}, f32[1792,128]{1,0:T(8,128)}) custom-call(f32[1664,768]{1,0:T(8,128)} %bitcast.107, bf16[2,768,1536]{2,1,0:T(8,128)(2,1)} %bitcast.113, f32[13,768]{1,0:T(8,128)} %reshape.145.vec_ref), custom_call_target="tpu_custom_call" | custom-call | tf_op jit(solution)/shard_map/temporal_fwd/pallas_call | solution.py:323
  237.9 80.3 %mlp_both.1 = (bf16[1664,768]{1,0:T(8,128)(2,1)}, f32[1664,768]{1,0:T(8,128)}, bf16[2,768,1536]{2,1,0:T(8,128)(2,1)}, bf16[2,768,1536]{2,1,0:T(8,128)(2,1)}, f32[8,768]{1,0:T(8,128)}, /*index=5*/f32[2,1536]{1,0:T(2,128)}) custom-call(f32[1664,768]{1,0:T(8,128)} %get-tuple-element.45.x_ref, bf16[1664,768]{1,0:T(8,128)(2,1)} %bitcast.115, ...), custom_call_target="tpu_custom_call" | custom-call | tf_op jit(solution)/shard_map/mlp_both/pallas_call | solution.py:472
  318.2 58.1 %temporal_bwd.1 = (f32[1664,768]{1,0:T(8,128)}, bf16[2,768,1536]{2,1,0:T(8,128)(2,1)}, f32[8,768]{1,0:T(8,128)}) custom-call(f32[1664,768]{1,0:T(8,128)} %bitcast.108, f32[1664,768]{1,0:T(8,128)} %get-tuple-element.49.up_ref, bf16[2,1792,1152]{2,1,0:T(8,128)(2,1)} %get-tuple-element.50.qkv_ref, bf16[2,1792,384]{2,1,0:T(8,128)(2,1)} %get-tuple-element.51.mix_ref, ...), custom_call_target="tpu_custom_call" | custom-call | tf_op jit(solution)/shard_map/temporal_bwd/pallas_call | solution.py:386
  376.3 5.1 copy.87
  381.4 6.2 %all-to-all-start.3 = ((f32[16,1,104,768]{3,2,1,0:T(8,128)}), f32[16,1,104,768]{3,2,1,0:T(8,128)}, u32[]{:S(2)}, u32[]{:S(2)}) async-start(f32[16,1,104,768]{3,2,1,0:T(8,128)} %bitcast.110), calls=%async_computation.3 | async-start | bytes 10223616 | tf_op jit(solution)/shard_map/all_to_all | solution.py:904
  387.7 1.6 copy.88
  389.3 3.4 all-to-all-done.3
  392.8 3.8 all-to-all-start.2
  396.6 5.3 copy.75
  401.9 58.4 %spatial_bwd.1 = (f32[8,208,768]{2,1,0:T(8,128)}, bf16[2,768,1536]{2,1,0:T(8,128)(2,1)}, f32[8,768]{1,0:T(8,128)}) custom-call(bf16[8,208,768]{2,1,0:T(8,128)(2,1)} %pad.15.x_ref, f32[8,208,768]{2,1,0:T(8,128)} %bitcast.109, bf16[8,2,208,1152]{3,2,1,0:T(8,128)(2,1)} %get-tuple-element.55.qkv_ref, bf16[8,2,208,384]{3,2,1,0:T(8,128)(2,1)} %get-tuple-element.56.mix_ref, ...), custom_call_target="tpu_custom_call" | custom-call | tf_op jit(solution)/shard_map/spatial_bwd/pallas_call | solution.py:237
  464.0 114.7 %reduce_all.1 = (f32[48,1536]{1,0:T(8,128)}, f32[48,1536]{1,0:T(8,128)}, f32[48,1536]{1,0:T(8,128)}, f32[48,1536]{1,0:T(8,128)}, f32[8,128]{1,0:T(8,128)}) custom-call(bf16[2,4,2,2,48,1536]{5,4,3,2,1,0:T(8,128)(2,1)} %bitcast.127, bf16[2,4,2,2,48,1536]{5,4,3,2,1,0:T(8,128)(2,1)} %bitcast.126, bf16[2,4,2,2,48,1536]{5,4,3,2,1,0:T(8,128)(2,1)} %bitcast.124, ...), custom_call_target="tpu_custom_call" | custom-call | tf_op jit(solution)/shard_map/reduce_all/pallas_call | solution.py:733
  578.7 1.3 slice_bitcast_fusion.4
  582.3 0.9 slice.88
  583.2 0.9 slice_bitcast_fusion
  584.1 0.9 slice.89
  585.1 4.9 slice.80
  590.0 5.2 reshape.164
  595.5 2.1 reshape.160
  600.7 1.7 copy.92
  (67 shorter events, 14.1 us)
Async XLA Ops:
  3.4 5.6 copy-start.7
  3.5 5.7 copy-start.6
  3.5 5.8 copy-start.3
  3.5 5.8 copy-start.2
  3.5 6.0 copy-start.8
  5.1 162.8 %all-to-all-start.1 = ((bf16[8,2,104,768]{3,2,0,1:T(8,128)(2,1)}), bf16[8,2,104,768]{3,2,0,1:T(8,128)(2,1)S(1)}, u32[]{:S(2)}, u32[]{:S(2)}) async-start(bf16[8,2,104,768]{3,2,0,1:T(8,128)(2,1)} %copy.68), calls=%async_computation.1 | async-start | bytes 5111808 | tf_op jit(solution)/shard_map/all_to_all | solution.py:892
  168.0 11.0 %all-to-all-start = ((f32[8,2,104,768]{3,2,0,1:T(8,128)}), f32[8,2,104,768]{3,2,0,1:T(8,128)}, u32[]{:S(2)}, u32[]{:S(2)}) async-start(f32[8,2,104,768]{3,2,0,1:T(8,128)} %copy.66), calls=%async_computation | async-start | bytes 10223616 | tf_op jit(solution)/shard_map/all_to_all | solution.py:892
  381.4 6.2 %copy-start.5 = (f32[8,768]{1,0:T(8,128)S(1)}, f32[8,768]{1,0:T(8,128)}, u32[]{:S(2)}) copy-start(f32[8,768]{1,0:T(8,128)} %get-tuple-element.65) | copy-start | bytes 73732
  381.4 6.2 %copy-start = (bf16[1664,768]{1,0:T(8,128)(2,1)S(1)}, bf16[1664,768]{1,0:T(8,128)(2,1)}, u32[]{:S(2)}) copy-start(bf16[1664,768]{1,0:T(8,128)(2,1)} %get-tuple-element.48) | copy-start | bytes 7667716
  381.4 11.3 %all-to-all-start.3 = ((f32[16,1,104,768]{3,2,1,0:T(8,128)}), f32[16,1,104,768]{3,2,1,0:T(8,128)}, u32[]{:S(2)}, u32[]{:S(2)}) async-start(f32[16,1,104,768]{3,2,1,0:T(8,128)} %bitcast.110), calls=%async_computation.3 | async-start | bytes 10223616 | tf_op jit(solution)/shard_map/all_to_all | solution.py:904
  392.8 202.4 %all-to-all-start.2 = ((bf16[16,1,104,768]{3,2,1,0:T(8,128)(2,1)}), bf16[16,1,104,768]{3,2,1,0:T(8,128)(2,1)S(1)}, u32[]{:S(2)}, u32[]{:S(2)}) async-start(bf16[16,1,104,768]{3,2,1,0:T(8,128)(2,1)} %bitcast.105), calls=%async_computation.2 | async-start | bytes 5111808 | tf_op jit(solution)/shard_map/all_to_all | solution.py:904
  401.9 60.7 %copy-start.4 = (f32[2,1536]{1,0:T(2,128)S(1)}, f32[2,1536]{1,0:T(2,128)}, u32[]{:S(2)}) copy-start(f32[2,1536]{1,0:T(2,128)} %get-tuple-element.67) | copy-start | bytes 36868
  595.5 6.9 %copy-start.1 = (f32[48,1536]{1,0:T(8,128)S(1)}, f32[48,1536]{1,0:T(8,128)}, u32[]{:S(2)}) copy-start(f32[48,1536]{1,0:T(8,128)} %get-tuple-element.71) | copy-start | bytes 884740

commit v3 on v1

v3 whole, which is shorter than its diff:
```python
import functools
import jax
import jax.numpy as jnp
from jax import lax
from jax.experimental import pallas as pl
from jax.experimental.pallas import tpu as pltpu
from jax.sharding import PartitionSpec as P

HEAD = 64
FRAMES = 16
PATCHES = 196
PAD = 208
EPSILON = 1e-06
BF = jnp.bfloat16
F32 = jnp.float32
NN = (((1,), (0,)), ((), ()))
NT = (((1,), (1,)), ((), ()))
TN = (((0,), (0,)), ((), ()))
VMEM_BYTES = 60 * 1024 * 1024


def dot(a, b, dims):
    return lax.dot_general(a, b, dims, preferred_element_type=F32)


def norm_parts(x):
    mean = jnp.mean(x, axis=-1, keepdims=True)
    centred = x - mean
    var = jnp.mean(centred * centred, axis=-1, keepdims=True)
    rstd = lax.rsqrt(var + EPSILON)
    return centred * rstd, rstd


def norm_back(grad_normed, xhat, rstd, gain):
    scaled = grad_normed * gain
    first = jnp.mean(scaled, axis=-1, keepdims=True)
    second = jnp.mean(scaled * xhat, axis=-1, keepdims=True)
    return rstd * (scaled - first - xhat * second)


def split_halves(pair):
    lane = lax.broadcasted_iota(jnp.int32, pair.shape, 1)
    zero = jnp.zeros_like(pair)
    return jnp.where(lane < HEAD, pair, zero), jnp.where(lane < HEAD, zero, pair)


def project(normed, w_ref, vec_ref, row_base, cols):
    parts = []
    for g in range(2):
        w = w_ref[g, :, 0 : 3 * cols]
        qkv = dot(normed, w, NN)
        bq = vec_ref[row_base + 1 : row_base + 2, g * cols : (g + 1) * cols]
        bv = vec_ref[row_base + 2 : row_base + 3, g * cols : (g + 1) * cols]
        q = (qkv[:, :cols] + bq).astype(BF) * BF(0.125)
        k = qkv[:, cols : 2 * cols].astype(BF)
        v = (qkv[:, 2 * cols :] + bv).astype(BF)
        parts.append((q, k, v))
    return parts


def stack_halves(pair):
    return jnp.concatenate(split_halves(pair), axis=0)


def merge_halves(both):
    rows = both.shape[0] // 2
    lane = lax.broadcasted_iota(jnp.int32, (rows, both.shape[1]), 1)
    return jnp.where(lane < HEAD, both[:rows], both[rows:])


def heads_forward(pairs, mask):
    scores = [dot(stack_halves(q), k, NT) for q, k, _ in pairs]
    exps, recips = [], []
    for s in scores:
        s = jnp.where(mask, s, -1e30)
        e = jnp.exp(s - jnp.max(s, axis=-1, keepdims=True))
        recips.append(1.0 / jnp.sum(e, axis=-1, keepdims=True))
        exps.append(e.astype(BF))
    outs = [merge_halves(dot(e, v, NN) * r) for e, r, (_, _, v) in zip(exps, recips, pairs)]
    return outs, exps, recips


def heads_backward(pairs):
    dors, deltas = [], []
    for q, k, v, o, do, e, r in pairs:
        both = stack_halves(do.astype(F32)) * r
        deltas.append(jnp.sum(both * jnp.concatenate([o, o], axis=0).astype(F32), axis=-1, keepdims=True))
        dors.append(both.astype(BF))
    dps = [dot(dor, p[2], NT) for dor, p in zip(dors, pairs)]
    dss = [(p[5].astype(F32) * (dp - delta)).astype(BF) for dp, delta, p in zip(dps, deltas, pairs)]
    dq = [(merge_halves(dot(ds, p[1], NN)) * 0.125).astype(BF) for ds, p in zip(dss, pairs)]
    dk = [dot(ds, stack_halves(p[0]), TN).astype(BF) for ds, p in zip(dss, pairs)]
    dv = [dot(p[5], dor, TN).astype(BF) for dor, p in zip(dors, pairs)]
    return dq, dk, dv


def spatial_mask():
    return lax.broadcasted_iota(jnp.int32, (2 * PAD, PAD), 1) < PATCHES


def attn_back_common(x, ub, up, w_ref, vec_ref, row_base, gain_row, mix_of, qkv_of, exps_of, gw_ref, gv_ref, cols, blocks):
    xhat, rstd = norm_parts(x)
    gain = vec_ref[gain_row : gain_row + 1, :]
    normed = (xhat * gain + vec_ref[row_base : row_base + 1, :]).astype(BF)
    dn = None
    gv_ref[3:4, :] += jnp.sum(up, axis=0, keepdims=True)
    rows = x.shape[0]
    step = rows // blocks
    for g in range(2):
        wo = w_ref[g, :, 3 * cols : 4 * cols]
        dmix = dot(ub, wo, NN).astype(BF)
        mix = mix_of(g)
        gw_ref[g, :, 3 * cols : 4 * cols] += dot(ub, mix, TN)
        parts = [[], [], []]
        for b in range(blocks):
            rs = slice(step * b, step * (b + 1))
            pairs = []
            for j in range(cols // 128):
                sl = slice(128 * j, 128 * (j + 1))
                q, k, v = qkv_of(g, j, rs)
                e, r = exps_of(g * (cols // 128) + j, b)
                pairs.append((q, k, v, mix[rs, sl], dmix[rs, sl], e, r))
            for part, got in zip(parts, heads_backward(pairs)):
                part.append(jnp.concatenate(got, axis=1))
        dq, dk, dv = [jnp.concatenate(part, axis=0) for part in parts]
        span = slice(g * cols, (g + 1) * cols)
        gv_ref[1:2, span] += jnp.sum(dq.astype(F32), axis=0, keepdims=True)
        gv_ref[2:3, span] += jnp.sum(dv.astype(F32), axis=0, keepdims=True)
        dqkv = jnp.concatenate([dq, dk, dv], axis=1)
        gw_ref[g, :, 0 : 3 * cols] += dot(normed, dqkv, TN)
        term = dot(dqkv, w_ref[g, :, 0 : 3 * cols], NT)
        dn = term if dn is None else dn + term
    gv_ref[0:1, :] += jnp.sum(dn, axis=0, keepdims=True)
    gv_ref[4:5, :] += jnp.sum(dn * xhat, axis=0, keepdims=True)
    return up + norm_back(dn, xhat, rstd, gain)


MESH = pl.DeviceIdType.MESH


class Place:
    def __init__(self, lines):
        self.lines = lines
        self.dp = lax.axis_index("dp")
        self.t = lax.axis_index("tensor")
        self.z = self.dp // 4
        self.y = (self.dp // 2) % 2
        self.x = self.dp % 2
        self.a = self.y * (1 - self.t) + self.x * self.t
        self.b = self.x * (1 - self.t) + self.y * self.t
        toward_y = self.dp + 2 - 4 * self.y
        toward_x = self.dp + 1 - 2 * self.x
        self.first = (toward_y * (1 - self.t) + toward_x * self.t, self.t)
        self.second = (toward_x * (1 - self.t) + toward_y * self.t, self.t)
        self.core = (self.dp, 1 - self.t)
        self.up = (self.dp + 4, self.t)
        self.down = (self.dp - 4, self.t)

    def yx(self, a, b, t):
        return a * (1 - t) + b * t, b * (1 - t) + a * t

    def greet(self, line):
        bar = pltpu.get_barrier_semaphore()
        for who in (self.core, self.first, self.second):
            pl.semaphore_signal(bar, inc=1, device_id=who, device_id_type=MESH)
        if not line:
            pl.semaphore_wait(bar, 3)
            return

        @pl.when(self.z > 0)
        def _():
            pl.semaphore_signal(bar, inc=1, device_id=self.down, device_id_type=MESH)

        @pl.when(self.z < self.lines - 1)
        def _():
            pl.semaphore_signal(bar, inc=1, device_id=self.up, device_id_type=MESH)

        inner = (self.z > 0).astype(jnp.int32) + (self.z < self.lines - 1).astype(jnp.int32)
        pl.semaphore_wait(bar, 3 + inner)


def remote(src, dst, sems, i, who):
    return pltpu.make_async_remote_copy(
        src_ref=src, dst_ref=dst, send_sem=sems[0].at[i], recv_sem=sems[1].at[i],
        device_id=who, device_id_type=MESH,
    )


def dma_sems(n):
    return pltpu.SemaphoreType.DMA((n,))


class LineGather:
    @staticmethod
    def scratch(lines):
        return [dma_sems(2 * (lines - 1)), dma_sems(2 * (lines - 1)), dma_sems(1)]

    def __init__(self, place, own_ref, col_ref, scratch):
        self.p, self.own, self.col = place, own_ref, col_ref
        self.sems, self.local = scratch[:2], scratch[2]
        self.hops = place.lines - 1
        self.stages = self.hops + 1

    def _keep(self):
        return pltpu.make_async_copy(self.own, self.col.at[self.p.z], self.local.at[0])

    def _up(self, k):
        block = self.col.at[self.p.z - k]
        return remote(self.own if k == 0 else block, block, self.sems, k, self.p.up)

    def _down(self, k):
        block = self.col.at[self.p.z + k]
        return remote(self.own if k == 0 else block, block, self.sems, self.hops + k, self.p.down)

    def _each(self, k, up, down):
        p = self.p

        @pl.when((p.z < self.hops) & (p.z >= k))
        def _():
            up(self._up(k))

        @pl.when((p.z > 0) & (p.z + k <= self.hops))
        def _():
            down(self._down(k))

    def _take(self, k):
        p = self.p

        @pl.when(p.z >= k + 1)
        def _():
            self._up(k).wait_recv()

        @pl.when(p.z + k + 1 <= self.hops)
        def _():
            self._down(k).wait_recv()

    def stage(self, k):
        start = lambda c: c.start()
        if k == 0:
            self._keep().start()
            self._each(0, start, start)
            return
        self._take(k - 1)
        if k < self.hops:
            self._each(k, start, start)
        else:
            self._keep().wait()
            done = lambda c: c.wait_send()
            for i in range(self.hops):
                self._each(i, done, done)


class PlaneGather:
    @staticmethod
    def scratch():
        return [dma_sems(5), dma_sems(5), dma_sems(1)]

    stages = 4

    def __init__(self, place, col_ref, full_ref, scratch):
        self.p, self.col, self.full = place, col_ref, full_ref
        self.sems, self.local = scratch[:2], scratch[2]

    def _keep(self):
        p = self.p
        return pltpu.make_async_copy(self.col, self.full.at[p.t, :, p.y, p.x], self.local.at[0])

    def _own(self, i, who):
        p = self.p
        return remote(self.col, self.full.at[p.t, :, p.y, p.x], self.sems, i, who)

    def _plane(self, i, who, b, act):
        p = self.p
        block0 = self.full.at[p.t, :, :, b]
        block1 = self.full.at[p.t, :, b, :]

        @pl.when(p.t == 0)
        def _():
            act(remote(block0, block0, self.sems, i, who))

        @pl.when(p.t == 1)
        def _():
            act(remote(block1, block1, self.sems, i, who))

    def _pass_on(self):
        p = self.p
        y, x = p.yx(1 - p.a, p.b, p.t)
        block = self.full.at[p.t, :, y, x]
        return remote(block, block, self.sems, 3, p.core)

    def stage(self, k):
        p = self.p
        if k == 0:
            self._keep().start()
            self._own(0, p.first).start()
            self._own(2, p.core).start()
        elif k == 1:
            self._keep().wait()
            self._own(0, p.first).wait_recv()
            self._plane(1, p.second, p.b, lambda c: c.start())
            self._pass_on().start()
        elif k == 2:
            self._plane(1, p.second, p.b, lambda c: c.wait_recv())
            self._plane(4, p.core, 1 - p.b, lambda c: c.start())
        else:
            self._own(2, p.core).wait()
            self._pass_on().wait()
            self._plane(4, p.core, 1 - p.b, lambda c: c.wait())
            self._own(0, p.first).wait_send()
            self._plane(1, p.second, p.b, lambda c: c.wait_send())


def add_blocks(u, v, dtype):
    return (u.astype(F32) + v.astype(F32)).astype(dtype)


class PlaneReduce:
    @staticmethod
    def scratch(lines, rows, width, dtype):
        block = (rows, width)
        return [
            pltpu.VMEM((lines, 2, 2) + block, dtype),
            pltpu.VMEM((lines, 2, 2) + block, dtype),
            pltpu.VMEM((lines, 2) + block, dtype),
            pltpu.VMEM((lines,) + block, dtype),
            dma_sems(6),
            dma_sems(6),
            dma_sems(4),
        ]

    n_scratch = 7
    stages = 4

    def __init__(self, place, g_ref, col_ref, scratch, span=None):
        self.p, self.g, self.col = place, g_ref, col_ref
        self.own, self.land0, self.land1, self.land2 = scratch[:4]
        self.sems, self.local = scratch[4:6], scratch[6]
        self.span = span

    def _part(self, t, y, x):
        if self.span is None:
            return self.g.at[t, :, y, x]
        return self.g.at[t, :, y, x, :, self.span]

    def _core(self):
        p, copies = self.p, []
        for a in range(2):
            for b in range(2):
                y, x = p.yx(a, b, 1 - p.t)
                copies.append(remote(self._part(1 - p.t, y, x), self.land0.at[:, a, b], self.sems, 2 * a + b, p.core))
        return copies

    def _load(self):
        p, copies = self.p, []
        for a in range(2):
            for b in range(2):
                y, x = p.yx(a, b, p.t)
                copies.append(
                    pltpu.make_async_copy(self._part(p.t, y, x), self.own.at[:, a, b], self.local.at[2 * a + b])
                )
        return copies

    def _first(self):
        return remote(self.own.at[:, 1 - self.p.a], self.land1, self.sems, 4, self.p.first)

    def _second(self):
        return remote(self.own.at[:, self.p.a, 1 - self.p.b], self.land2, self.sems, 5, self.p.second)

    def stage(self, k):
        p, dtype = self.p, self.own.dtype
        if k == 0:
            for c in self._core() + self._load():
                c.start()
            return
        if k == 1:
            for c in self._load() + self._core():
                c.wait()

            def away(i, _):
                self.own[i, 1 - p.a] = add_blocks(self.own[i, 1 - p.a], self.land0[i, 1 - p.a], dtype)
                return _

            lax.fori_loop(0, p.lines, away, 0)
            self._first().start()

            def stay(i, _):
                self.own[i, p.a] = add_blocks(self.own[i, p.a], self.land0[i, p.a], dtype)
                return _

            lax.fori_loop(0, p.lines, stay, 0)
        elif k == 2:
            self._first().wait()

            def body(i, _):
                self.own[i, p.a] = add_blocks(self.own[i, p.a], self.land1[i], dtype)
                return _

            lax.fori_loop(0, p.lines, body, 0)
            self._second().start()
        else:
            self._second().wait()

            def body(i, _):
                self.col[i] = add_blocks(self.own[i, p.a, p.b], self.land2[i], dtype)
                return _

            lax.fori_loop(0, p.lines, body, 0)


class LineReduce:
    @staticmethod
    def scratch(lines, rows, width, dtype):
        return [
            pltpu.VMEM((lines, rows, width), dtype),
            pltpu.VMEM((lines, rows, width), dtype),
            dma_sems(2 * (lines - 1)),
            dma_sems(2 * (lines - 1)),
        ]

    n_scratch = 4

    def __init__(self, place, col_ref, out_ref, scratch):
        self.p, self.col, self.out = place, col_ref, out_ref
        self.from_down, self.from_up = scratch[:2]
        self.sems = scratch[2:4]
        self.stages = place.lines

    def _up(self, d):
        block = self.from_down.at[d]
        return remote(block, block, self.sems, d - 1, self.p.up)

    def _down(self, d):
        block = self.from_up.at[d]
        return remote(block, block, self.sems, self.p.lines - 1 + d, self.p.down)

    def stage(self, step):
        p, n = self.p, self.p.lines
        dtype = self.from_down.dtype
        for z in range(n):
            sends_up = [d for d in range(z + 1, n) if z + (n - 1 - d) == step]
            sends_down = [d for d in range(z) if (n - 1 - z) + d == step]
            if step == n - 1:
                pass
            elif not sends_up and not sends_down:
                continue

            @pl.when(p.z == z)
            def _():
                for d in sends_up:
                    if z > 0:
                        self._up(d).wait_recv()
                        self.from_down[d] = add_blocks(self.from_down[d], self.col[d], dtype)
                    else:
                        self.from_down[d] = self.col[d]
                    self._up(d).start()
                for d in sends_down:
                    if z < n - 1:
                        self._down(d).wait_recv()
                        self.from_up[d] = add_blocks(self.from_up[d], self.col[d], dtype)
                    else:
                        self.from_up[d] = self.col[d]
                    self._down(d).start()
                if step == n - 1:
                    total = self.col[z].astype(F32)
                    if z > 0:
                        self._up(z).wait_recv()
                        total = total + self.from_down[z].astype(F32)
                    if z < n - 1:
                        self._down(z).wait_recv()
                        total = total + self.from_up[z].astype(F32)
                    self.out[...] = total
                    for d in range(z + 1, n):
                        self._up(d).wait_send()
                    for d in range(z):
                        self._down(d).wait_send()


def at_step(step, *stages):
    @pl.when(pl.program_id(0) == step)
    def _():
        for job, k in stages:
            job.stage(k)


def take(refs, *counts):
    out, i = [], 0
    for c in counts:
        out.append(refs[i : i + c])
        i += c
    return out


GROUP = 8 * FRAMES
STEP_GROUPS = 2


def temporal_mask():
    a = lax.broadcasted_iota(jnp.int32, (2 * GROUP, GROUP), 0)
    b = lax.broadcasted_iota(jnp.int32, (2 * GROUP, GROUP), 1)
    return (a % 8) == (b % 8)


def any_spec():
    return pl.BlockSpec(memory_space=pl.ANY)


def whole_spec(shape):
    return pl.BlockSpec(tuple(shape), lambda i: (0,) * len(shape))


def struct(shape, dtype):
    return jax.ShapeDtypeStruct(tuple(shape), dtype)


def full_shape(lines, rows, width):
    return (2, lines, 2, 2, rows, width)


def kernel_params(collective_id):
    if collective_id is None:
        return pltpu.CompilerParams(vmem_limit_bytes=VMEM_BYTES)
    return pltpu.CompilerParams(
        vmem_limit_bytes=VMEM_BYTES, collective_id=collective_id, has_side_effects=True
    )


def first_body(lines, tok, cot, tile, own0, own1, own2, x_out, cot_b, full_tile, full0, col_tile, col0, col1, col2,
               tok_v, cot_v, frames_v, ex_send, ex_recv, ex_local, loads, *scratch):
    place = Place(lines)
    t = place.t
    load_cot = pltpu.make_async_copy(cot, cot_v, loads.at[0])
    load_tok = pltpu.make_async_copy(tok, tok_v, loads.at[1])
    load_cot.start()
    load_tok.start()
    place.greet(True)
    parts = take(scratch, 3, 3, 3, 3, 3, 3)
    tile_line = LineGather(place, tile, col_tile, parts[0])
    line0 = LineGather(place, own0, col0, parts[1])
    line1 = LineGather(place, own1, col1, parts[2])
    line2 = LineGather(place, own2, col2, parts[3])
    tile_plane = PlaneGather(place, col_tile, full_tile, parts[4])
    plane0 = PlaneGather(place, col0, full0, parts[5])
    hops = lines - 1

    def line_stage(k):
        tile_line.stage(k)
        line0.stage(k)

    line_stage(0)
    frames = x_out.shape[0]
    half = frames // 2
    D = x_out.shape[2]
    zeros = jnp.zeros((PAD - PATCHES, D), F32)
    load_cot.wait()
    for part in range(2):
        rows = cot_v[half * PATCHES * part : half * PATCHES * (part + 1)].astype(F32)
        for f in range(half):
            frame = jnp.concatenate([rows[PATCHES * f : PATCHES * (f + 1)], zeros], axis=0)
            frames_v[half * part + f] = frame.reshape(PAD // 8, 8, D)
    groups = PAD // 16
    mine = pltpu.make_async_copy(
        frames_v.at[:, pl.ds(groups * t, groups)], cot_b.at[pl.ds(frames * t, frames)], ex_local.at[0]
    )
    theirs = remote(
        frames_v.at[:, pl.ds(groups * (1 - t), groups)], cot_b.at[pl.ds(frames * t, frames)],
        (ex_send, ex_recv), 0, place.core,
    )
    mine.start()
    theirs.start()
    line_stage(1)
    load_tok.wait()
    for part in range(2):
        rows = tok_v[half * PATCHES * part : half * PATCHES * (part + 1)].astype(F32)
        for f in range(half):
            frame = jnp.concatenate([rows[PATCHES * f : PATCHES * (f + 1)], zeros], axis=0)
            x_out[half * part + f] = frame.astype(BF)
    for k in range(2, hops + 1):
        line_stage(k)
    tile_plane.stage(0)
    plane0.stage(0)
    line1.stage(0)
    line1.stage(1)
    tile_plane.stage(1)
    plane0.stage(1)
    for k in range(2, hops + 1):
        line1.stage(k)
    for k in range(hops):
        line2.stage(k)
    tile_plane.stage(2)
    plane0.stage(2)
    line2.stage(hops)
    tile_plane.stage(3)
    plane0.stage(3)
    mine.wait()
    theirs.wait()


def first_call(tokens, cot, tile, own0, own1, own2, lines, collective_id):
    rows, D = tokens.shape
    frames = rows // PATCHES
    groups = PAD // 16
    depth, width = own0.shape
    line = LineGather.scratch(lines)
    plane = PlaneGather.scratch()
    return pl.pallas_call(
        functools.partial(first_body, lines),
        in_specs=[any_spec()] * 6,
        out_specs=[pl.BlockSpec(memory_space=pltpu.VMEM)] + [any_spec()] * 7,
        out_shape=[
            struct((frames, PAD, D), BF),
            struct((2 * frames, groups, 8, D), F32),
            struct(full_shape(lines, 8, 128), F32),
            struct(full_shape(lines, depth, width), BF),
            struct((lines, 8, 128), F32),
            struct((lines, depth, width), BF),
            struct((lines, depth, width), BF),
            struct((lines, depth, width), BF),
        ],
        scratch_shapes=[
            pltpu.VMEM((rows, D), BF),
            pltpu.VMEM((rows, D), BF),
            pltpu.VMEM((frames, PAD // 8, 8, D), F32),
            dma_sems(1),
            dma_sems(1),
            dma_sems(1),
            dma_sems(2),
        ]
        + line * 4
        + plane * 2,
        name="first_gather",
        compiler_params=kernel_params(collective_id),
    )(tokens, cot, tile, own0, own1, own2)


def spatial_forward(x, w_ref, vec_ref, qkv_ref, mix_ref, p_ref, r_ref):
    cols = w_ref.shape[2] // 4
    xhat, _ = norm_parts(x)
    normed = (xhat * vec_ref[10:11, :] + vec_ref[0:1, :]).astype(BF)
    mask = spatial_mask()
    branch = vec_ref[3:4, :]
    for g, (q, k, v) in enumerate(project(normed, w_ref, vec_ref, 0, cols)):
        qkv_ref[0, g, :, 0:cols] = q
        qkv_ref[0, g, :, cols : 2 * cols] = k
        qkv_ref[0, g, :, 2 * cols : 3 * cols] = v
        pairs = []
        for j in range(cols // 128):
            sl = slice(128 * j, 128 * (j + 1))
            pairs.append((q[:, sl], k[:, sl], v[:, sl]))
        mixes, exps, recips = heads_forward(pairs, mask)
        for j in range(cols // 128):
            pair = g * (cols // 128) + j
            p_ref[0, pair] = exps[j]
            r_ref[0, :, pair : pair + 1] = recips[j]
        mix = jnp.concatenate(mixes, axis=1).astype(BF)
        mix_ref[0, g] = mix
        branch = branch + dot(mix, w_ref[g, :, 3 * cols : 4 * cols], NT)
    return x + branch


def spatial_fwd_kernel(lines, *refs):
    if lines is None:
        x_ref, w_ref, vec_ref, s_ref, qkv_ref, mix_ref, p_ref, r_ref = refs
        s = spatial_forward(x_ref[0].astype(F32), w_ref, vec_ref, qkv_ref, mix_ref, p_ref, r_ref)
        s_ref[0] = s.reshape(s_ref.shape[1:])
        return
    (x_ref, w_ref, vec_ref, col1, own3), (s_b, qkv_ref, mix_ref, p_ref, r_ref, full1, col3), (
        slots, ex_send, ex_recv, ex_local), parts = take(refs, 5, 7, 4, 6)
    place = Place(lines)
    t = place.t
    i = pl.program_id(0)
    frames = pl.num_programs(0)
    groups = PAD // 16
    plane1 = PlaneGather(place, col1, full1, parts[:3])
    line3 = LineGather(place, own3, col3, parts[3:])
    last = line3.stages - 1

    @pl.when(i == 0)
    def _():
        place.greet(True)

    at_step(0, (plane1, 0), (line3, 0))
    for k in range(1, last):
        at_step(k, (line3, k))
    at_step(2, (plane1, 1))
    at_step(4, (line3, last))
    at_step(7, (plane1, 2))

    def sends(f):
        slot = slots.at[f % 2]
        return (
            pltpu.make_async_copy(
                slot.at[pl.ds(groups * t, groups)], s_b.at[frames * t + f], ex_local.at[f]
            ),
            remote(
                slot.at[pl.ds(groups * (1 - t), groups)], s_b.at[frames * t + f], (ex_send, ex_recv), f, place.core
            ),
        )

    def sent(f):
        here, there = sends(f)
        here.wait()
        there.wait_send()

    s = spatial_forward(x_ref[0].astype(F32), w_ref, vec_ref, qkv_ref, mix_ref, p_ref, r_ref)

    @pl.when(i >= 2)
    def _():
        sent(i - 2)

    slots[i % 2] = s.reshape(slots.shape[1:])
    for c in sends(i):
        c.start()

    @pl.when(i == frames - 1)
    def _():
        plane1.stage(3)
        sent(i - 1)
        sent(i)

        def body(f, _):
            sends(f)[1].wait_recv()
            return _

        lax.fori_loop(0, frames, body, 0)


def spatial_fwd(x, w, vec, links=None):
    frames, _, D = x.shape
    cols = D // 2
    pairs = D // 128
    groups = PAD // 16
    in_specs = [
        pl.BlockSpec((1, PAD, D), lambda i: (i, 0, 0)),
        whole_spec(w.shape),
        whole_spec(vec.shape),
    ]
    out_specs = [
        pl.BlockSpec((1, PAD // 8, 8, D), lambda i: (i, 0, 0, 0)),
        pl.BlockSpec((1, 2, PAD, 3 * cols), lambda i: (i, 0, 0, 0)),
        pl.BlockSpec((1, 2, PAD, cols), lambda i: (i, 0, 0, 0)),
        pl.BlockSpec((1, pairs, 2 * PAD, PAD), lambda i: (i, 0, 0, 0)),
        pl.BlockSpec((1, 2 * PAD, 128), lambda i: (i, 0, 0)),
    ]
    out_shape = [
        struct((frames, PAD // 8, 8, D), F32),
        struct((frames, 2, PAD, 3 * cols), BF),
        struct((frames, 2, PAD, cols), BF),
        struct((frames, pairs, 2 * PAD, PAD), BF),
        struct((frames, 2 * PAD, 128), F32),
    ]
    args, scratch, lines, collective_id = [x, w, vec], [], None, None
    if links is not None:
        col1, own3, lines, collective_id = links
        args += [col1, own3]
        in_specs += [any_spec()] * 2
        out_specs[0] = any_spec()
        out_shape[0] = struct((2 * frames, groups, 8, D), F32)
        out_specs += [any_spec()] * 2
        out_shape += [struct(full_shape(*col1.shape), BF), struct(col1.shape, BF)]
        scratch = [pltpu.VMEM((2, PAD // 8, 8, D), F32)] + [dma_sems(frames)] * 3
        scratch += PlaneGather.scratch() + LineGather.scratch(lines)
    return pl.pallas_call(
        functools.partial(spatial_fwd_kernel, lines),
        grid=(frames,),
        in_specs=in_specs,
        out_specs=out_specs,
        out_shape=out_shape,
        scratch_shapes=scratch,
        name="spatial_fwd",
        compiler_params=kernel_params(collective_id),
    )(*args)


def spatial_bwd_kernel(lines, *refs):
    ins, outs, (gw_ref,), rest = take(refs, 8 if lines is None else 12, 3 if lines is None else 7, 1, len(refs))
    x_ref, up_ref, qkv_ref, mix_ref, p_ref, r_ref, w_ref, vec_ref = ins[:8]
    gx_ref, gb_ref, gv_ref = outs[:3]
    cols = w_ref.shape[2] // 4
    i = pl.program_id(0)

    @pl.when(i == 0)
    def _():
        gw_ref[...] = jnp.zeros_like(gw_ref)
        gv_ref[...] = jnp.zeros_like(gv_ref)

    if lines is not None:
        out_a, g1, col2, col3 = ins[8:]
        out_ref, colsum1, sum2, sum3 = outs[3:]
        place = Place(lines)
        parts = take(rest, PlaneReduce.n_scratch, LineReduce.n_scratch, LineReduce.n_scratch)
        plane1 = PlaneReduce(place, g1, colsum1, parts[0])
        line2 = LineReduce(place, col2, sum2, parts[1])
        line3 = LineReduce(place, col3, sum3, parts[2])

        @pl.when(i == 0)
        def _():
            place.greet(True)

        for k in range(line2.stages):
            at_step(k, (line2, k), (line3, k))
        at_step(0, (plane1, 0))
        at_step(1, (plane1, 1))
        at_step(4, (plane1, 2))
        at_step(6, (plane1, 3))
        out = out_a[0].reshape(PAD, out_a.shape[3])
        out_ref[0] = out[: out_ref.shape[1]].astype(BF)

    up = up_ref[0].reshape(PAD, up_ref.shape[3])
    gx = attn_back_common(
        x_ref[0].astype(F32), up.astype(BF), up, w_ref, vec_ref, 0, 10,
        lambda g: mix_ref[0, g],
        lambda g, j, rs: tuple(
            qkv_ref[0, g, :, cols * t + 128 * j : cols * t + 128 * (j + 1)] for t in range(3)
        ),
        lambda pair, b: (p_ref[0, pair], r_ref[0, :, pair : pair + 1]),
        gw_ref, gv_ref, cols, 1,
    )
    gx_ref[0] = gx[: gx_ref.shape[1]]

    @pl.when(i == pl.num_programs(0) - 1)
    def _():
        gb_ref[...] = gw_ref[...].astype(BF)


def spatial_bwd(x, up, qkv, mix, p, r, w, vec, links=None):
    frames, _, D = x.shape
    cols = D // 2
    pairs = D // 128
    in_specs = [
        pl.BlockSpec((1, PAD, D), lambda i: (i, 0, 0)),
        pl.BlockSpec((1, PAD // 8, 8, D), lambda i: (i, 0, 0, 0)),
        pl.BlockSpec((1, 2, PAD, 3 * cols), lambda i: (i, 0, 0, 0)),
        pl.BlockSpec((1, 2, PAD, cols), lambda i: (i, 0, 0, 0)),
        pl.BlockSpec((1, pairs, 2 * PAD, PAD), lambda i: (i, 0, 0, 0)),
        pl.BlockSpec((1, 2 * PAD, 128), lambda i: (i, 0, 0)),
        whole_spec(w.shape),
        whole_spec(vec.shape),
    ]
    out_specs = [
        pl.BlockSpec((1, PATCHES, D), lambda i: (i, 0, 0)),
        whole_spec((2, D, 4 * cols)),
        whole_spec((8, D)),
    ]
    out_shape = [
        struct((frames, PATCHES, D), F32),
        struct((2, D, 4 * cols), BF),
        struct((8, D), F32),
    ]
    args = [x, up, qkv, mix, p, r, w, vec]
    scratch, lines, collective_id = [pltpu.VMEM((2, D, 4 * cols), F32)], None, None
    if links is not None:
        out_a, g1, col2, col3, lines, collective_id = links
        args += [out_a, g1, col2, col3]
        block = col2.shape[1:]
        in_specs += [
            pl.BlockSpec((1, PAD // 8, 8, D), lambda i: (i, 0, 0, 0)),
            any_spec(),
            whole_spec(col2.shape),
            whole_spec(col3.shape),
        ]
        out_specs += [
            pl.BlockSpec((1, PATCHES, D), lambda i: (i, 0, 0)),
            whole_spec(col2.shape),
            whole_spec(block),
            whole_spec(block),
        ]
        out_shape += [struct((frames, PATCHES, D), BF), struct(col2.shape, BF), struct(block, F32), struct(block, F32)]
        scratch += PlaneReduce.scratch(lines, *block, BF) + LineReduce.scratch(lines, *block, BF) * 2
    return pl.pallas_call(
        functools.partial(spatial_bwd_kernel, lines),
        grid=(frames,),
        in_specs=in_specs,
        out_specs=out_specs,
        out_shape=out_shape,
        scratch_shapes=scratch,
        name="spatial_bwd",
        compiler_params=kernel_params(collective_id),
    )(*args)


def group_rows(block, live):
    parts = []
    for b in range(block.shape[1]):
        rows = block[:, b].reshape(GROUP, block.shape[3])
        parts.append(rows if b == 0 else jnp.where(live(b), rows, 0.0))
    return jnp.concatenate(parts, axis=0)


def temporal_forward(x, w_ref, vec_ref, qkv_ref, mix_ref, p_ref, r_ref):
    cols = w_ref.shape[2] // 4
    n = x.shape[0]
    xhat, _ = norm_parts(x)
    normed = (xhat * vec_ref[11:12, :] + vec_ref[4:5, :]).astype(BF)
    mask = temporal_mask()
    branch = vec_ref[7:8, :]
    for g, (q, k, v) in enumerate(project(normed, w_ref, vec_ref, 4, cols)):
        qkv_ref[g, :, 0:cols] = q
        qkv_ref[g, :, cols : 2 * cols] = k
        qkv_ref[g, :, 2 * cols : 3 * cols] = v
        pairs = []
        for b in range(n // GROUP):
            rs = slice(GROUP * b, GROUP * (b + 1))
            for j in range(cols // 128):
                sl = slice(128 * j, 128 * (j + 1))
                pairs.append((q[rs, sl], k[rs, sl], v[rs, sl]))
        mixes, exps, recips = heads_forward(pairs, mask)
        blocks = []
        for b in range(n // GROUP):
            for j in range(cols // 128):
                pair, i = g * (cols // 128) + j, b * (cols // 128) + j
                p_ref[pair, 2 * GROUP * b : 2 * GROUP * (b + 1)] = exps[i]
                r_ref[2 * GROUP * b : 2 * GROUP * (b + 1), pair : pair + 1] = recips[i]
            blocks.append(jnp.concatenate(mixes[b * (cols // 128) : (b + 1) * (cols // 128)], axis=1))
        mix = jnp.concatenate(blocks, axis=0).astype(BF)
        mix_ref[g] = mix
        branch = branch + dot(mix, w_ref[g, :, 3 * cols : 4 * cols], NT)
    return x + branch


def temporal_fwd_kernel(lines, groups, *refs):
    ins, (s_ref, qkv_ref, mix_ref, p_ref, r_ref), rest = take(refs, 3 if lines is None else 5, 5, len(refs))
    x_ref, w_ref, vec_ref = ins[:3]
    i = pl.program_id(0)
    steps = pl.num_programs(0)
    if lines is not None:
        col2, col3 = ins[3:]
        full2, full3 = rest[:2]
        place = Place(lines)
        plane2 = PlaneGather(place, col2, full2, rest[2:5])
        plane3 = PlaneGather(place, col3, full3, rest[5:8])

        @pl.when(i == 0)
        def _():
            place.greet(False)

        at_step(0, (plane2, 0))
        at_step(2, (plane2, 1), (plane3, 0))
    x = group_rows(x_ref[...], lambda b: STEP_GROUPS * i + b < groups)
    s = temporal_forward(x, w_ref, vec_ref, qkv_ref, mix_ref, p_ref, r_ref)
    for b in range(STEP_GROUPS):
        s_ref[:, b] = s[GROUP * b : GROUP * (b + 1)].reshape(FRAMES, 8, s.shape[1])
    if lines is not None:
        at_step(6, (plane3, 1), (plane2, 2), (plane3, 2), (plane2, 3), (plane3, 3))


def temporal_specs(groups, D):
    cols = D // 2
    n = STEP_GROUPS * GROUP
    steps = -(-groups // STEP_GROUPS)
    pairs = D // 128
    stream = pl.BlockSpec((FRAMES, STEP_GROUPS, 8, D), lambda i: (0, i, 0, 0))
    specs = [
        pl.BlockSpec((2, n, 3 * cols), lambda i: (0, i, 0)),
        pl.BlockSpec((2, n, cols), lambda i: (0, i, 0)),
        pl.BlockSpec((pairs, 2 * n, GROUP), lambda i: (0, i, 0)),
        pl.BlockSpec((2 * n, 128), lambda i: (i, 0)),
    ]
    shapes = [
        struct((2, steps * n, 3 * cols), BF),
        struct((2, steps * n, cols), BF),
        struct((pairs, 2 * steps * n, GROUP), BF),
        struct((2 * steps * n, 128), F32),
    ]
    return steps, stream, specs, shapes


def temporal_fwd(x, w, vec, links=None):
    groups, D = x.shape[1], x.shape[3]
    steps, stream, kept_specs, kept_shapes = temporal_specs(groups, D)
    in_specs = [stream, whole_spec(w.shape), whole_spec(vec.shape)]
    out_specs = [stream] + kept_specs
    out_shape = [struct(x.shape, F32)] + kept_shapes
    args, scratch, lines, collective_id = [x, w, vec], [], None, None
    if links is not None:
        col2, col3, lines, collective_id = links
        args += [col2, col3]
        in_specs += [any_spec()] * 2
        out_specs += [any_spec()] * 2
        out_shape += [struct(full_shape(*col2.shape), BF)] * 2
        scratch = PlaneGather.scratch() * 2
    return pl.pallas_call(
        functools.partial(temporal_fwd_kernel, lines, groups),
        grid=(steps,),
        in_specs=in_specs,
        out_specs=out_specs,
        out_shape=out_shape,
        scratch_shapes=scratch,
        name="temporal_fwd",
        compiler_params=kernel_params(collective_id),
    )(*args)


def temporal_bwd_kernel(lines, groups, *refs):
    ins, outs, (gw_ref,), rest = take(refs, 8 if lines is None else 11, 3 if lines is None else 6, 1, len(refs))
    x_ref, up_ref, qkv_ref, mix_ref, p_ref, r_ref, w_ref, vec_ref = ins[:8]
    gx_ref, gb_ref, gv_ref = outs[:3]
    cols = w_ref.shape[2] // 4
    i = pl.program_id(0)
    steps = pl.num_programs(0)

    @pl.when(i == 0)
    def _():
        gw_ref[...] = jnp.zeros_like(gw_ref)
        gv_ref[...] = jnp.zeros_like(gv_ref)

    if lines is not None:
        out_b, g2, g3 = ins[8:]
        out_a, col2, col3 = outs[3:]
        place = Place(lines)
        t = place.t
        frames = FRAMES // 2
        (slots, ex_send, ex_recv, ex_local), parts2, parts3 = take(
            rest, 4, PlaneReduce.n_scratch, PlaneReduce.n_scratch)
        plane2 = PlaneReduce(place, g2, col2, parts2)
        plane3 = PlaneReduce(place, g3, col3, parts3)
        out_here = pltpu.make_async_copy(
            out_b.at[pl.ds(frames * t, frames)], out_a.at[:, pl.ds(groups * t, groups)], ex_local.at[steps]
        )
        out_there = remote(
            out_b.at[pl.ds(frames * (1 - t), frames)], out_a.at[:, pl.ds(groups * t, groups)],
            (ex_send, ex_recv), steps, place.core,
        )

        @pl.when(i == 0)
        def _():
            place.greet(False)

        at_step(0, (plane2, 0), (plane3, 0))

        @pl.when(i == 0)
        def _():
            out_here.start()
            out_there.start()

        at_step(1, (plane2, 1))
        at_step(3, (plane2, 2), (plane3, 1))
        at_step(5, (plane2, 3))
        at_step(6, (plane3, 2))

    live = lambda b: STEP_GROUPS * i + b < groups
    x = group_rows(x_ref[...], live)
    up = group_rows(up_ref[...], live)
    gx = attn_back_common(
        x, up.astype(BF), up, w_ref, vec_ref, 4, 11,
        lambda g: mix_ref[g],
        lambda g, j, rs: tuple(
            qkv_ref[g, rs, cols * t + 128 * j : cols * t + 128 * (j + 1)] for t in range(3)
        ),
        lambda pair, b: (
            p_ref[pair, 2 * GROUP * b : 2 * GROUP * (b + 1)],
            r_ref[2 * GROUP * b : 2 * GROUP * (b + 1), pair : pair + 1],
        ),
        gw_ref, gv_ref, cols, x.shape[0] // GROUP,
    )

    @pl.when(i == steps - 1)
    def _():
        gb_ref[...] = gw_ref[...].astype(BF)

    if lines is None:
        for b in range(STEP_GROUPS):
            gx_ref[:, b] = gx[GROUP * b : GROUP * (b + 1)].reshape(FRAMES, 8, gx.shape[1])
        return

    odd = groups % STEP_GROUPS

    def sends(s, count):
        slot = slots.at[s % 2]
        dst = gx_ref.at[:, pl.ds(groups * t + STEP_GROUPS * s, count)]
        return (
            pltpu.make_async_copy(slot.at[pl.ds(frames * t, frames), pl.ds(0, count)], dst, ex_local.at[s]),
            remote(
                slot.at[pl.ds(frames * (1 - t), frames), pl.ds(0, count)], dst, (ex_send, ex_recv), s, place.core
            ),
        )

    def sent(s, count):
        here, there = sends(s, count)
        here.wait()
        there.wait_send()

    @pl.when(i >= 2)
    def _():
        sent(i - 2, STEP_GROUPS)

    for b in range(STEP_GROUPS):
        slots[i % 2, :, b] = gx[GROUP * b : GROUP * (b + 1)].reshape(FRAMES, 8, gx.shape[1])

    @pl.when(i < steps - 1)
    def _():
        for c in sends(i, STEP_GROUPS):
            c.start()

    @pl.when(i == steps - 1)
    def _():
        tail = odd if odd else STEP_GROUPS
        for c in sends(i, tail):
            c.start()
        plane3.stage(3)
        out_here.wait()
        out_there.wait()
        sent(i - 1, STEP_GROUPS)
        sent(i, tail)

        def body(s, _):
            sends(s, STEP_GROUPS)[1].wait_recv()
            return _

        lax.fori_loop(0, steps - 1, body, 0)
        sends(i, tail)[1].wait_recv()


def temporal_bwd(x, up, qkv, mix, p, r, w, vec, links=None):
    groups, D = x.shape[1], x.shape[3]
    cols = D // 2
    steps, stream, kept_specs, _ = temporal_specs(groups, D)
    in_specs = [stream, stream] + kept_specs + [whole_spec(w.shape), whole_spec(vec.shape)]
    out_specs = [stream, whole_spec((2, D, 4 * cols)), whole_spec((8, D))]
    out_shape = [struct(x.shape, F32), struct((2, D, 4 * cols), BF), struct((8, D), F32)]
    args = [x, up, qkv, mix, p, r, w, vec]
    scratch, lines, collective_id = [pltpu.VMEM((2, D, 4 * cols), F32)], None, None
    if links is not None:
        out_b, g2, g3, lines, collective_id = links
        args += [out_b, g2, g3]
        rows, width = g2.shape[4:]
        in_specs += [any_spec()] * 3
        out_specs[0] = any_spec()
        a_shape = (FRAMES // 2, 2 * groups, 8, D)
        out_shape[0] = struct(a_shape, F32)
        col = (lines, rows, width)
        out_specs += [any_spec(), whole_spec(col), whole_spec(col)]
        out_shape += [struct(a_shape, F32), struct(col, BF), struct(col, BF)]
        scratch += [pltpu.VMEM((2, FRAMES, STEP_GROUPS, 8, D), F32)] + [dma_sems(steps + 1)] * 3
        scratch += PlaneReduce.scratch(*col, BF) * 2
    return pl.pallas_call(
        functools.partial(temporal_bwd_kernel, lines, groups),
        grid=(steps,),
        in_specs=in_specs,
        out_specs=out_specs,
        out_shape=out_shape,
        scratch_shapes=scratch,
        name="temporal_bwd",
        compiler_params=kernel_params(collective_id),
    )(*args)


def last_kernel(lines, g0, tiles, col1, sum0, sum_tile, sum1, colsum0, colsum_tile, *scratch):
    place = Place(lines)
    place.greet(True)
    width = g0.shape[5] // 2
    n, m = PlaneReduce.n_scratch, LineReduce.n_scratch
    parts = take(scratch, n, n, n, m, m, m, m)
    spans = [slice(0, width), slice(width, 2 * width)]
    planes = [PlaneReduce(place, g0, colsum0.at[h], parts[h], pl.ds(width * h, width)) for h in range(2)]
    small = PlaneReduce(place, tiles, colsum_tile, parts[2])
    line1 = LineReduce(place, col1, sum1, parts[3])
    lines0 = [LineReduce(place, colsum0.at[h], sum0.at[:, spans[h]], parts[4 + h]) for h in range(2)]
    line_small = LineReduce(place, colsum_tile, sum_tile, parts[6])
    planes[0].stage(0)
    small.stage(0)
    planes[1].stage(0)
    line1.stage(0)
    planes[0].stage(1)
    small.stage(1)
    planes[1].stage(1)
    line1.stage(1)
    planes[0].stage(2)
    small.stage(2)
    line1.stage(2)
    planes[1].stage(2)
    for k in range(3, line1.stages):
        line1.stage(k)
    planes[0].stage(3)
    small.stage(3)
    lines0[0].stage(0)
    line_small.stage(0)
    lines0[0].stage(1)
    line_small.stage(1)
    planes[1].stage(3)
    lines0[1].stage(0)
    for k in range(2, lines + 1):
        if k < lines:
            lines0[0].stage(k)
            line_small.stage(k)
        lines0[1].stage(k - 1)


def last_call(g0, tiles, col1, lines, collective_id):
    rows, width = g0.shape[4:]
    half = width // 2
    vmem = pl.BlockSpec(memory_space=pltpu.VMEM)
    return pl.pallas_call(
        functools.partial(last_kernel, lines),
        in_specs=[any_spec(), any_spec(), vmem],
        out_specs=[vmem] * 3,
        out_shape=[struct((rows, width), F32), struct(tiles.shape[4:], F32), struct((rows, width), F32)],
        scratch_shapes=[
            pltpu.VMEM((2, lines, rows, half), BF),
            pltpu.VMEM((lines,) + tiles.shape[4:], F32),
        ]
        + PlaneReduce.scratch(lines, rows, half, BF) * 2
        + PlaneReduce.scratch(lines, *tiles.shape[4:], F32)
        + LineReduce.scratch(lines, rows, width, BF)
        + LineReduce.scratch(lines, rows, half, BF) * 2
        + LineReduce.scratch(lines, *tiles.shape[4:], F32),
        name="last_reduce",
        compiler_params=kernel_params(collective_id),
    )(g0, tiles, col1)


MLP_ROWS = 416
INV_SQRT2 = 0.7071067811865476
INV_SQRT2PI = 0.3989422804014327


def mlp_kernel(x_ref, cot_ref, wi_ref, wo_ref, vec_ref, hid_ref, out_ref, up_ref, gi_ref, go_ref, gv_ref, gh_ref, ai_ref, ao_ref):
    @pl.when(pl.program_id(0) == 0)
    def _():
        ai_ref[...] = jnp.zeros_like(ai_ref)
        ao_ref[...] = jnp.zeros_like(ao_ref)
        gv_ref[...] = jnp.zeros_like(gv_ref)
        gh_ref[...] = jnp.zeros_like(gh_ref)

    width = wi_ref.shape[2]
    x = x_ref[...]
    xhat, rstd = norm_parts(x)
    gain = vec_ref[12:13, :]
    normed = (xhat * gain + vec_ref[8:9, :]).astype(BF)
    up = cot_ref[...]
    ub = up.astype(BF)
    gv_ref[3:4, :] += jnp.sum(up, axis=0, keepdims=True)
    branch = vec_ref[9:10, :]
    dn = None
    chunk = 768
    for g in range(2):
        for c in range(width // chunk):
            sl = slice(chunk * c, chunk * (c + 1))
            pre = dot(normed, wi_ref[g, :, sl], NN) + hid_ref[g : g + 1, sl]
            cdf = 0.5 + 0.5 * lax.erf(pre * INV_SQRT2)
            act = (pre * cdf).astype(BF)
            branch = branch + dot(act, wo_ref[g, :, sl], NT)
            ao_ref[g, :, sl] += dot(ub, act, TN)
            dact = dot(ub, wo_ref[g, :, sl], NN).astype(BF).astype(F32)
            slope = cdf + pre * (jnp.exp(pre * pre * -0.5) * INV_SQRT2PI)
            dpre32 = dact * slope
            dpre = dpre32.astype(BF)
            gh_ref[g : g + 1, sl] += jnp.sum(dpre.astype(F32), axis=0, keepdims=True)
            ai_ref[g, :, sl] += dot(normed, dpre, TN)
            term = dot(dpre, wi_ref[g, :, sl], NT)
            dn = term if dn is None else dn + term
    out_ref[...] = x + branch
    gv_ref[0:1, :] += jnp.sum(dn, axis=0, keepdims=True)
    gv_ref[4:5, :] += jnp.sum(dn * xhat, axis=0, keepdims=True)
    up_ref[...] = up + norm_back(dn, xhat, rstd, gain)

    @pl.when(pl.program_id(0) == pl.num_programs(0) - 1)
    def _():
        gi_ref[...] = ai_ref[...].astype(BF)
        go_ref[...] = ao_ref[...].astype(BF)


def mlp_both(x, cot, w_in, w_down, vec, hidden):
    rows, D = x.shape
    width = hidden.shape[1]
    n = MLP_ROWS
    whole = lambda *shape: pl.BlockSpec(shape, lambda i: (0,) * len(shape))
    one = pl.Buffered(1)
    return pl.pallas_call(
        mlp_kernel,
        grid=(rows // n,),
        in_specs=[
            pl.BlockSpec((n, D), lambda i: (i, 0)),
            pl.BlockSpec((n, D), lambda i: (i, 0)),
            pl.BlockSpec((2, D, width), lambda i: (0, 0, 0), pipeline_mode=one),
            pl.BlockSpec((2, D, width), lambda i: (0, 0, 0), pipeline_mode=one),
            whole(*vec.shape),
            whole(*hidden.shape),
        ],
        out_specs=[
            pl.BlockSpec((n, D), lambda i: (i, 0)),
            pl.BlockSpec((n, D), lambda i: (i, 0)),
            pl.BlockSpec((2, D, width), lambda i: (0, 0, 0)),
            pl.BlockSpec((2, D, width), lambda i: (0, 0, 0)),
            whole(8, D),
            whole(*hidden.shape),
        ],
        out_shape=[
            jax.ShapeDtypeStruct((rows, D), F32),
            jax.ShapeDtypeStruct((rows, D), F32),
            jax.ShapeDtypeStruct((2, D, width), BF),
            jax.ShapeDtypeStruct((2, D, width), BF),
            jax.ShapeDtypeStruct((8, D), F32),
            jax.ShapeDtypeStruct(hidden.shape, F32),
        ],
        scratch_shapes=[pltpu.VMEM((2, D, width), F32), pltpu.VMEM((2, D, width), F32)],
        name="mlp_both",
        compiler_params=pltpu.CompilerParams(vmem_limit_bytes=VMEM_BYTES),
    )(x, cot, w_in, w_down, vec, hidden)


def swap_to_patches(rows):
    return lax.all_to_all(rows, "tensor", split_axis=1, concat_axis=0, tiled=True)


def swap_to_frames(rows):
    return lax.all_to_all(rows, "tensor", split_axis=0, concat_axis=1, tiled=True)


def pad_frames(rows):
    D = rows.shape[1]
    return jnp.pad(rows.reshape(-1, PATCHES, D), ((0, 0), (0, PAD - PATCHES), (0, 0)))


def shards(tokens, cotangent, attn_qkv, attn_out, mlp_in, mlp_out, norm_gains, biases, hidden_bias):
    D = tokens.shape[1]
    depth = mlp_in.shape[1]
    cols = attn_qkv.shape[4]
    units = mlp_in.shape[2]
    frames = tokens.shape[0] // PATCHES
    everyone = ("dp", "tensor")
    chips = D // depth
    devices = 2 * chips
    share = D // devices
    owns = [
        jnp.concatenate([attn_qkv[0, s].reshape(depth, 3 * cols), attn_out[0, s].T], axis=1)
        for s in range(2)
    ]
    owns += [mlp_in[0], mlp_out[0].T]
    small = jnp.concatenate(
        [biases[0].reshape(-1), norm_gains[0].reshape(-1), hidden_bias[0].reshape(-1)]
    )
    count = small.shape[0]

    def vectors(small):
        vec = small[:, : 13 * share].reshape(devices, 13, share).transpose(1, 0, 2).reshape(13, D)
        return vec, small[:, 13 * share :].reshape(2, units)

    def spread(gv_s, gv_t, gv_m, g_hidden):
        vec_grad = jnp.concatenate(
            [gv_s[0:4], gv_t[0:4], gv_m[0:1], gv_m[3:4], gv_s[4:5], gv_t[4:5], gv_m[4:5]]
        )
        vec_grad = vec_grad.reshape(13, devices, share).transpose(1, 0, 2).reshape(devices, 13 * share)
        return jnp.concatenate([vec_grad, g_hidden.reshape(devices, -1)], axis=1)

    flat = lambda w: w.reshape(2, D, w.shape[-1])
    rows_of = lambda v: v.reshape(-1, D)
    if depth % 16 == 0 and chips % 4 == 0:
        lines = chips // 4
        cut = lambda g: g.reshape(full_shape(lines, depth, g.shape[2]))
        tile = jnp.pad(small, (0, 1024 - count)).reshape(8, 128)
        x, cot, full_tile, full0, _, _, col1, col2 = first_call(
            tokens, cotangent, tile, owns[0], owns[1], owns[2], lines, 1
        )
        vec, hidden = vectors(
            full_tile.reshape(2, chips, 1024).transpose(1, 0, 2).reshape(devices, 1024)[:, :count]
        )
        w0 = flat(full0)
        x1, *kept_s, full1, col3 = spatial_fwd(x, w0, vec, (col1, owns[3], lines, 2))
        w1 = flat(full1)
        x2, *kept_t, full2, full3 = temporal_fwd(x1, w1, vec, (col2, col3, lines, 3))
        out_b, up2, g_in, g_down, gv_m, g_hidden = mlp_both(
            rows_of(x2), rows_of(cot), flat(full2), flat(full3), vec, hidden
        )
        up1, g_t, gv_t, out_a, col2, col3 = temporal_bwd(
            x1, up2.reshape(x1.shape), *kept_t, w1, vec,
            (out_b.reshape(x1.shape), cut(g_in), cut(g_down), lines, 4),
        )
        up0, g_s, gv_s, output, col1, g_in, g_down = spatial_bwd(
            x, up1, *kept_s, w0, vec, (out_a, cut(g_t), col2, col3, lines, 5)
        )
        tiles = jnp.pad(spread(gv_s, gv_t, gv_m, g_hidden), ((0, 0), (0, 1024 - count)))
        tiles = tiles.reshape(chips, 2, 1024).transpose(1, 0, 2).reshape(full_shape(lines, 8, 128))
        g_s, small_grad, g_t = last_call(cut(g_s), tiles, col1, lines, 6)
        small_grad = small_grad.reshape(-1)[:count]
    else:
        small = lax.all_gather(small.reshape(1, -1), everyone, axis=0, tiled=True)
        vec, hidden = vectors(small)
        weights = [flat(lax.all_gather(w, ("tensor", "dp"), axis=0, tiled=True).reshape(2, D, -1)) for w in owns]
        x = pad_frames(tokens)
        fold = lambda v: v.reshape(frames, PAD // 8, 8, D)
        x1, *kept_s = spatial_fwd(x, weights[0], vec)
        x1 = swap_to_patches(x1)
        x2, *kept_t = temporal_fwd(x1, weights[1], vec)
        cot = swap_to_patches(fold(pad_frames(cotangent).astype(F32)))
        out_b, up2, g_in, g_down, gv_m, g_hidden = mlp_both(
            rows_of(x2), rows_of(cot), weights[2], weights[3], vec, hidden
        )
        output = swap_to_frames(out_b.reshape(x1.shape)).reshape(frames, PAD, D)[:, :PATCHES].astype(BF)
        up1, g_t, gv_t = temporal_bwd(x1, up2.reshape(x1.shape), *kept_t, weights[1], vec)
        up0, g_s, gv_s = spatial_bwd(x, swap_to_frames(up1), *kept_s, weights[0], vec)
        g_s, g_t, g_in, g_down = [
            lax.psum_scatter(
                g.reshape(2 * D, g.shape[2]), ("tensor", "dp"), scatter_dimension=0, tiled=True
            ).astype(F32)
            for g in (g_s, g_t, g_in, g_down)
        ]
        small_grad = lax.psum_scatter(
            spread(gv_s, gv_t, gv_m, g_hidden), everyone, scatter_dimension=0, tiled=True
        )[0]
    grad_qkv = jnp.stack([g[:, : 3 * cols].reshape(depth, 3, cols) for g in (g_s, g_t)])[None]
    grad_out = jnp.stack([g[:, 3 * cols :].T for g in (g_s, g_t)])[None]
    grad_biases = small_grad[: 10 * share].reshape(1, 10, share)
    grad_gains = small_grad[10 * share : 13 * share].reshape(1, 3, share)
    grad_hidden = small_grad[13 * share :].reshape(1, -1)
    return (
        rows_of(output),
        rows_of(up0),
        grad_qkv,
        grad_out,
        g_in[None],
        g_down.T[None],
        grad_gains,
        grad_biases,
        grad_hidden,
    )


def solution(mesh):
    placed = (
        P(("dp", "tensor"), None),
        P(("dp", "tensor"), None),
        P(None, None, "dp", None, "tensor"),
        P(None, None, "tensor", "dp"),
        P(None, "dp", "tensor"),
        P(None, "tensor", "dp"),
        P(None, None, ("dp", "tensor")),
        P(None, None, ("dp", "tensor")),
        P(None, ("dp", "tensor")),
    )
    return jax.shard_map(
        shards, mesh=mesh, in_specs=placed, out_specs=placed, check_vma=False
    )
```

time: 828 us -> 470 us (0.57)
  waiting for transfers between devices: 362 us -> 0 us
  Pallas kernels: 279 us -> 438 us
  blocking collectives: 108 us -> 0 us
  local copies, waits for them, and re-layouts: 52.1 us -> 26.6 us
  between operations: 14.4 us -> 1.09 us
    reduce_scatter x4 -> x0, waiting for transfers between devices: 296 us -> none  [scatter(): lax.psum_scatter(grad.reshape(2 * D, grad.shape[2]), ('tensor', 'dp'), sc...]
    pallas_call x4 -> x6, Pallas kernels: 198 us -> 356 us  [the longest x1 86.8 us: temporal_bwd(): pl.pallas_call(functools.partial(temporal_bwd_kernel, lines, groups), gri...]
    unnamed x2 -> x0, blocking collectives: 86.1 us -> none
    all_gather x1 -> x0, waiting for transfers between devices: 64.7 us -> none  [shards(): lax.all_gather(own, ('tensor', 'dp'), axis=0, tiled=True)]
    all_to_all x3 -> x0, blocking collectives: 21.8 us -> none  [the longest x2 14 us: to_frames(): lax.all_to_all(blocks.reshape(2 * frames, 1, PAD // 2, D), 'tensor', spli...]
    reshape x13 -> x14, local copies, waits for them, and re-layouts: 23.1 us -> 14.3 us  [the longest x2 9.31 us: shards(): rows_of = lambda v: v.reshape(-1, D)]
  transfers between devices with their start and end apart: 6 -> 0, of which waited for: 4 -> 0; matrix products, arithmetic and copies ran while one was open for 5% -> 0% of each run, Pallas kernels for 7% -> 0%
where the time goes in v3:
time: 470 us
  Pallas kernels  438 us (93%)
  local copies, waits for them, and re-layouts  26.6 us (6%)
    pallas_call x1, Pallas kernels, temporal_bwd(): pl.pallas_call(functools.partial(temporal_bwd_kernel, lines, groups), gri...  86.8 us
    pallas_call x1, Pallas kernels, mlp_both(): pl.pallas_call(mlp_kernel, grid=(rows // n,), in_specs=[pl.BlockSpec((n,...  81.7 us
    pallas_call x1, Pallas kernels, temporal_fwd(): pl.pallas_call(functools.partial(temporal_fwd_kernel, lines, groups), gri...  61.9 us
    pallas_call x1, Pallas kernels, first_call(): pl.pallas_call(functools.partial(first_body, lines), in_specs=[any_spec()...  60.5 us
    pallas_call x1, Pallas kernels, spatial_bwd(): pl.pallas_call(functools.partial(spatial_bwd_kernel, lines), grid=(frames...  59.7 us
    pallas_call x1, Pallas kernels, spatial_fwd(): pl.pallas_call(functools.partial(spatial_fwd_kernel, lines), grid=(frames...  44 us
    pallas_call x1, Pallas kernels, last_call(): pl.pallas_call(functools.partial(last_kernel, lines), in_specs=[any_spec(...  43 us

profile of v3, /device:TPU:0, one launch (start us, length us, event | category | flops | bytes accessed | tf_op | source)
XLA Modules:
  0.0 469.6 jit_solution(16051533763289011786)
XLA Ops:
  0.6 0.7 reduce.1
  1.4 0.7 reduce
  2.2 1.3 fusion.tile
  3.5 0.8 slice_bitcast_fusion.2
  4.3 1.0 fusion.1
  5.5 0.7 pad_maximum_fusion
  6.2 60.5 %first_gather.1 = (bf16[8,208,768]{2,1,0:T(8,128)(2,1)}, f32[16,13,8,768]{3,2,1,0:T(8,128)}, f32[2,4,2,2,8,128]{5,4,3,2,1,0:T(8,128)}, bf16[2,4,2,2,48,1536]{5,4...) custom-call(bf16[1568,768]{1,0:T(8,128)(2,1)} %tok.1, ...), custom_call_target="tpu_custom_call" | custom-call | tf_op jit(solution)/shard_map/first_gather/pallas_call | solution.py:605
  66.7 0.9 reshape.107
  68.0 0.7 reshape.116.hid_ref
  68.9 0.8 reshape.110.refs_2_.vec_ref.refs_7_
  69.7 44.0 %spatial_fwd.1 = (f32[16,13,8,768]{3,2,1,0:T(8,128)}, bf16[8,2,208,1152]{3,2,1,0:T(8,128)(2,1)}, bf16[8,2,208,384]{3,2,1,0:T(8,128)(2,1)}, bf16[8,6,416,208]{3,2...) custom-call(bf16[8,208,768]{2,1,0:T(8,128)(2,1)} %get-tuple-element., ...), custom_call_target="tpu_custom_call" | custom-call | tf_op jit(solution)/shard_map/spatial_fwd/pallas_call | solution.py:762
  113.7 61.9 %temporal_fwd.1 = (f32[16,13,8,768]{3,2,1,0:T(8,128)}, bf16[2,1792,1152]{2,1,0:T(8,128)(2,1)}, bf16[2,1792,384]{2,1,0:T(8,128)(2,1)}, bf16[6,3584,128]{2,1,0:T(8...) custom-call(f32[16,13,8,768]{3,2,1,0:T(8,128)} %get-tuple-element.55, ...), custom_call_target="tpu_custom_call" | custom-call | tf_op jit(solution)/shard_map/temporal_fwd/pallas_call | solution.py:981
  175.6 81.7 %mlp_both.1 = (f32[1664,768]{1,0:T(8,128)}, f32[1664,768]{1,0:T(8,128)}, bf16[2,768,1536]{2,1,0:T(8,128)(2,1)}, bf16[2,768,1536]{2,1,0:T(8,128)(2,1)}, f32[8,768]{1,0:T(8,128)}, /*index=5*/f32[2,1536]{1,0:T(2,128)}) custom-call(f32[1664,768]{1,0:T(8,128)} %bitcast.72, f32[1664,768]{1,0:T(8,128)} %bitcast.71, bf16[2,768,1536]{2,1,0:T(8,128)(2,1)} %bitcast.77, ...), custom_call_target="tpu_custom_call" | custom-call | tf_op jit(solution)/shard_map/mlp_both/pallas_call | solution.py:1268
  257.3 86.8 %temporal_bwd.1 = (f32[8,26,8,768]{3,2,1,0:T(8,128)}, bf16[2,768,1536]{2,1,0:T(8,128)(2,1)}, f32[8,768]{1,0:T(8,128)}, f32[8,26,8,768]{3,2,1,0:T(8,128)}, bf16[4...) custom-call(f32[16,13,8,768]{3,2,1,0:T(8,128)} %get-tuple-element.55.refs_0_, f32[16,13,8,768]{3,2,1,0:T(8,128)} %bitcast.70, ...), custom_call_target="tpu_custom_call" | custom-call | tf_op jit(solution)/shard_map/temporal_bwd/pallas_call | solution.py:1135
  344.1 59.7 %spatial_bwd.1 = (f32[8,196,768]{2,1,0:T(8,128)}, bf16[2,768,1536]{2,1,0:T(8,128)(2,1)}, f32[8,768]{1,0:T(8,128)}, bf16[8,196,768]{2,1,0:T(8,128)(2,1)}, bf16[4,...) custom-call(bf16[8,208,768]{2,1,0:T(8,128)(2,1)} %get-tuple-element.51.refs_0_, ...), custom_call_target="tpu_custom_call" | custom-call | tf_op jit(solution)/shard_map/spatial_bwd/pallas_call | solution.py:869
  403.8 4.1 reshape.122
  408.0 0.9 fusion.2
  409.6 0.7 copy.56.tiles
  410.3 43.0 %last_reduce.1 = (f32[48,1536]{1,0:T(8,128)}, f32[8,128]{1,0:T(8,128)}, f32[48,1536]{1,0:T(8,128)}) custom-call(bf16[2,4,2,2,48,1536]{5,4,3,2,1,0:T(8,128)(2,1)} %bitcast.76, f32[2,4,2,2,8,128]{5,4,3,2,1,0:T(8,128)} %copy.56.tiles, bf16[4,48,1536]{2,1,0:T(8,128)(2,1)} %get-tuple-element.87.col1), custom_call_target="tpu_custom_call" | custom-call | tf_op jit(solution)/shard_map/last_reduce/pallas_call | solution.py:1192
  453.3 1.3 slice_bitcast_fusion.4
  454.5 0.8 slice.84
  455.3 0.7 slice.85
  456.6 0.7 reshape.132
  457.3 0.9 slice_bitcast_fusion.1
  458.2 0.9 slice.80
  459.2 0.9 slice_bitcast_fusion
  460.1 0.9 slice.81
  461.1 0.7 maximum_bitcast_fusion.1
  462.0 0.8 copy.54
  462.8 5.2 %reshape.123 = f32[1568,768]{1,0:T(8,128)} reshape(f32[8,196,768]{2,1,0:T(8,128)} %get-tuple-element.81) | data formatting | bytes 9633792 | tf_op jit(solution)/shard_map/reshape | solution.py:1346
  468.0 0.7 copy.63
  468.7 0.7 copy.64
  (38 shorter events, 2.6 us)
Async XLA Ops:
  403.8 4.1 copy-start.4
  403.8 4.1 copy-start.3
  403.8 5.1 %copy-start.2 = (f32[2,1536]{1,0:T(2,128)S(1)}, f32[2,1536]{1,0:T(2,128)}, u32[]{:S(2)}) copy-start(f32[2,1536]{1,0:T(2,128)} %get-tuple-element.86) | copy-start | bytes 36868
  462.8 5.2 %copy-start.1 = (f32[48,1536]{1,0:T(8,128)S(1)}, f32[48,1536]{1,0:T(8,128)}, u32[]{:S(2)}) copy-start(f32[48,1536]{1,0:T(8,128)} %get-tuple-element.90) | copy-start | bytes 884740
  462.8 5.9 %copy-start = (f32[48,1536]{1,0:T(8,128)S(1)}, f32[48,1536]{1,0:T(8,128)}, u32[]{:S(2)}) copy-start(f32[48,1536]{1,0:T(8,128)} %get-tuple-element.91) | copy-start | bytes 884740

commit v4 on v3

v4 whole, which is shorter than its diff:
```python
import functools
import jax
import jax.numpy as jnp
from jax import lax
from jax.experimental import pallas as pl
from jax.experimental.pallas import tpu as pltpu
from jax.sharding import PartitionSpec as P

HEAD = 64
FRAMES = 16
PATCHES = 196
PAD = 208
EPSILON = 1e-06
BF = jnp.bfloat16
F32 = jnp.float32
NN = (((1,), (0,)), ((), ()))
NT = (((1,), (1,)), ((), ()))
TN = (((0,), (0,)), ((), ()))
VMEM_BYTES = 60 * 1024 * 1024


def dot(a, b, dims):
    return lax.dot_general(a, b, dims, preferred_element_type=F32)


def norm_parts(x):
    mean = jnp.mean(x, axis=-1, keepdims=True)
    centred = x - mean
    var = jnp.mean(centred * centred, axis=-1, keepdims=True)
    rstd = lax.rsqrt(var + EPSILON)
    return centred * rstd, rstd


def norm_back(grad_normed, xhat, rstd, gain):
    scaled = grad_normed * gain
    first = jnp.mean(scaled, axis=-1, keepdims=True)
    second = jnp.mean(scaled * xhat, axis=-1, keepdims=True)
    return rstd * (scaled - first - xhat * second)


def split_halves(pair):
    lane = lax.broadcasted_iota(jnp.int32, pair.shape, 1)
    zero = jnp.zeros_like(pair)
    return jnp.where(lane < HEAD, pair, zero), jnp.where(lane < HEAD, zero, pair)


def project(normed, w_ref, vec_ref, row_base, cols):
    parts = []
    for g in range(2):
        qkv = dot(normed, w_ref[g], NN)
        bq = vec_ref[row_base + 1 : row_base + 2, g * cols : (g + 1) * cols]
        bv = vec_ref[row_base + 2 : row_base + 3, g * cols : (g + 1) * cols]
        q = (qkv[:, :cols] + bq).astype(BF) * BF(0.125)
        k = qkv[:, cols : 2 * cols].astype(BF)
        v = (qkv[:, 2 * cols :] + bv).astype(BF)
        parts.append((q, k, v))
    return parts


def stack_halves(pair):
    return jnp.concatenate(split_halves(pair), axis=0)


def merge_halves(both):
    rows = both.shape[0] // 2
    lane = lax.broadcasted_iota(jnp.int32, (rows, both.shape[1]), 1)
    return jnp.where(lane < HEAD, both[:rows], both[rows:])


def heads_forward(pairs, mask):
    scores = [dot(stack_halves(q), k, NT) for q, k, _ in pairs]
    exps, recips = [], []
    for s in scores:
        s = jnp.where(mask, s, -1e30)
        e = jnp.exp(s - jnp.max(s, axis=-1, keepdims=True))
        recips.append(1.0 / jnp.sum(e, axis=-1, keepdims=True))
        exps.append(e.astype(BF))
    outs = [merge_halves(dot(e, v, NN) * r) for e, r, (_, _, v) in zip(exps, recips, pairs)]
    return outs, exps, recips


def heads_backward(pairs):
    dors, deltas = [], []
    for q, k, v, o, do, e, r in pairs:
        both = stack_halves(do.astype(F32)) * r
        deltas.append(jnp.sum(both * jnp.concatenate([o, o], axis=0).astype(F32), axis=-1, keepdims=True))
        dors.append(both.astype(BF))
    dps = [dot(dor, p[2], NT) for dor, p in zip(dors, pairs)]
    dss = [(p[5].astype(F32) * (dp - delta)).astype(BF) for dp, delta, p in zip(dps, deltas, pairs)]
    dq = [(merge_halves(dot(ds, p[1], NN)) * 0.125).astype(BF) for ds, p in zip(dss, pairs)]
    dk = [dot(ds, stack_halves(p[0]), TN).astype(BF) for ds, p in zip(dss, pairs)]
    dv = [dot(p[5], dor, TN).astype(BF) for dor, p in zip(dors, pairs)]
    return dq, dk, dv


def spatial_mask():
    return lax.broadcasted_iota(jnp.int32, (2 * PAD, PAD), 1) < PATCHES


def attn_back_common(x, ub, up, w_ref, wo_ref, vec_ref, row_base, gain_row, mix_of, qkv_of, exps_of, gw_ref, go_ref, gv_ref, cols, blocks):
    xhat, rstd = norm_parts(x)
    gain = vec_ref[gain_row : gain_row + 1, :]
    normed = (xhat * gain + vec_ref[row_base : row_base + 1, :]).astype(BF)
    dn = None
    gv_ref[3:4, :] += jnp.sum(up, axis=0, keepdims=True)
    rows = x.shape[0]
    step = rows // blocks
    for g in range(2):
        dmix = dot(ub, wo_ref[g], NN).astype(BF)
        mix = mix_of(g)
        go_ref[g] += dot(ub, mix, TN)
        parts = [[], [], []]
        for b in range(blocks):
            rs = slice(step * b, step * (b + 1))
            pairs = []
            for j in range(cols // 128):
                sl = slice(128 * j, 128 * (j + 1))
                q, k, v = qkv_of(g, j, rs)
                e, r = exps_of(g * (cols // 128) + j, b)
                pairs.append((q, k, v, mix[rs, sl], dmix[rs, sl], e, r))
            for part, got in zip(parts, heads_backward(pairs)):
                part.append(jnp.concatenate(got, axis=1))
        dq, dk, dv = [jnp.concatenate(part, axis=0) for part in parts]
        span = slice(g * cols, (g + 1) * cols)
        gv_ref[1:2, span] += jnp.sum(dq.astype(F32), axis=0, keepdims=True)
        gv_ref[2:3, span] += jnp.sum(dv.astype(F32), axis=0, keepdims=True)
        dqkv = jnp.concatenate([dq, dk, dv], axis=1)
        gw_ref[g] += dot(normed, dqkv, TN)
        term = dot(dqkv, w_ref[g], NT)
        dn = term if dn is None else dn + term
    gv_ref[0:1, :] += jnp.sum(dn, axis=0, keepdims=True)
    gv_ref[4:5, :] += jnp.sum(dn * xhat, axis=0, keepdims=True)
    return up + norm_back(dn, xhat, rstd, gain)


MESH = pl.DeviceIdType.MESH


class Place:
    def __init__(self, lines):
        self.lines = lines
        self.dp = lax.axis_index("dp")
        self.t = lax.axis_index("tensor")
        self.z = self.dp // 4
        self.y = (self.dp // 2) % 2
        self.x = self.dp % 2
        self.a = self.y * (1 - self.t) + self.x * self.t
        self.b = self.x * (1 - self.t) + self.y * self.t
        toward_y = self.dp + 2 - 4 * self.y
        toward_x = self.dp + 1 - 2 * self.x
        self.first = (toward_y * (1 - self.t) + toward_x * self.t, self.t)
        self.second = (toward_x * (1 - self.t) + toward_y * self.t, self.t)
        self.core = (self.dp, 1 - self.t)
        self.up = (self.dp + 4, self.t)
        self.down = (self.dp - 4, self.t)

    def yx(self, a, b, t):
        return a * (1 - t) + b * t, b * (1 - t) + a * t

    def greet(self):
        bar = pltpu.get_barrier_semaphore()
        for who in (self.core, self.first, self.second):
            pl.semaphore_signal(bar, inc=1, device_id=who, device_id_type=MESH)

        @pl.when(self.z > 0)
        def _():
            pl.semaphore_signal(bar, inc=1, device_id=self.down, device_id_type=MESH)

        @pl.when(self.z < self.lines - 1)
        def _():
            pl.semaphore_signal(bar, inc=1, device_id=self.up, device_id_type=MESH)

        inner = (self.z > 0).astype(jnp.int32) + (self.z < self.lines - 1).astype(jnp.int32)
        pl.semaphore_wait(bar, 3 + inner)


def remote(src, dst, sems, i, who):
    return pltpu.make_async_remote_copy(
        src_ref=src, dst_ref=dst, send_sem=sems[0].at[i], recv_sem=sems[1].at[i],
        device_id=who, device_id_type=MESH,
    )


def dma_sems(n):
    return pltpu.SemaphoreType.DMA((n,))


def begin(c):
    c.start()


def arrived(c):
    c.wait_recv()


def left(c):
    c.wait_send()


def whole(c):
    c.wait()


class LineGather:
    @staticmethod
    def scratch(lines):
        n = 2 * (lines - 1) + 1
        return [dma_sems(n), dma_sems(n), dma_sems(1)]

    n_scratch = 3

    def __init__(self, place, own, col, scratch, to_core=None, kept=False):
        self.p, self.own, self.col, self.to_core, self.kept = place, own, col, to_core, kept
        self.sems, self.local = scratch[:2], scratch[2]
        self.hops = place.lines - 1
        self.stages = self.hops + (1 if to_core is None else 2)

    def keep(self):
        return pltpu.make_async_copy(self.own, self.col.at[self.p.z], self.local.at[0])

    def _up(self, k):
        block = self.col.at[self.p.z - k]
        return remote(self.own if k == 0 else block, block, self.sems, k, self.p.up)

    def _down(self, k):
        block = self.col.at[self.p.z + k]
        return remote(self.own if k == 0 else block, block, self.sems, self.hops + k, self.p.down)

    def _sent(self, k, act):
        p = self.p

        @pl.when((p.z < self.hops) & (p.z >= k))
        def _():
            act(self._up(k))

        @pl.when((p.z > 0) & (p.z + k <= self.hops))
        def _():
            act(self._down(k))

    def _take(self, k):
        p = self.p

        @pl.when(p.z >= k + 1)
        def _():
            arrived(self._up(k))

        @pl.when(p.z + k + 1 <= self.hops)
        def _():
            arrived(self._down(k))

    def _core(self):
        return remote(self.to_core, self.to_core, self.sems, 2 * self.hops, self.p.core)

    def stage(self, k):
        if k == 0:
            if not self.kept:
                self.keep().start()
            self._sent(0, begin)
        elif k <= self.hops:
            self._take(k - 1)
            if k < self.hops:
                self._sent(k, begin)
                return
            if not self.kept:
                self.keep().wait()
            if self.to_core is not None:
                self._core().start()
            for i in range(self.hops):
                self._sent(i, left)
        else:
            self._core().wait()


class PlaneGather:
    @staticmethod
    def scratch():
        return [dma_sems(5), dma_sems(5), dma_sems(1)]

    n_scratch = 3
    stages = 4

    def __init__(self, place, block, spot, scratch, cores=True, kept=False):
        self.p, self.block, self.spot, self.cores, self.kept = place, block, spot, cores, kept
        self.sems, self.local = scratch[:2], scratch[2]

    def _keep(self):
        return pltpu.make_async_copy(self.block, self.spot(self.p.y, self.p.x), self.local.at[0])

    def _own(self, i, who):
        return remote(self.block, self.spot(self.p.y, self.p.x), self.sems, i, who)

    def _plane(self, i, who, b, act):
        p = self.p
        every = slice(None)

        @pl.when(p.t == 0)
        def _():
            part = self.spot(every, b)
            act(remote(part, part, self.sems, i, who))

        @pl.when(p.t == 1)
        def _():
            part = self.spot(b, every)
            act(remote(part, part, self.sems, i, who))

    def _pass_on(self):
        p = self.p
        part = self.spot(*p.yx(1 - p.a, p.b, p.t))
        return remote(part, part, self.sems, 3, p.core)

    def stage(self, k):
        p = self.p
        if k == 0:
            if not self.kept:
                self._keep().start()
            self._own(0, p.first).start()
            if self.cores:
                self._own(2, p.core).start()
        elif k == 1:
            if not self.kept:
                self._keep().wait()
            arrived(self._own(0, p.first))
            self._plane(1, p.second, p.b, begin)
            if self.cores:
                self._pass_on().start()
        elif k == 2:
            self._plane(1, p.second, p.b, arrived)
            if self.cores:
                self._plane(4, p.core, 1 - p.b, begin)
        else:
            if self.cores:
                self._own(2, p.core).wait()
                self._pass_on().wait()
                self._plane(4, p.core, 1 - p.b, whole)
            left(self._own(0, p.first))
            self._plane(1, p.second, p.b, left)


class When:
    def __init__(self, valid, make):
        self.valid, self.make = valid, make

    def stage(self, k):
        @pl.when(self.valid)
        def _():
            self.make().stage(k)


def add_blocks(u, v, dtype):
    return (u.astype(F32) + v.astype(F32)).astype(dtype)


class CoreSum:
    @staticmethod
    def scratch(n, block, dtype):
        return [
            pltpu.VMEM((n, 2, 2) + block, dtype),
            pltpu.VMEM((n, 2, 2) + block, dtype),
            dma_sems(4),
            dma_sems(4),
            dma_sems(4),
        ]

    n_scratch = 5

    def __init__(self, place, g_ref, scratch, span=None):
        self.p, self.g, self.span = place, g_ref, span
        self.own, self.land, self.sems, self.local = scratch[0], scratch[1], scratch[2:4], scratch[4]

    def _part(self, t, y, x):
        if self.span is None:
            return self.g.at[t, :, y, x]
        return self.g.at[t, :, y, x, :, self.span]

    def _copies(self):
        p, copies = self.p, []
        for a in range(2):
            for b in range(2):
                y, x = p.yx(a, b, 1 - p.t)
                copies.append(
                    remote(self._part(1 - p.t, y, x), self.land.at[:, a, b], self.sems, 2 * a + b, p.core)
                )
                y, x = p.yx(a, b, p.t)
                copies.append(
                    pltpu.make_async_copy(self._part(p.t, y, x), self.own.at[:, a, b], self.local.at[2 * a + b])
                )
        return copies

    def start(self):
        for c in self._copies():
            c.start()

    def wait(self):
        for c in self._copies():
            c.wait()

    def add(self, a):
        def body(i, _):
            self.own[i, a] = add_blocks(self.own[i, a], self.land[i, a], self.own.dtype)
            return _

        lax.fori_loop(0, self.own.shape[0], body, 0)


class PlaneSum:
    @staticmethod
    def scratch(n, block, dtype):
        return [pltpu.VMEM((n, 2) + block, dtype), pltpu.VMEM((n,) + block, dtype), dma_sems(2), dma_sems(2)]

    n_scratch = 4
    stages = 3

    def __init__(self, place, own, col, scratch):
        self.p, self.own, self.col = place, own, col
        self.land1, self.land2, self.sems = scratch[0], scratch[1], scratch[2:4]
        self.n = self.land2.shape[0]

    def _first(self):
        return remote(self.own.at[:, 1 - self.p.a], self.land1, self.sems, 0, self.p.first)

    def _second(self):
        return remote(self.land1.at[:, 1 - self.p.b], self.land2, self.sems, 1, self.p.second)

    def stage(self, k):
        p = self.p
        if k == 0:
            self._first().start()
        elif k == 1:
            self._first().wait()

            def away(i, _):
                self.land1[i, 1 - p.b] = add_blocks(
                    self.own[i, p.a, 1 - p.b], self.land1[i, 1 - p.b], self.land1.dtype
                )
                return _

            lax.fori_loop(0, self.n, away, 0)
            self._second().start()
        else:
            self._second().wait()

            def body(i, _):
                total = self.own[i, p.a, p.b].astype(F32) + self.land1[i, p.b].astype(F32)
                self.col[i] = (total + self.land2[i].astype(F32)).astype(self.col.dtype)
                return _

            lax.fori_loop(0, self.n, body, 0)


class LineSum:
    @staticmethod
    def scratch(lines, block, dtype):
        return [
            pltpu.VMEM((lines,) + block, dtype),
            pltpu.VMEM((lines,) + block, dtype),
            dma_sems(2 * (lines - 1)),
            dma_sems(2 * (lines - 1)),
        ]

    n_scratch = 4

    def __init__(self, place, col, out, scratch):
        self.p, self.col, self.out = place, col, out
        self.from_down, self.from_up = scratch[:2]
        self.sems = scratch[2:4]
        self.stages = place.lines

    def _up(self, d):
        block = self.from_down.at[d]
        return remote(block, block, self.sems, d - 1, self.p.up)

    def _down(self, d):
        block = self.from_up.at[d]
        return remote(block, block, self.sems, self.p.lines - 1 + d, self.p.down)

    def stage(self, step):
        n = self.p.lines
        for z in range(n):
            up = [d for d in range(z + 1, n) if z + (n - 1 - d) == step]
            down = [d for d in range(z) if (n - 1 - z) + d == step]
            if step < n - 1 and not up and not down:
                continue
            pl.when(self.p.z == z)(functools.partial(self._at, z, up, down, step == n - 1))

    def _at(self, z, up, down, last):
        n, dtype = self.p.lines, self.from_down.dtype
        for d in up:
            if z > 0:
                arrived(self._up(d))
                self.from_down[d] = add_blocks(self.from_down[d], self.col[d], dtype)
            else:
                self.from_down[d] = self.col[d]
            self._up(d).start()
        for d in down:
            if z < n - 1:
                arrived(self._down(d))
                self.from_up[d] = add_blocks(self.from_up[d], self.col[d], dtype)
            else:
                self.from_up[d] = self.col[d]
            self._down(d).start()
        if not last:
            return
        total = self.col[z].astype(F32)
        if z > 0:
            arrived(self._up(z))
            total = total + self.from_down[z].astype(F32)
        if z < n - 1:
            arrived(self._down(z))
            total = total + self.from_up[z].astype(F32)
        self.out[...] = total.astype(self.out.dtype)
        for d in range(z + 1, n):
            left(self._up(d))
        for d in range(z):
            left(self._down(d))


class PlaneReduce:
    @staticmethod
    def scratch(n, block, dtype):
        return CoreSum.scratch(n, block, dtype) + PlaneSum.scratch(n, block, dtype)

    n_scratch = 9

    def __init__(self, place, g_ref, col, scratch, span=None):
        self.p = place
        self.cores = CoreSum(place, g_ref, scratch[:5], span)
        self.plane = PlaneSum(place, self.cores.own, col, scratch[5:])

    def stage(self, k):
        if k == 0:
            self.cores.start()
        elif k == 1:
            self.cores.wait()
            self.cores.add(1 - self.p.a)
            self.plane.stage(0)
            self.cores.add(self.p.a)
        else:
            self.plane.stage(k - 1)


class LineReduce:
    @staticmethod
    def scratch(n, block, dtype):
        return CoreSum.scratch(n, block, dtype) + LineSum.scratch(n, (2, 2) + block, dtype)

    n_scratch = 9

    def __init__(self, place, g_ref, out, scratch):
        self.cores = CoreSum(place, g_ref, scratch[:5])
        self.line = LineSum(place, self.cores.own, out, scratch[5:])

    def stage(self, k):
        if k == 0:
            self.cores.start()
            return
        if k == 1:
            self.cores.wait()
            self.cores.add(0)
            self.cores.add(1)
        self.line.stage(k - 1)


def at_step(step, *stages):
    @pl.when(pl.program_id(0) == step)
    def _():
        for job, k in stages:
            job.stage(k)


def take(refs, *counts):
    out, i = [], 0
    for c in counts:
        out.append(refs[i : i + c])
        i += c
    return out


GROUP = 8 * FRAMES
STEP_GROUPS = 2


def temporal_mask():
    a = lax.broadcasted_iota(jnp.int32, (2 * GROUP, GROUP), 0)
    b = lax.broadcasted_iota(jnp.int32, (2 * GROUP, GROUP), 1)
    return (a % 8) == (b % 8)


def any_spec():
    return pl.BlockSpec(memory_space=pl.ANY)


def whole_spec(shape):
    return pl.BlockSpec(tuple(shape), lambda i: (0,) * len(shape))


def struct(shape, dtype):
    return jax.ShapeDtypeStruct(tuple(shape), dtype)


def full_shape(lines, rows, width):
    return (2, lines, 2, 2, rows, width)


def kernel_params(collective_id):
    if collective_id is None:
        return pltpu.CompilerParams(vmem_limit_bytes=VMEM_BYTES)
    return pltpu.CompilerParams(
        vmem_limit_bytes=VMEM_BYTES, collective_id=collective_id, has_side_effects=True
    )


def padded_frames(rows, put):
    frames = rows.shape[0] // PATCHES
    half = frames // 2
    zeros = jnp.zeros((PAD - PATCHES, rows.shape[1]), F32)
    for part in range(2):
        block = rows[half * PATCHES * part : half * PATCHES * (part + 1)].astype(F32)
        for f in range(half):
            put(half * part + f, jnp.concatenate([block[PATCHES * f : PATCHES * (f + 1)], zeros], axis=0))


def first_kernel(lines, *refs):
    (tok, cot, tile, q0, o0, q1, o1), (x_out, cot_b, full_tile, full_q, full_o, *results), (
        col_q1, block_o1, col_tile, block_o0, tok_v, cot_v, frames_v, ex_send, ex_recv, ex_local, loads), scratch = take(
        refs, 7, 7, 11, len(refs))
    place = Place(lines)
    t, z, y, x = place.t, place.z, place.y, place.x
    hops = lines - 1
    load_cot = pltpu.make_async_copy(cot, cot_v, loads.at[0])
    load_tok = pltpu.make_async_copy(tok, tok_v, loads.at[1])
    load_cot.start()
    load_tok.start()
    place.greet()
    pool = list(scratch)

    def sems():
        three = pool[:3]
        del pool[:3]
        return three

    tile_line = LineGather(place, tile, col_tile, sems())
    q0_line = LineGather(place, q0, full_q.at[t, :, y, x], sems(), kept=True)
    o0_line = LineGather(place, block_o0, full_o.at[t], sems(), to_core=full_o.at[t])
    q1_line = LineGather(place, q1, col_q1, sems())
    tile_plane = PlaneGather(place, col_tile, lambda v, u: full_tile.at[t, :, v, u], sems())
    o0_plane = PlaneGather(place, o0, lambda v, u: block_o0.at[v, u], sems(), cores=False)
    o1_plane = PlaneGather(place, o1, lambda v, u: block_o1.at[v, u], sems(), cores=False)
    own_slab = PlaneGather(place, q0, lambda v, u: full_q.at[t, z, v, u], sems())
    slabs = {}
    for k in range(1, lines):
        for sign in (-1, 1):
            far, own_sems = z + sign * k, sems()
            slabs[k, sign] = When(
                (far >= 0) & (far <= hops),
                functools.partial(
                    PlaneGather, place, full_q.at[t, far, y, x],
                    lambda v, u, far=far: full_q.at[t, far, v, u], own_sems, kept=True,
                ),
            )

    def pair(k, stage):
        slabs[k, -1].stage(stage)
        slabs[k, 1].stage(stage)

    q0_line.stage(0)
    own_slab.stage(0)
    o0_plane.stage(0)
    tile_line.stage(0)
    load_cot.wait()
    D = tok.shape[1]
    frames = x_out.shape[0]

    def put_cot(f, rows):
        frames_v[f] = rows.reshape(PAD // 8, 8, D)

    padded_frames(cot_v, put_cot)
    own_slab.stage(1)
    q0_line.stage(1)
    pair(1, 0)
    o0_plane.stage(1)
    tile_line.stage(1)
    q1_line.stage(0)
    o1_plane.stage(0)
    groups = PAD // 16
    mine = pltpu.make_async_copy(
        frames_v.at[:, pl.ds(groups * t, groups)], cot_b.at[pl.ds(frames * t, frames)], ex_local.at[0]
    )
    theirs = remote(
        frames_v.at[:, pl.ds(groups * (1 - t), groups)], cot_b.at[pl.ds(frames * t, frames)],
        (ex_send, ex_recv), 0, place.core,
    )
    mine.start()
    theirs.start()
    load_tok.wait()

    def put_tok(f, rows):
        x_out[f] = rows.astype(BF)

    padded_frames(tok_v, put_tok)
    o0_plane.stage(2)
    o0_plane.stage(3)
    o0_line.stage(0)
    pair(1, 1)
    own_slab.stage(2)
    for k in range(2, lines):
        q0_line.stage(k)
        pair(k, 0)
        tile_line.stage(k)
        q1_line.stage(k - 1)
        pair(k, 1)
        pair(k - 1, 2)
        o0_line.stage(k - 1)
    tile_plane.stage(0)
    o1_plane.stage(1)
    tile_plane.stage(1)
    o1_plane.stage(2)
    pair(hops, 2)
    o0_line.stage(hops)
    tile_plane.stage(2)
    q1_line.stage(hops)
    o1_plane.stage(3)
    tile_plane.stage(3)
    o0_line.stage(hops + 1)
    own_slab.stage(3)
    for k in range(1, lines):
        pair(k, 3)
    for result, part in zip(results, (col_q1, block_o1)):
        result[...] = part[...]
    mine.wait()
    theirs.wait()


def first_call(tokens, cot, tile, q0, o0, q1, o1, lines, collective_id):
    rows, D = tokens.shape
    frames = rows // PATCHES
    groups = PAD // 16
    vmem = pl.BlockSpec(memory_space=pltpu.VMEM)
    col = lambda own: struct((lines,) + own.shape, own.dtype)
    block = lambda own: struct((2, 2) + own.shape, own.dtype)
    full = lambda own: struct(full_shape(lines, *own.shape), own.dtype)
    vmem_like = lambda s: pltpu.VMEM(s.shape, s.dtype)
    return pl.pallas_call(
        functools.partial(first_kernel, lines),
        in_specs=[any_spec()] * 2 + [vmem] * 5,
        out_specs=[vmem] + [any_spec()] * 4 + [vmem] * 2,
        out_shape=[
            struct((frames, PAD, D), BF),
            struct((2 * frames, groups, 8, D), F32),
            full(tile),
            full(q0),
            full(o0),
            col(q1),
            block(o1),
        ],
        scratch_shapes=[
            vmem_like(col(q1)),
            vmem_like(block(o1)),
            vmem_like(col(tile)),
            vmem_like(block(o0)),
            pltpu.VMEM((rows, D), BF),
            pltpu.VMEM((rows, D), BF),
            pltpu.VMEM((frames, PAD // 8, 8, D), F32),
            dma_sems(1),
            dma_sems(1),
            dma_sems(1),
            dma_sems(2),
        ]
        + LineGather.scratch(lines) * 4
        + PlaneGather.scratch() * (4 + 2 * (lines - 1)),
        name="first_gather",
        compiler_params=kernel_params(collective_id),
    )(tokens, cot, tile, q0, o0, q1, o1)


def spatial_forward(x, w_ref, wo_ref, vec_ref, qkv_ref, mix_ref, p_ref, r_ref):
    cols = wo_ref.shape[2]
    xhat, _ = norm_parts(x)
    normed = (xhat * vec_ref[10:11, :] + vec_ref[0:1, :]).astype(BF)
    mask = spatial_mask()
    branch = vec_ref[3:4, :]
    for g, (q, k, v) in enumerate(project(normed, w_ref, vec_ref, 0, cols)):
        qkv_ref[0, g, :, 0:cols] = q
        qkv_ref[0, g, :, cols : 2 * cols] = k
        qkv_ref[0, g, :, 2 * cols : 3 * cols] = v
        pairs = []
        for j in range(cols // 128):
            sl = slice(128 * j, 128 * (j + 1))
            pairs.append((q[:, sl], k[:, sl], v[:, sl]))
        mixes, exps, recips = heads_forward(pairs, mask)
        for j in range(cols // 128):
            pair = g * (cols // 128) + j
            p_ref[0, pair] = exps[j]
            r_ref[0, :, pair : pair + 1] = recips[j]
        mix = jnp.concatenate(mixes, axis=1).astype(BF)
        mix_ref[0, g] = mix
        branch = branch + dot(mix, wo_ref[g], NT)
    return x + branch


def spatial_fwd_kernel(lines, *refs):
    if lines is None:
        x_ref, w_ref, wo_ref, vec_ref, s_ref, qkv_ref, mix_ref, p_ref, r_ref = refs
        s = spatial_forward(x_ref[0].astype(F32), w_ref, wo_ref, vec_ref, qkv_ref, mix_ref, p_ref, r_ref)
        s_ref[0] = s.reshape(s_ref.shape[1:])
        return
    (x_ref, w_ref, wo_ref, vec_ref), (col_q1, block_o1, q2, o2, q3, o3), (s_b, qkv_ref, mix_ref, p_ref, r_ref), (
        full_q1, full_o1), results, landed, (slots, ex_send, ex_recv, ex_local), *parts = take(
        refs, 4, 6, 5, 2, 4, 4, 4, 3, 3, 3, 3, 3, 3)
    col_q2, col_q3, block_o2, block_o3 = landed
    place = Place(lines)
    t = place.t
    i = pl.program_id(0)
    frames = pl.num_programs(0)
    groups = PAD // 16
    hops = lines - 1
    q1 = PlaneGather(place, col_q1, lambda v, u: full_q1.at[t, :, v, u], parts[0])
    o1 = LineGather(place, block_o1, full_o1.at[t], parts[1], to_core=full_o1.at[t])
    l2 = LineGather(place, q2, col_q2, parts[2])
    l3 = LineGather(place, q3, col_q3, parts[3])
    p2 = PlaneGather(place, o2, lambda v, u: block_o2.at[v, u], parts[4], cores=False)
    p3 = PlaneGather(place, o3, lambda v, u: block_o3.at[v, u], parts[5], cores=False)

    @pl.when(i == 0)
    def _():
        place.greet()

    at_step(0, (q1, 0), (o1, 0), (l2, 0), (l3, 0), (p2, 0), (p3, 0))
    at_step(2, (p2, 1), (p3, 1))
    at_step(3, (q1, 1), (o1, 1), (l2, 1), (l3, 1))
    at_step(5, (p2, 2), (p2, 3), (p3, 2), (p3, 3))
    at_step(6, *[(job, k) for k in range(2, hops) for job in (o1, l2, l3)])
    at_step(7, (q1, 2))

    def here(f):
        return pltpu.make_async_copy(
            slots.at[f % 2, pl.ds(groups * t, groups)], s_b.at[frames * t + f], ex_local.at[f]
        )

    def there(f):
        return remote(
            slots.at[f % 2, pl.ds(groups * (1 - t), groups)], s_b.at[frames * t + f], (ex_send, ex_recv), f, place.core
        )

    def sent(f):
        here(f).wait()
        left(there(f))

    s = spatial_forward(x_ref[0].astype(F32), w_ref, wo_ref, vec_ref, qkv_ref, mix_ref, p_ref, r_ref)

    @pl.when(i >= 2)
    def _():
        sent(i - 2)

    slots[i % 2] = s.reshape(slots.shape[1:])
    here(i).start()
    there(i).start()

    @pl.when(i == frames - 1)
    def _():
        o1.stage(hops)
        l2.stage(hops)
        l3.stage(hops)
        q1.stage(3)
        o1.stage(hops + 1)
        for result, part in zip(results, landed):
            result[...] = part[...]
        sent(i - 1)
        sent(i)

        def body(f, _):
            arrived(there(f))
            return _

        lax.fori_loop(0, frames, body, 0)


def spatial_fwd(x, w, wo, vec, links=None):
    frames, _, D = x.shape
    cols = D // 2
    pairs = D // 128
    groups = PAD // 16
    in_specs = [
        pl.BlockSpec((1, PAD, D), lambda i: (i, 0, 0)),
        whole_spec(w.shape),
        whole_spec(wo.shape),
        whole_spec(vec.shape),
    ]
    out_specs = [
        pl.BlockSpec((1, PAD // 8, 8, D), lambda i: (i, 0, 0, 0)),
        pl.BlockSpec((1, 2, PAD, 3 * cols), lambda i: (i, 0, 0, 0)),
        pl.BlockSpec((1, 2, PAD, cols), lambda i: (i, 0, 0, 0)),
        pl.BlockSpec((1, pairs, 2 * PAD, PAD), lambda i: (i, 0, 0, 0)),
        pl.BlockSpec((1, 2 * PAD, 128), lambda i: (i, 0, 0)),
    ]
    out_shape = [
        struct((frames, PAD // 8, 8, D), F32),
        struct((frames, 2, PAD, 3 * cols), BF),
        struct((frames, 2, PAD, cols), BF),
        struct((frames, pairs, 2 * PAD, PAD), BF),
        struct((frames, 2 * PAD, 128), F32),
    ]
    args, scratch, lines, collective_id = [x, w, wo, vec], [], None, None
    if links is not None:
        col_q1, block_o1, q2, o2, q3, o3, lines, collective_id = links
        args += [col_q1, block_o1, q2, o2, q3, o3]
        in_specs += [whole_spec(v.shape) for v in args[4:]]
        out_specs[0] = any_spec()
        out_shape[0] = struct((2 * frames, groups, 8, D), F32)
        col, block = col_q1.shape, block_o1.shape
        out_specs += [any_spec()] * 2 + [whole_spec(col)] * 2 + [whole_spec(block)] * 2
        out_shape += [struct(full_shape(*col), BF), struct((2, lines) + block, BF)]
        out_shape += [struct(col, BF)] * 2 + [struct(block, BF)] * 2
        scratch = [pltpu.VMEM(col, BF)] * 2 + [pltpu.VMEM(block, BF)] * 2
        scratch += [pltpu.VMEM((2, PAD // 8, 8, D), F32)] + [dma_sems(frames)] * 3
        scratch += PlaneGather.scratch() + LineGather.scratch(lines) * 3 + PlaneGather.scratch() * 2
    return pl.pallas_call(
        functools.partial(spatial_fwd_kernel, lines),
        grid=(frames,),
        in_specs=in_specs,
        out_specs=out_specs,
        out_shape=out_shape,
        scratch_shapes=scratch,
        name="spatial_fwd",
        compiler_params=kernel_params(collective_id),
    )(*args)


def spatial_bwd_kernel(lines, *refs):
    linked = lines is not None
    ins, joins, outs, results, (gw_ref, go_ref), rest = take(
        refs, 9, 7 if linked else 0, 4, 7 if linked else 0, 2, len(refs))
    x_ref, up_ref, qkv_ref, mix_ref, p_ref, r_ref, w_ref, wo_ref, vec_ref = ins
    gx_ref, gbw_ref, gbo_ref, gv_ref = outs
    cols = wo_ref.shape[2]
    i = pl.program_id(0)
    last = pl.num_programs(0) - 1

    @pl.when(i == 0)
    def _():
        gw_ref[...] = jnp.zeros_like(gw_ref)
        go_ref[...] = jnp.zeros_like(go_ref)
        gv_ref[...] = jnp.zeros_like(gv_ref)

    if linked:
        out_a, gw1, go1, col2, col3, block2, block3 = joins
        out_ref, col1, block1, sum_q2, sum_q3, sum_o2, sum_o3 = results
        place = Place(lines)
        parts = take(rest, PlaneReduce.n_scratch, LineReduce.n_scratch, 4, 4, 4, 4)
        q1 = PlaneReduce(place, gw1, col1, parts[0])
        o1 = LineReduce(place, go1, block1.at[0], parts[1])
        l2 = LineSum(place, col2, sum_q2, parts[2])
        l3 = LineSum(place, col3, sum_q3, parts[3])
        p2 = PlaneSum(place, block2, sum_o2, parts[4])
        p3 = PlaneSum(place, block3, sum_o3, parts[5])

        @pl.when(i == 0)
        def _():
            place.greet()

        at_step(0, (q1, 0), (o1, 0), (l2, 0), (l3, 0), (p2, 0), (p3, 0))
        at_step(1, (q1, 1))
        at_step(2, (o1, 1), (l2, 1), (l3, 1), (p2, 1), (p3, 1))
        at_step(3, (p2, 2), (p3, 2))
        at_step(4, (q1, 2), (o1, 2), *[(job, k) for k in range(2, lines - 1) for job in (l2, l3)])
        at_step(5, (l2, lines - 1), (l3, lines - 1))
        at_step(6, (q1, 3), *[(o1, k) for k in range(3, lines)])
        at_step(7, (o1, lines))
        out = out_a[0].reshape(PAD, out_a.shape[3])
        out_ref[0] = out[: out_ref.shape[1]].astype(BF)

    up = up_ref[0].reshape(PAD, up_ref.shape[3])
    gx = attn_back_common(
        x_ref[0].astype(F32), up.astype(BF), up, w_ref, wo_ref, vec_ref, 0, 10,
        lambda g: mix_ref[0, g],
        lambda g, j, rs: tuple(
            qkv_ref[0, g, :, cols * t + 128 * j : cols * t + 128 * (j + 1)] for t in range(3)
        ),
        lambda pair, b: (p_ref[0, pair], r_ref[0, :, pair : pair + 1]),
        gw_ref, go_ref, gv_ref, cols, 1,
    )
    gx_ref[0] = gx[: gx_ref.shape[1]]

    @pl.when(i == last)
    def _():
        gbw_ref[...] = gw_ref[...].astype(BF)
        gbo_ref[...] = go_ref[...].astype(BF)


def spatial_bwd(x, up, qkv, mix, p, r, w, wo, vec, links=None):
    frames, _, D = x.shape
    cols = D // 2
    pairs = D // 128
    frame_spec = pl.BlockSpec((1, PAD // 8, 8, D), lambda i: (i, 0, 0, 0))
    in_specs = [
        pl.BlockSpec((1, PAD, D), lambda i: (i, 0, 0)),
        frame_spec,
        pl.BlockSpec((1, 2, PAD, 3 * cols), lambda i: (i, 0, 0, 0)),
        pl.BlockSpec((1, 2, PAD, cols), lambda i: (i, 0, 0, 0)),
        pl.BlockSpec((1, pairs, 2 * PAD, PAD), lambda i: (i, 0, 0, 0)),
        pl.BlockSpec((1, 2 * PAD, 128), lambda i: (i, 0, 0)),
        whole_spec(w.shape),
        whole_spec(wo.shape),
        whole_spec(vec.shape),
    ]
    live_spec = pl.BlockSpec((1, PATCHES, D), lambda i: (i, 0, 0))
    out_specs = [live_spec, whole_spec(w.shape), whole_spec(wo.shape), whole_spec((8, D))]
    out_shape = [
        struct((frames, PATCHES, D), F32), struct(w.shape, BF), struct(wo.shape, BF), struct((8, D), F32)
    ]
    args = [x, up, qkv, mix, p, r, w, wo, vec]
    scratch, lines, collective_id = [pltpu.VMEM(w.shape, F32), pltpu.VMEM(wo.shape, F32)], None, None
    if links is not None:
        out_a, gw1, go1, col2, col3, block2, block3, lines, collective_id = links
        args += [out_a, gw1, go1, col2, col3, block2, block3]
        q_block, o_block = gw1.shape[4:], go1.shape[4:]
        in_specs += [frame_spec] + [any_spec()] * 2 + [whole_spec(v.shape) for v in args[-4:]]
        more = [
            struct(col2.shape, BF), struct(block2.shape, BF), struct(q_block, F32), struct(q_block, F32),
            struct((1,) + o_block, F32), struct((1,) + o_block, F32),
        ]
        out_specs += [live_spec] + [whole_spec(s.shape) for s in more]
        out_shape += [struct((frames, PATCHES, D), BF)] + more
        scratch += PlaneReduce.scratch(lines, q_block, BF) + LineReduce.scratch(lines, o_block, BF)
        scratch += LineSum.scratch(lines, q_block, BF) * 2 + PlaneSum.scratch(1, o_block, BF) * 2
    return pl.pallas_call(
        functools.partial(spatial_bwd_kernel, lines),
        grid=(frames,),
        in_specs=in_specs,
        out_specs=out_specs,
        out_shape=out_shape,
        scratch_shapes=scratch,
        name="spatial_bwd",
        compiler_params=kernel_params(collective_id),
    )(*args)


def group_rows(block, live):
    parts = []
    for b in range(block.shape[1]):
        rows = block[:, b].reshape(GROUP, block.shape[3])
        parts.append(rows if b == 0 else jnp.where(live(b), rows, 0.0))
    return jnp.concatenate(parts, axis=0)


def temporal_forward(x, w_ref, wo_ref, vec_ref, qkv_ref, mix_ref, p_ref, r_ref):
    cols = wo_ref.shape[2]
    n = x.shape[0]
    xhat, _ = norm_parts(x)
    normed = (xhat * vec_ref[11:12, :] + vec_ref[4:5, :]).astype(BF)
    mask = temporal_mask()
    branch = vec_ref[7:8, :]
    for g, (q, k, v) in enumerate(project(normed, w_ref, vec_ref, 4, cols)):
        qkv_ref[g, :, 0:cols] = q
        qkv_ref[g, :, cols : 2 * cols] = k
        qkv_ref[g, :, 2 * cols : 3 * cols] = v
        pairs = []
        for b in range(n // GROUP):
            rs = slice(GROUP * b, GROUP * (b + 1))
            for j in range(cols // 128):
                sl = slice(128 * j, 128 * (j + 1))
                pairs.append((q[rs, sl], k[rs, sl], v[rs, sl]))
        mixes, exps, recips = heads_forward(pairs, mask)
        blocks = []
        for b in range(n // GROUP):
            for j in range(cols // 128):
                pair, i = g * (cols // 128) + j, b * (cols // 128) + j
                p_ref[pair, 2 * GROUP * b : 2 * GROUP * (b + 1)] = exps[i]
                r_ref[2 * GROUP * b : 2 * GROUP * (b + 1), pair : pair + 1] = recips[i]
            blocks.append(jnp.concatenate(mixes[b * (cols // 128) : (b + 1) * (cols // 128)], axis=1))
        mix = jnp.concatenate(blocks, axis=0).astype(BF)
        mix_ref[g] = mix
        branch = branch + dot(mix, wo_ref[g], NT)
    return x + branch


def temporal_fwd_kernel(lines, groups, *refs):
    linked = lines is not None
    (x_ref, w_ref, wo_ref, vec_ref), joins, (s_ref, qkv_ref, mix_ref, p_ref, r_ref), results, *parts = take(
        refs, 4, 4 if linked else 0, 5, 4 if linked else 0, 3, 3, 3, 3)
    i = pl.program_id(0)
    if linked:
        col_q2, col_q3, block_o2, block_o3 = joins
        full_q2, full_q3, full_o2, full_o3 = results
        place = Place(lines)
        t, hops = place.t, lines - 1
        q2 = PlaneGather(place, col_q2, lambda v, u: full_q2.at[t, :, v, u], parts[0])
        q3 = PlaneGather(place, col_q3, lambda v, u: full_q3.at[t, :, v, u], parts[1])
        o2 = LineGather(place, block_o2, full_o2.at[t], parts[2], to_core=full_o2.at[t])
        o3 = LineGather(place, block_o3, full_o3.at[t], parts[3], to_core=full_o3.at[t])

        @pl.when(i == 0)
        def _():
            place.greet()

        at_step(0, (q2, 0), (o2, 0), (o3, 0))
        at_step(2, (q2, 1), (q3, 0))
        at_step(3, (o2, 1), (o3, 1))
        at_step(5, *[(job, k) for k in range(2, hops) for job in (o2, o3)])
        at_step(6, (q3, 1))
    x = group_rows(x_ref[...], lambda b: STEP_GROUPS * i + b < groups)
    s = temporal_forward(x, w_ref, wo_ref, vec_ref, qkv_ref, mix_ref, p_ref, r_ref)
    for b in range(STEP_GROUPS):
        s_ref[:, b] = s[GROUP * b : GROUP * (b + 1)].reshape(FRAMES, 8, s.shape[1])
    if linked:
        at_step(
            6, (q2, 2), (o2, hops), (o3, hops), (q2, 3), (o2, hops + 1), (o3, hops + 1), (q3, 2), (q3, 3)
        )


def temporal_specs(groups, D):
    cols = D // 2
    n = STEP_GROUPS * GROUP
    steps = -(-groups // STEP_GROUPS)
    pairs = D // 128
    stream = pl.BlockSpec((FRAMES, STEP_GROUPS, 8, D), lambda i: (0, i, 0, 0))
    specs = [
        pl.BlockSpec((2, n, 3 * cols), lambda i: (0, i, 0)),
        pl.BlockSpec((2, n, cols), lambda i: (0, i, 0)),
        pl.BlockSpec((pairs, 2 * n, GROUP), lambda i: (0, i, 0)),
        pl.BlockSpec((2 * n, 128), lambda i: (i, 0)),
    ]
    shapes = [
        struct((2, steps * n, 3 * cols), BF),
        struct((2, steps * n, cols), BF),
        struct((pairs, 2 * steps * n, GROUP), BF),
        struct((2 * steps * n, 128), F32),
    ]
    return steps, stream, specs, shapes


def temporal_fwd(x, w, wo, vec, links=None):
    groups, D = x.shape[1], x.shape[3]
    steps, stream, kept_specs, kept_shapes = temporal_specs(groups, D)
    in_specs = [stream, whole_spec(w.shape), whole_spec(wo.shape), whole_spec(vec.shape)]
    out_specs = [stream] + kept_specs
    out_shape = [struct(x.shape, F32)] + kept_shapes
    args, scratch, lines, collective_id = [x, w, wo, vec], [], None, None
    if links is not None:
        col_q2, col_q3, block_o2, block_o3, lines, collective_id = links
        args += [col_q2, col_q3, block_o2, block_o3]
        in_specs += [whole_spec(v.shape) for v in args[4:]]
        out_specs += [any_spec()] * 4
        out_shape += [struct(full_shape(*col_q2.shape), BF)] * 2 + [struct((2, lines) + block_o2.shape, BF)] * 2
        scratch = PlaneGather.scratch() * 2 + LineGather.scratch(lines) * 2
    return pl.pallas_call(
        functools.partial(temporal_fwd_kernel, lines, groups),
        grid=(steps,),
        in_specs=in_specs,
        out_specs=out_specs,
        out_shape=out_shape,
        scratch_shapes=scratch,
        name="temporal_fwd",
        compiler_params=kernel_params(collective_id),
    )(*args)


def temporal_bwd_kernel(lines, groups, *refs):
    linked = lines is not None
    ins, joins, outs, results, (gw_ref, go_ref), rest = take(
        refs, 9, 5 if linked else 0, 4, 5 if linked else 0, 2, len(refs))
    x_ref, up_ref, qkv_ref, mix_ref, p_ref, r_ref, w_ref, wo_ref, vec_ref = ins
    gx_ref, gbw_ref, gbo_ref, gv_ref = outs
    cols = wo_ref.shape[2]
    i = pl.program_id(0)
    steps = pl.num_programs(0)

    @pl.when(i == 0)
    def _():
        gw_ref[...] = jnp.zeros_like(gw_ref)
        go_ref[...] = jnp.zeros_like(go_ref)
        gv_ref[...] = jnp.zeros_like(gv_ref)

    if linked:
        out_b, gq2, gq3, go2, go3 = joins
        out_a, col2, col3, block2, block3 = results
        place = Place(lines)
        t = place.t
        frames = FRAMES // 2
        (slots, held, ex_send, ex_recv, ex_local), *parts = take(
            rest, 5, PlaneReduce.n_scratch, PlaneReduce.n_scratch, LineReduce.n_scratch, LineReduce.n_scratch)
        q2 = PlaneReduce(place, gq2, col2, parts[0])
        q3 = PlaneReduce(place, gq3, col3, parts[1])
        o2 = LineReduce(place, go2, block2.at[0], parts[2])
        o3 = LineReduce(place, go3, block3.at[0], parts[3])
        out_load = pltpu.make_async_copy(out_b.at[pl.ds(frames * t, frames)], held, ex_local.at[steps])
        out_here = pltpu.make_async_copy(held, out_a.at[:, pl.ds(groups * t, groups)], ex_local.at[steps])
        out_there = remote(
            out_b.at[pl.ds(frames * (1 - t), frames)], out_a.at[:, pl.ds(groups * t, groups)],
            (ex_send, ex_recv), steps, place.core,
        )

        @pl.when(i == 0)
        def _():
            place.greet()

        at_step(0, (q2, 0), (o2, 0), (q3, 0), (o3, 0))

        @pl.when(i == 2)
        def _():
            out_load.start()
            out_there.start()

        @pl.when(i == 3)
        def _():
            out_load.wait()
            out_here.start()

        at_step(1, (q2, 1))
        at_step(2, (o2, 1), (q3, 1), (o3, 1))
        at_step(4, (q2, 2), (o2, 2), (o3, 2))
        at_step(5, (q3, 2))
        at_step(6, (q2, 3), *[(job, k) for k in range(3, lines) for job in (o2, o3)])

    live = lambda b: STEP_GROUPS * i + b < groups
    x = group_rows(x_ref[...], live)
    up = group_rows(up_ref[...], live)
    gx = attn_back_common(
        x, up.astype(BF), up, w_ref, wo_ref, vec_ref, 4, 11,
        lambda g: mix_ref[g],
        lambda g, j, rs: tuple(
            qkv_ref[g, rs, cols * t + 128 * j : cols * t + 128 * (j + 1)] for t in range(3)
        ),
        lambda pair, b: (
            p_ref[pair, 2 * GROUP * b : 2 * GROUP * (b + 1)],
            r_ref[2 * GROUP * b : 2 * GROUP * (b + 1), pair : pair + 1],
        ),
        gw_ref, go_ref, gv_ref, cols, x.shape[0] // GROUP,
    )

    @pl.when(i == steps - 1)
    def _():
        gbw_ref[...] = gw_ref[...].astype(BF)
        gbo_ref[...] = go_ref[...].astype(BF)

    if not linked:
        for b in range(STEP_GROUPS):
            gx_ref[:, b] = gx[GROUP * b : GROUP * (b + 1)].reshape(FRAMES, 8, gx.shape[1])
        return

    tail = groups % STEP_GROUPS or STEP_GROUPS

    def target(s, count):
        return gx_ref.at[:, pl.ds(groups * t + STEP_GROUPS * s, count)]

    def here(s, count):
        part = slots.at[s % 2, pl.ds(frames * t, frames), pl.ds(0, count)]
        return pltpu.make_async_copy(part, target(s, count), ex_local.at[s])

    def there(s, count):
        part = slots.at[s % 2, pl.ds(frames * (1 - t), frames), pl.ds(0, count)]
        return remote(part, target(s, count), (ex_send, ex_recv), s, place.core)

    def sent(s, count):
        here(s, count).wait()
        left(there(s, count))

    @pl.when(i >= 2)
    def _():
        sent(i - 2, STEP_GROUPS)

    for b in range(STEP_GROUPS):
        slots[i % 2, :, b] = gx[GROUP * b : GROUP * (b + 1)].reshape(FRAMES, 8, gx.shape[1])

    @pl.when(i < steps - 1)
    def _():
        here(i, STEP_GROUPS).start()
        there(i, STEP_GROUPS).start()

    @pl.when(i == steps - 1)
    def _():
        here(i, tail).start()
        there(i, tail).start()
        o2.stage(lines)
        o3.stage(lines)
        q3.stage(3)
        out_here.wait()
        out_there.wait()
        sent(i - 1, STEP_GROUPS)
        sent(i, tail)

        def body(s, _):
            arrived(there(s, STEP_GROUPS))
            return _

        lax.fori_loop(0, steps - 1, body, 0)
        arrived(there(i, tail))


def temporal_bwd(x, up, qkv, mix, p, r, w, wo, vec, links=None):
    groups, D = x.shape[1], x.shape[3]
    steps, stream, kept_specs, _ = temporal_specs(groups, D)
    in_specs = [stream, stream] + kept_specs + [whole_spec(v.shape) for v in (w, wo, vec)]
    out_specs = [stream, whole_spec(w.shape), whole_spec(wo.shape), whole_spec((8, D))]
    out_shape = [struct(x.shape, F32), struct(w.shape, BF), struct(wo.shape, BF), struct((8, D), F32)]
    args = [x, up, qkv, mix, p, r, w, wo, vec]
    scratch, lines, collective_id = [pltpu.VMEM(w.shape, F32), pltpu.VMEM(wo.shape, F32)], None, None
    if links is not None:
        out_b, gq2, gq3, go2, go3, lines, collective_id = links
        args += [out_b, gq2, gq3, go2, go3]
        q_block, o_block = gq2.shape[4:], go2.shape[4:]
        in_specs += [any_spec()] * 5
        out_specs[0] = any_spec()
        a_shape = (FRAMES // 2, 2 * groups, 8, D)
        out_shape[0] = struct(a_shape, F32)
        more = [struct((lines,) + q_block, BF)] * 2 + [struct((1, 2, 2) + o_block, BF)] * 2
        out_specs += [any_spec()] + [whole_spec(s.shape) for s in more]
        out_shape += [struct(a_shape, F32)] + more
        scratch += [pltpu.VMEM((2, FRAMES, STEP_GROUPS, 8, D), F32), pltpu.VMEM((FRAMES // 2, groups, 8, D), F32)]
        scratch += [dma_sems(steps + 1)] * 3
        scratch += PlaneReduce.scratch(lines, q_block, BF) * 2 + LineReduce.scratch(lines, o_block, BF) * 2
    return pl.pallas_call(
        functools.partial(temporal_bwd_kernel, lines, groups),
        grid=(steps,),
        in_specs=in_specs,
        out_specs=out_specs,
        out_shape=out_shape,
        scratch_shapes=scratch,
        name="temporal_bwd",
        compiler_params=kernel_params(collective_id),
    )(*args)


LAST_CUT = 640


def last_kernel(lines, *refs):
    (gq0, go0, tiles, col1, block1), (sum_q0, sum_o0, sum_tile, sum_q1, sum_o1), (
        col_a, col_b, col_tile, block0), *parts = take(
        refs, 5, 5, 4, 9, 9, 9, 9, 4, 4, 4, 4, 4, 4)
    place = Place(lines)
    place.greet()
    width = sum_q0.shape[1]
    qa = PlaneReduce(place, gq0, col_a, parts[0], pl.ds(0, LAST_CUT))
    qb = PlaneReduce(place, gq0, col_b, parts[1], pl.ds(LAST_CUT, width - LAST_CUT))
    small = PlaneReduce(place, tiles, col_tile, parts[2])
    o0 = LineReduce(place, go0, block0.at[0], parts[3])
    qa_line = LineSum(place, col_a, sum_q0.at[:, 0:LAST_CUT], parts[4])
    qb_line = LineSum(place, col_b, sum_q0.at[:, LAST_CUT:width], parts[5])
    small_line = LineSum(place, col_tile, sum_tile, parts[6])
    q1_line = LineSum(place, col1, sum_q1, parts[7])
    o1_plane = PlaneSum(place, block1, sum_o1, parts[8])
    o0_plane = PlaneSum(place, block0, sum_o0, parts[9])
    n = lines
    qa.stage(0)
    qb.stage(0)
    o0.stage(0)
    small.stage(0)
    q1_line.stage(0)
    qa.stage(1)
    qb.stage(1)
    o1_plane.stage(0)
    small.stage(1)
    o0.stage(1)
    q1_line.stage(1)
    qa.stage(2)
    small.stage(2)
    o0.stage(2)
    for k in range(2, n - 1):
        q1_line.stage(k)
    qb.stage(2)
    qa.stage(3)
    qa_line.stage(0)
    small.stage(3)
    small_line.stage(0)
    q1_line.stage(n - 1)
    for k in range(3, n + 1):
        o0.stage(k)
    o0_plane.stage(0)
    o1_plane.stage(1)
    qb.stage(3)
    qb_line.stage(0)
    for k in range(1, n):
        qa_line.stage(k)
        small_line.stage(k)
        qb_line.stage(k)
        if k == 1:
            o0_plane.stage(1)
            o1_plane.stage(2)
    o0_plane.stage(2)


def last_call(gq0, go0, tiles, col1, block1, lines, collective_id):
    q_block, o_block, tile = gq0.shape[4:], go0.shape[4:], tiles.shape[4:]
    rows, width = q_block
    cut_a, cut_b = (rows, LAST_CUT), (rows, width - LAST_CUT)
    vmem = pl.BlockSpec(memory_space=pltpu.VMEM)
    return pl.pallas_call(
        functools.partial(last_kernel, lines),
        in_specs=[any_spec()] * 3 + [vmem] * 2,
        out_specs=[vmem] * 5,
        out_shape=[
            struct(q_block, F32), struct((1,) + o_block, F32), struct(tile, F32), struct(q_block, F32),
            struct((1,) + o_block, F32),
        ],
        scratch_shapes=[
            pltpu.VMEM((lines,) + cut_a, BF),
            pltpu.VMEM((lines,) + cut_b, BF),
            pltpu.VMEM((lines,) + tile, F32),
            pltpu.VMEM((1, 2, 2) + o_block, BF),
        ]
        + PlaneReduce.scratch(lines, cut_a, BF)
        + PlaneReduce.scratch(lines, cut_b, BF)
        + PlaneReduce.scratch(lines, tile, F32)
        + LineReduce.scratch(lines, o_block, BF)
        + LineSum.scratch(lines, cut_a, BF)
        + LineSum.scratch(lines, cut_b, BF)
        + LineSum.scratch(lines, tile, F32)
        + LineSum.scratch(lines, q_block, BF)
        + PlaneSum.scratch(1, o_block, BF) * 2,
        name="last_reduce",
        compiler_params=kernel_params(collective_id),
    )(gq0, go0, tiles, col1, block1)


MLP_ROWS = 416
MLP_CHUNK = 1536
INV_SQRT2 = 0.7071067811865476
INV_SQRT2PI = 0.3989422804014327


def mlp_kernel(x_ref, cot_ref, wia, wib, woa, wob, vec_ref, hid_ref, out_ref, up_ref,
               gia, gib, goa, gob, gv_ref, gh_ref, wi_ref, wo_ref, ai_ref, ao_ref, dn_ref, sems):
    i = pl.program_id(0)
    last = pl.num_programs(0) - 1
    chunks = wi_ref.shape[0]
    per = chunks // 2
    wide, width = wia.shape[2], per * MLP_CHUNK

    def copies(table, out):
        found = []
        for vmem, first, second in table:
            for g in range(2):
                for c in range(per):
                    start, stop = MLP_CHUNK * c, MLP_CHUNK * (c + 1)
                    for array, low, high in ((first, 0, wide), (second, wide, width)):
                        lo, hi = max(start, low), min(stop, high)
                        if lo < hi:
                            here = vmem.at[g * per + c, :, pl.ds(lo - start, hi - lo)]
                            there = array.at[g, :, pl.ds(lo - low, hi - lo)]
                            sem = sems.at[int(out), len(found)]
                            found.append(pltpu.make_async_copy(*((here, there) if out else (there, here)), sem))
        return found

    @pl.when(i == 0)
    def _():
        loads = copies(((wi_ref, wia, wib), (wo_ref, woa, wob)), False)
        for copy in loads:
            copy.start()
        for ref in (ai_ref, ao_ref, gv_ref, gh_ref):
            ref[...] = jnp.zeros_like(ref)
        for copy in loads:
            copy.wait()

    x = x_ref[...]
    xhat, rstd = norm_parts(x)
    gain = vec_ref[12:13, :]
    normed = (xhat * gain + vec_ref[8:9, :]).astype(BF)
    up = cot_ref[...]
    ub = up.astype(BF)
    gv_ref[3:4, :] += jnp.sum(up, axis=0, keepdims=True)
    out_ref[...] = x + vec_ref[9:10, :]
    dn_ref[...] = jnp.zeros_like(dn_ref)

    def chunk(k, _):
        pre = dot(normed, wi_ref[k], NN) + hid_ref[k]
        cdf = 0.5 + 0.5 * lax.erf(pre * INV_SQRT2)
        act = (pre * cdf).astype(BF)
        out_ref[...] += dot(act, wo_ref[k], NT)
        ao_ref[k] += dot(ub, act, TN)
        dact = dot(ub, wo_ref[k], NN).astype(BF).astype(F32)
        slope = cdf + pre * (jnp.exp(pre * pre * -0.5) * INV_SQRT2PI)
        dpre = (dact * slope).astype(BF)
        gh_ref[k] += jnp.sum(dpre.astype(F32), axis=0, keepdims=True)
        ai_ref[k] += dot(normed, dpre, TN)
        dn_ref[...] += dot(dpre, wi_ref[k], NT)
        return _

    lax.fori_loop(0, chunks, chunk, 0)
    dn = dn_ref[...]
    gv_ref[0:1, :] += jnp.sum(dn, axis=0, keepdims=True)
    gv_ref[4:5, :] += jnp.sum(dn * xhat, axis=0, keepdims=True)
    up_ref[...] = up + norm_back(dn, xhat, rstd, gain)

    @pl.when(i == last)
    def _():
        def place(k, _):
            wi_ref[k] = ai_ref[k].astype(BF)
            wo_ref[k] = ao_ref[k].astype(BF)
            return _

        lax.fori_loop(0, chunks, place, 0)
        stores = copies(((wi_ref, gia, gib), (wo_ref, goa, gob)), True)
        for copy in stores:
            copy.start()
        for copy in stores:
            copy.wait()


def mlp_both(x, cot, wia, wib, woa, wob, vec, hidden):
    rows, D = x.shape
    width = hidden.shape[1]
    chunks = 2 * width // MLP_CHUNK
    row_spec = pl.BlockSpec((MLP_ROWS, D), lambda i: (i, 0))
    mats = [wia, wib, woa, wob]
    both = (chunks, D, MLP_CHUNK)
    units = (chunks, 1, MLP_CHUNK)
    outs = pl.pallas_call(
        mlp_kernel,
        grid=(rows // MLP_ROWS,),
        in_specs=[row_spec, row_spec] + [any_spec()] * 4 + [whole_spec(vec.shape), whole_spec(units)],
        out_specs=[row_spec, row_spec] + [any_spec()] * 4 + [whole_spec((8, D)), whole_spec(units)],
        out_shape=[struct((rows, D), F32)] * 2
        + [struct(m.shape, BF) for m in mats]
        + [struct((8, D), F32), struct(units, F32)],
        scratch_shapes=[pltpu.VMEM(both, BF)] * 2
        + [pltpu.VMEM(both, F32)] * 2
        + [pltpu.VMEM((MLP_ROWS, D), F32), pltpu.SemaphoreType.DMA((2, 6 * chunks))],
        name="mlp_both",
        compiler_params=kernel_params(None),
    )(x, cot, *mats, vec, hidden.reshape(units))
    return (*outs[:-1], outs[-1].reshape(hidden.shape))


def swap_to_patches(rows):
    return lax.all_to_all(rows, "tensor", split_axis=1, concat_axis=0, tiled=True)


def swap_to_frames(rows):
    return lax.all_to_all(rows, "tensor", split_axis=0, concat_axis=1, tiled=True)


def pad_frames(rows):
    D = rows.shape[1]
    return jnp.pad(rows.reshape(-1, PATCHES, D), ((0, 0), (0, PAD - PATCHES), (0, 0)))


def shards(tokens, cotangent, attn_qkv, attn_out, mlp_in, mlp_out, norm_gains, biases, hidden_bias):
    D = tokens.shape[1]
    depth = mlp_in.shape[1]
    cols = attn_qkv.shape[4]
    units = mlp_in.shape[2]
    frames = tokens.shape[0] // PATCHES
    everyone = ("dp", "tensor")
    chips = D // depth
    devices = 2 * chips
    share = D // devices
    wide = 3 * cols
    down = mlp_out[0].T
    owns = []
    for s in range(2):
        owns += [attn_qkv[0, s].reshape(depth, wide), attn_out[0, s].T]
    owns += [mlp_in[0, :, :wide], mlp_in[0, :, wide:], down[:, :wide], down[:, wide:]]
    small = jnp.concatenate(
        [biases[0].reshape(-1), norm_gains[0].reshape(-1), hidden_bias[0].reshape(-1)]
    )
    count = small.shape[0]

    def vectors(small):
        vec = small[:, : 13 * share].reshape(devices, 13, share).transpose(1, 0, 2).reshape(13, D)
        return vec, small[:, 13 * share :].reshape(2, units)

    def spread(gv_s, gv_t, gv_m, g_hidden):
        vec_grad = jnp.concatenate(
            [gv_s[0:4], gv_t[0:4], gv_m[0:1], gv_m[3:4], gv_s[4:5], gv_t[4:5], gv_m[4:5]]
        )
        vec_grad = vec_grad.reshape(13, devices, share).transpose(1, 0, 2).reshape(devices, 13 * share)
        return jnp.concatenate([vec_grad, g_hidden.reshape(devices, -1)], axis=1)

    flat = lambda w: w.reshape(2, D, w.shape[-1])
    rows_of = lambda v: v.reshape(-1, D)
    if depth % 16 == 0 and chips % 4 == 0:
        lines = chips // 4
        cut = lambda g: g.reshape(full_shape(lines, depth, g.shape[2]))
        tile = jnp.pad(small, (0, 1024 - count)).reshape(8, 128)
        x, cot, full_tile, *w0, col_q1, block_o1 = first_call(tokens, cotangent, tile, *owns[:4], lines, 1)
        vec, hidden = vectors(
            full_tile.reshape(2, chips, 1024).transpose(1, 0, 2).reshape(devices, 1024)[:, :count]
        )
        w0 = [flat(w) for w in w0]
        x1, *kept_s, q1, o1, col_q2, col_q3, block_o2, block_o3 = spatial_fwd(
            x, *w0, vec, (col_q1, block_o1, *owns[4:], lines, 2)
        )
        w1 = [flat(q1), flat(o1)]
        x2, *kept_t, q2, q3, o2, o3 = temporal_fwd(
            x1, *w1, vec, (col_q2, col_q3, block_o2, block_o3, lines, 3)
        )
        out_b, up2, gq2, go2, gq3, go3, gv_m, g_hidden = mlp_both(
            rows_of(x2), rows_of(cot), flat(q2), flat(o2), flat(q3), flat(o3), vec, hidden
        )
        up1, gq1, go1, gv_t, out_a, col2, col3, block2, block3 = temporal_bwd(
            x1, up2.reshape(x1.shape), *kept_t, *w1, vec,
            (out_b.reshape(x1.shape), cut(gq2), cut(gq3), cut(go2), cut(go3), lines, 4),
        )
        up0, gq0, go0, gv_s, output, col1, block1, gq2, gq3, go2, go3 = spatial_bwd(
            x, up1, *kept_s, *w0, vec, (out_a, cut(gq1), cut(go1), col2, col3, block2, block3, lines, 5)
        )
        tiles = jnp.pad(spread(gv_s, gv_t, gv_m, g_hidden), ((0, 0), (0, 1024 - count)))
        tiles = tiles.reshape(chips, 2, 1024).transpose(1, 0, 2).reshape(full_shape(lines, 8, 128))
        gq0, go0, small_grad, gq1, go1 = last_call(cut(gq0), cut(go0), tiles, col1, block1, lines, 6)
        small_grad = small_grad.reshape(-1)[:count]
        go0, go1, go2, go3 = [g[0] for g in (go0, go1, go2, go3)]
    else:
        small = lax.all_gather(small.reshape(1, -1), everyone, axis=0, tiled=True)
        vec, hidden = vectors(small)
        weights = [flat(lax.all_gather(w, ("tensor", "dp"), axis=0, tiled=True).reshape(2, D, -1)) for w in owns]
        x = pad_frames(tokens)
        fold = lambda v: v.reshape(frames, PAD // 8, 8, D)
        x1, *kept_s = spatial_fwd(x, *weights[0:2], vec)
        x1 = swap_to_patches(x1)
        x2, *kept_t = temporal_fwd(x1, *weights[2:4], vec)
        cot = swap_to_patches(fold(pad_frames(cotangent).astype(F32)))
        out_b, up2, *mlp_grads, gv_m, g_hidden = mlp_both(
            rows_of(x2), rows_of(cot), *weights[4:], vec, hidden
        )
        output = swap_to_frames(out_b.reshape(x1.shape)).reshape(frames, PAD, D)[:, :PATCHES].astype(BF)
        up1, *grads1, gv_t = temporal_bwd(x1, up2.reshape(x1.shape), *kept_t, *weights[2:4], vec)
        up0, *grads0, gv_s = spatial_bwd(x, swap_to_frames(up1), *kept_s, *weights[0:2], vec)
        gq0, go0, gq1, go1, gq2, go2, gq3, go3 = [
            lax.psum_scatter(
                g.reshape(2 * D, g.shape[2]), ("tensor", "dp"), scatter_dimension=0, tiled=True
            ).astype(F32)
            for g in grads0 + grads1 + mlp_grads
        ]
        small_grad = lax.psum_scatter(
            spread(gv_s, gv_t, gv_m, g_hidden), everyone, scatter_dimension=0, tiled=True
        )[0]
    grad_qkv = jnp.stack([gq0.reshape(depth, 3, cols), gq1.reshape(depth, 3, cols)])[None]
    grad_out = jnp.stack([go0.T, go1.T])[None]
    grad_biases = small_grad[: 10 * share].reshape(1, 10, share)
    grad_gains = small_grad[10 * share : 13 * share].reshape(1, 3, share)
    grad_hidden = small_grad[13 * share :].reshape(1, -1)
    return (
        rows_of(output),
        rows_of(up0),
        grad_qkv,
        grad_out,
        jnp.concatenate([gq2, go2], axis=1)[None],
        jnp.concatenate([gq3, go3], axis=1).T[None],
        grad_gains,
        grad_biases,
        grad_hidden,
    )


def solution(mesh):
    placed = (
        P(("dp", "tensor"), None),
        P(("dp", "tensor"), None),
        P(None, None, "dp", None, "tensor"),
        P(None, None, "tensor", "dp"),
        P(None, "dp", "tensor"),
        P(None, "tensor", "dp"),
        P(None, None, ("dp", "tensor")),
        P(None, None, ("dp", "tensor")),
        P(None, ("dp", "tensor")),
    )
    return jax.shard_map(
        shards, mesh=mesh, in_specs=placed, out_specs=placed, check_vma=False
    )
```

time: 470 us -> 392 us (0.83); the launches traced: 470 us -> 384 us
  Pallas kernels: 438 us -> 346 us
    pallas_call x1, Pallas kernels: 86.8 us -> 52.1 us  [temporal_bwd(): pl.pallas_call(functools.partial(temporal_bwd_kernel, lines, groups), gri...]
    pallas_call x2, Pallas kernels: 142 us -> 111 us  [the longest x1 70.8 us: mlp_both(): pl.pallas_call(mlp_kernel, grid=(rows // MLP_ROWS,), in_specs=[row_spec,...]
    pallas_call x1, Pallas kernels: 61.9 us -> 43 us  [temporal_fwd(): pl.pallas_call(functools.partial(temporal_fwd_kernel, lines, groups), gri...]
    pallas_call x1, Pallas kernels: 44 us -> 36.4 us  [spatial_fwd(): pl.pallas_call(functools.partial(spatial_fwd_kernel, lines), grid=(frames...]
where the time goes in v4:
time: 392 us; the launch traced here: 384 us
  Pallas kernels  346 us (88%)
  local copies, waits for them, and re-layouts  31.1 us (8%)
  other arithmetic  5.47 us (1%)
    pallas_call x1, Pallas kernels, mlp_both(): pl.pallas_call(mlp_kernel, grid=(rows // MLP_ROWS,), in_specs=[row_spec,...  70.8 us
    pallas_call x1, Pallas kernels, spatial_bwd(): pl.pallas_call(functools.partial(spatial_bwd_kernel, lines), grid=(frames...  58.8 us
    pallas_call x1, Pallas kernels, temporal_bwd(): pl.pallas_call(functools.partial(temporal_bwd_kernel, lines, groups), gri...  52.1 us
    pallas_call x1, Pallas kernels, last_call(): pl.pallas_call(functools.partial(last_kernel, lines), in_specs=[any_spec(...  45.7 us
    pallas_call x1, Pallas kernels, temporal_fwd(): pl.pallas_call(functools.partial(temporal_fwd_kernel, lines, groups), gri...  43 us
    pallas_call x1, Pallas kernels, first_call(): pl.pallas_call(functools.partial(first_kernel, lines), in_specs=[any_spec...  39.8 us
    pallas_call x1, Pallas kernels, spatial_fwd(): pl.pallas_call(functools.partial(spatial_fwd_kernel, lines), grid=(frames...  36.4 us
    reshape x2, local copies, waits for them, and re-layouts, shards(): rows_of = lambda v: v.reshape(-1, D)  9.24 us

profile of v4, /device:TPU:0, one launch (start us, length us, event | category | flops | bytes accessed | tf_op | source)
XLA Modules:
  0.0 384.4 jit_solution(2002177271629444454)
XLA Ops:
  0.6 0.7 reduce.1
  1.4 0.7 reduce
  2.2 1.3 fusion.refs_2_
  3.5 1.4 slice.89.refs_9_
  4.9 1.4 slice_bitcast_fusion.1.refs_7_
  6.3 1.4 slice_bitcast_fusion.2
  7.7 1.5 slice.88.refs_8_
  9.3 1.5 slice_bitcast_fusion.refs_6_
  10.8 1.0 fusion.1
  13.3 39.8 %first_gather.1 = (bf16[8,208,768]{2,1,0:T(8,128)(2,1)}, f32[16,13,8,768]{3,2,1,0:T(8,128)}, f32[2,4,2,2,8,128]{5,4,3,2,1,0:T(8,128)}, bf16[2,4,2,2,48,1152]{5,4...) custom-call(bf16[1568,768]{1,0:T(8,128)(2,1)} %refs_0_.1, ...), custom_call_target="tpu_custom_call" | custom-call | tf_op jit(solution)/shard_map/first_gather/pallas_call | solution.py:742
  53.0 0.9 reshape.126
  54.2 0.7 reshape_reshape.6.hid_ref
  55.2 0.8 reshape.129.refs_3_.vec_ref.refs_8_
  55.9 36.4 %spatial_fwd.1 = (f32[16,13,8,768]{3,2,1,0:T(8,128)}, bf16[8,2,208,1152]{3,2,1,0:T(8,128)(2,1)}, bf16[8,2,208,384]{3,2,1,0:T(8,128)(2,1)}, bf16[8,6,416,208]{3,2...) custom-call(bf16[8,208,768]{2,1,0:T(8,128)(2,1)} %get-tuple-element., ...), custom_call_target="tpu_custom_call" | custom-call | tf_op jit(solution)/shard_map/spatial_fwd/pallas_call | solution.py:916
  92.4 43.0 %temporal_fwd.1 = (f32[16,13,8,768]{3,2,1,0:T(8,128)}, bf16[2,1792,1152]{2,1,0:T(8,128)(2,1)}, bf16[2,1792,384]{2,1,0:T(8,128)(2,1)}, bf16[6,3584,128]{2,1,0:T(8...) custom-call(f32[16,13,8,768]{3,2,1,0:T(8,128)} %get-tuple-element.75, ...), custom_call_target="tpu_custom_call" | custom-call | tf_op jit(solution)/shard_map/temporal_fwd/pallas_call | solution.py:1145
  135.3 70.8 %mlp_both.1 = (f32[1664,768]{1,0:T(8,128)}, f32[1664,768]{1,0:T(8,128)}, bf16[2,768,1152]{2,1,0:T(8,128)(2,1)}, bf16[2,768,384]{2,1,0:T(8,128)(2,1)}, bf16[2,768...) custom-call(f32[1664,768]{1,0:T(8,128)} %bitcast.89, ...), custom_call_target="tpu_custom_call" | custom-call | tf_op jit(solution)/shard_map/mlp_both/pallas_call | solution.py:1507
  206.1 52.1 %temporal_bwd.1 = (f32[8,26,8,768]{3,2,1,0:T(8,128)}, bf16[2,768,1152]{2,1,0:T(8,128)(2,1)}, bf16[2,768,384]{2,1,0:T(8,128)(2,1)}, f32[8,768]{1,0:T(8,128)}, f32...) custom-call(f32[16,13,8,768]{3,2,1,0:T(8,128)} %get-tuple-element.75, ...), custom_call_target="tpu_custom_call" | custom-call | tf_op jit(solution)/shard_map/temporal_bwd/pallas_call | solution.py:1311
  258.2 58.8 %spatial_bwd.1 = (f32[8,196,768]{2,1,0:T(8,128)}, bf16[2,768,1152]{2,1,0:T(8,128)(2,1)}, bf16[2,768,384]{2,1,0:T(8,128)(2,1)}, f32[8,768]{1,0:T(8,128)}, bf16[8,...) custom-call(bf16[8,208,768]{2,1,0:T(8,128)(2,1)} %get-tuple-element., ...), custom_call_target="tpu_custom_call" | custom-call | tf_op jit(solution)/shard_map/spatial_bwd/pallas_call | solution.py:1025
  317.1 4.1 %reshape.146 = bf16[1568,768]{1,0:T(8,128)(2,1)} reshape(bf16[8,196,768]{2,1,0:T(8,128)(2,1)} %get-tuple-element.110) | data formatting | bytes 4816896 | tf_op jit(solution)/shard_map/reshape | solution.py:1570
  321.2 0.9 fusion.2
  322.9 0.7 copy.56.refs_2_
  323.6 45.7 %last_reduce.1 = (f32[48,1152]{1,0:T(8,128)}, f32[1,48,384]{2,1,0:T(8,128)}, f32[8,128]{1,0:T(8,128)}, f32[48,1152]{1,0:T(8,128)}, f32[1,48,384]{2,1,0:T(8,128)}) custom-call(bf16[2,4,2,2,48,1152]{5,4,3,2,1,0:T(8,128)(2,1)} %bitcast.97, bf16[2,4,2,2,48,384]{5,4,3,2,1,0:T(8,128)(2,1)} %bitcast.105, f32[2,4,2,2,8,128]{5,4,3,2,1,0:T(8,128)} %copy.56.refs_2_, ...), custom_call_target="tpu_custom_call" | custom-call | tf_op jit(solution)/shard_map/last_reduce/pallas_call | solution.py:1387
  369.3 1.3 slice_bitcast_fusion.4
  370.5 0.8 slice.84
  371.3 0.7 slice.85
  372.6 0.7 reshape.156
  373.3 1.0 stack_reshape.6
  374.3 1.6 maximum_bitcast_fusion.3
  375.9 1.0 stack_reshape.7
  377.1 0.8 copy.54
  377.9 0.9 maximum_bitcast_fusion.1
  378.7 5.2 %reshape.147 = f32[1568,768]{1,0:T(8,128)} reshape(f32[8,196,768]{2,1,0:T(8,128)} %get-tuple-element.111) | data formatting | bytes 9633792 | tf_op jit(solution)/shard_map/reshape | solution.py:1570
  (41 shorter events, 3.7 us)
Async XLA Ops:
  317.0 4.1 %copy-start.6 = (f32[8,768]{1,0:T(8,128)S(1)}, f32[8,768]{1,0:T(8,128)}, u32[]{:S(2)}) copy-start(f32[8,768]{1,0:T(8,128)} %get-tuple-element.114) | copy-start | bytes 73732
  317.0 4.1 %copy-start.5 = (f32[8,768]{1,0:T(8,128)S(1)}, f32[8,768]{1,0:T(8,128)}, u32[]{:S(2)}) copy-start(f32[8,768]{1,0:T(8,128)} %get-tuple-element.115) | copy-start | bytes 73732
  317.1 5.1 %copy-start.4 = (f32[2,1,1536]{2,1,0:T(1,128)S(1)}, f32[2,1,1536]{2,1,0:T(1,128)}, u32[]{:S(2)}) copy-start(f32[2,1,1536]{2,1,0:T(1,128)} %get-tuple-element.117) | copy-start | bytes 36868
  323.6 54.3 %copy-start = (f32[48,1152]{1,0:T(8,128)S(1)}, f32[48,1152]{1,0:T(8,128)}, u32[]{:S(2)}) copy-start(f32[48,1152]{1,0:T(8,128)} %get-tuple-element.124) | copy-start | bytes 663556
  323.6 54.3 %copy-start.1 = (f32[48,1152]{1,0:T(8,128)S(1)}, f32[48,1152]{1,0:T(8,128)}, u32[]{:S(2)}) copy-start(f32[48,1152]{1,0:T(8,128)} %get-tuple-element.126) | copy-start | bytes 663556
  323.6 54.3 %copy-start.2 = (f32[1,48,384]{2,1,0:T(8,128)S(1)}, f32[1,48,384]{2,1,0:T(8,128)}, u32[]{:S(2)}) copy-start(f32[1,48,384]{2,1,0:T(8,128)} %get-tuple-element.125) | copy-start | bytes 221188
  323.6 54.3 %copy-start.3 = (f32[1,48,384]{2,1,0:T(8,128)S(1)}, f32[1,48,384]{2,1,0:T(8,128)}, u32[]{:S(2)}) copy-start(f32[1,48,384]{2,1,0:T(8,128)} %get-tuple-element.127) | copy-start | bytes 221188

commit v5 on v4

--- a/solution.py
+++ b/solution.py
@@ -347,6 +347,8 @@
 
 
 def add_blocks(u, v, dtype):
+    if u.dtype == v.dtype == dtype:
+        return u + v
     return (u.astype(F32) + v.astype(F32)).astype(dtype)
 
 
@@ -609,6 +611,9 @@
     )
 
 
+TILE = (24, 128)
+
+
 def padded_frames(rows, put):
     frames = rows.shape[0] // PATCHES
     half = frames // 2
@@ -620,17 +625,32 @@
 
 
 def first_kernel(lines, *refs):
-    (tok, cot, tile, q0, o0, q1, o1), (x_out, cot_b, full_tile, full_q, full_o, *results), (
-        col_q1, block_o1, col_tile, block_o0, tok_v, cot_v, frames_v, ex_send, ex_recv, ex_local, loads), scratch = take(
-        refs, 7, 7, 11, len(refs))
+    (tok, cot, gains, biases, hidden, qkv, outs), (x_out, cot_b, full_tile, full_q, full_o, *results), (
+        tile, q0, q1, col_q1, block_o1, col_tile, block_o0, tok_v, cot_v, frames_v, ex_send, ex_recv, ex_local, loads), scratch = take(
+        refs, 7, 7, 14, len(refs))
     place = Place(lines)
     t, z, y, x = place.t, place.z, place.y, place.x
     hops = lines - 1
     load_cot = pltpu.make_async_copy(cot, cot_v, loads.at[0])
     load_tok = pltpu.make_async_copy(tok, tok_v, loads.at[1])
+    part = qkv.shape[3]
+    load_qkv = [
+        pltpu.make_async_copy(qkv.at[s, k], own.at[:, pl.ds(part * k, part)], loads.at[2 + 3 * s + k])
+        for s, own in enumerate((q0, q1))
+        for k in range(3)
+    ]
+    for copy in load_qkv:
+        copy.start()
     load_cot.start()
     load_tok.start()
+    tile[...] = jnp.zeros_like(tile)
+    tile[0:10, 0 : biases.shape[1]] = biases[...]
+    tile[10:13, 0 : gains.shape[1]] = gains[...]
+    tile[16:17, 0 : hidden.shape[1]] = hidden[...]
+    o0, o1 = outs.at[0], outs.at[1]
     place.greet()
+    for copy in load_qkv:
+        copy.wait()
     pool = list(scratch)
 
     def sems():
@@ -730,18 +750,22 @@
     theirs.wait()
 
 
-def first_call(tokens, cot, tile, q0, o0, q1, o1, lines, collective_id):
+def first_call(tokens, cot, gains, biases, hidden, qkv, outs, lines, collective_id):
     rows, D = tokens.shape
     frames = rows // PATCHES
     groups = PAD // 16
     vmem = pl.BlockSpec(memory_space=pltpu.VMEM)
+    depth, part = qkv.shape[2:]
+    tile = struct(TILE, F32)
+    q0 = q1 = struct((depth, 3 * part), BF)
+    o0 = o1 = struct(outs.shape[1:], BF)
     col = lambda own: struct((lines,) + own.shape, own.dtype)
     block = lambda own: struct((2, 2) + own.shape, own.dtype)
     full = lambda own: struct(full_shape(lines, *own.shape), own.dtype)
     vmem_like = lambda s: pltpu.VMEM(s.shape, s.dtype)
     return pl.pallas_call(
         functools.partial(first_kernel, lines),
-        in_specs=[any_spec()] * 2 + [vmem] * 5,
+        in_specs=[any_spec()] * 2 + [vmem] * 3 + [any_spec(), vmem],
         out_specs=[vmem] + [any_spec()] * 4 + [vmem] * 2,
         out_shape=[
             struct((frames, PAD, D), BF),
@@ -753,6 +777,9 @@
             block(o1),
         ],
         scratch_shapes=[
+            vmem_like(tile),
+            vmem_like(q0),
+            vmem_like(q1),
             vmem_like(col(q1)),
             vmem_like(block(o1)),
             vmem_like(col(tile)),
@@ -763,13 +790,13 @@
             dma_sems(1),
             dma_sems(1),
             dma_sems(1),
-            dma_sems(2),
+            dma_sems(8),
         ]
         + LineGather.scratch(lines) * 4
         + PlaneGather.scratch() * (4 + 2 * (lines - 1)),
         name="first_gather",
         compiler_params=kernel_params(collective_id),
-    )(tokens, cot, tile, q0, o0, q1, o1)
+    )(tokens, cot, gains, biases, hidden, qkv, outs)
 
 
 def spatial_forward(x, w_ref, wo_ref, vec_ref, qkv_ref, mix_ref, p_ref, r_ref):
@@ -803,9 +830,9 @@
         s = spatial_forward(x_ref[0].astype(F32), w_ref, wo_ref, vec_ref, qkv_ref, mix_ref, p_ref, r_ref)
         s_ref[0] = s.reshape(s_ref.shape[1:])
         return
-    (x_ref, w_ref, wo_ref, vec_ref), (col_q1, block_o1, q2, o2, q3, o3), (s_b, qkv_ref, mix_ref, p_ref, r_ref), (
+    (x_ref, w_ref, wo_ref, vec_ref), (col_q1, block_o1, own2, own3), (s_b, qkv_ref, mix_ref, p_ref, r_ref), (
         full_q1, full_o1), results, landed, (slots, ex_send, ex_recv, ex_local), *parts = take(
-        refs, 4, 6, 5, 2, 4, 4, 4, 3, 3, 3, 3, 3, 3)
+        refs, 4, 4, 5, 2, 4, 4, 4, 3, 3, 3, 3, 3, 3)
     col_q2, col_q3, block_o2, block_o3 = landed
     place = Place(lines)
     t = place.t
@@ -813,6 +840,9 @@
     frames = pl.num_programs(0)
     groups = PAD // 16
     hops = lines - 1
+    wide = col_q2.shape[2]
+    q2, q3 = [own.at[:, pl.ds(0, wide)] for own in (own2, own3)]
+    o2, o3 = [own.at[:, pl.ds(wide, own.shape[1] - wide)] for own in (own2, own3)]
     q1 = PlaneGather(place, col_q1, lambda v, u: full_q1.at[t, :, v, u], parts[0])
     o1 = LineGather(place, block_o1, full_o1.at[t], parts[1], to_core=full_o1.at[t])
     l2 = LineGather(place, q2, col_q2, parts[2])
@@ -901,8 +931,8 @@
     ]
     args, scratch, lines, collective_id = [x, w, wo, vec], [], None, None
     if links is not None:
-        col_q1, block_o1, q2, o2, q3, o3, lines, collective_id = links
-        args += [col_q1, block_o1, q2, o2, q3, o3]
+        col_q1, block_o1, own2, own3, lines, collective_id = links
+        args += [col_q1, block_o1, own2, own3]
         in_specs += [whole_spec(v.shape) for v in args[4:]]
         out_specs[0] = any_spec()
         out_shape[0] = struct((2 * frames, groups, 8, D), F32)
@@ -925,6 +955,16 @@
     )(*args)
 
 
+SHARED = 4
+
+
+def place_frame(i, ref, rows):
+    for f in range(SHARED):
+        @pl.when(i % SHARED == f)
+        def _():
+            ref[PATCHES * f : PATCHES * (f + 1)] = rows
+
+
 def spatial_bwd_kernel(lines, *refs):
     linked = lines is not None
     ins, joins, outs, results, (gw_ref, go_ref), rest = take(
@@ -965,8 +1005,11 @@
         at_step(5, (l2, lines - 1), (l3, lines - 1))
         at_step(6, (q1, 3), *[(o1, k) for k in range(3, lines)])
         at_step(7, (o1, lines))
-        out = out_a[0].reshape(PAD, out_a.shape[3])
-        out_ref[0] = out[: out_ref.shape[1]].astype(BF)
+        place_frame(i, rest[-1], out_a[0].reshape(PAD, out_a.shape[3])[:PATCHES])
+
+        @pl.when(i % SHARED == SHARED - 1)
+        def _():
+            out_ref[...] = rest[-1][...].astype(BF)
 
     up = up_ref[0].reshape(PAD, up_ref.shape[3])
     gx = attn_back_common(
@@ -978,7 +1021,7 @@
         lambda pair, b: (p_ref[0, pair], r_ref[0, :, pair : pair + 1]),
         gw_ref, go_ref, gv_ref, cols, 1,
     )
-    gx_ref[0] = gx[: gx_ref.shape[1]]
+    place_frame(i, gx_ref, gx[:PATCHES])
 
     @pl.when(i == last)
     def _():
@@ -1002,10 +1045,10 @@
         whole_spec(wo.shape),
         whole_spec(vec.shape),
     ]
-    live_spec = pl.BlockSpec((1, PATCHES, D), lambda i: (i, 0, 0))
+    live_spec = pl.BlockSpec((SHARED * PATCHES, D), lambda i: (i // SHARED, 0))
     out_specs = [live_spec, whole_spec(w.shape), whole_spec(wo.shape), whole_spec((8, D))]
     out_shape = [
-        struct((frames, PATCHES, D), F32), struct(w.shape, BF), struct(wo.shape, BF), struct((8, D), F32)
+        struct((frames * PATCHES, D), F32), struct(w.shape, BF), struct(wo.shape, BF), struct((8, D), F32)
     ]
     args = [x, up, qkv, mix, p, r, w, wo, vec]
     scratch, lines, collective_id = [pltpu.VMEM(w.shape, F32), pltpu.VMEM(wo.shape, F32)], None, None
@@ -1019,9 +1062,10 @@
             struct((1,) + o_block, F32), struct((1,) + o_block, F32),
         ]
         out_specs += [live_spec] + [whole_spec(s.shape) for s in more]
-        out_shape += [struct((frames, PATCHES, D), BF)] + more
+        out_shape += [struct((frames * PATCHES, D), BF)] + more
         scratch += PlaneReduce.scratch(lines, q_block, BF) + LineReduce.scratch(lines, o_block, BF)
         scratch += LineSum.scratch(lines, q_block, BF) * 2 + PlaneSum.scratch(1, o_block, BF) * 2
+        scratch += [pltpu.VMEM((SHARED * PATCHES, D), F32)]
     return pl.pallas_call(
         functools.partial(spatial_bwd_kernel, lines),
         grid=(frames,),
@@ -1341,41 +1385,45 @@
     o1_plane = PlaneSum(place, block1, sum_o1, parts[8])
     o0_plane = PlaneSum(place, block0, sum_o0, parts[9])
     n = lines
+    o0.stage(0)
     qa.stage(0)
     qb.stage(0)
-    o0.stage(0)
     small.stage(0)
+    o1_plane.stage(0)
+    o0.stage(1)
+    qa.stage(1)
     q1_line.stage(0)
-    qa.stage(1)
     qb.stage(1)
-    o1_plane.stage(0)
     small.stage(1)
-    o0.stage(1)
-    q1_line.stage(1)
+    o0.stage(2)
     qa.stage(2)
     small.stage(2)
-    o0.stage(2)
-    for k in range(2, n - 1):
-        q1_line.stage(k)
+    o1_plane.stage(1)
+    q1_line.stage(1)
     qb.stage(2)
     qa.stage(3)
     qa_line.stage(0)
     small.stage(3)
     small_line.stage(0)
-    q1_line.stage(n - 1)
-    for k in range(3, n + 1):
+    o0.stage(3)
+    for k in range(2, n - 1):
+        q1_line.stage(k)
+    qb.stage(3)
+    qb_line.stage(0)
+    qa_line.stage(1)
+    small_line.stage(1)
+    for k in range(4, n + 1):
         o0.stage(k)
     o0_plane.stage(0)
-    o1_plane.stage(1)
-    qb.stage(3)
-    qb_line.stage(0)
-    for k in range(1, n):
+    qb_line.stage(1)
+    q1_line.stage(n - 1)
+    o1_plane.stage(2)
+    for k in range(2, n):
         qa_line.stage(k)
         small_line.stage(k)
+        if k == 2:
+            o0_plane.stage(1)
         qb_line.stage(k)
-        if k == 1:
-            o0_plane.stage(1)
-            o1_plane.stage(2)
     o0_plane.stage(2)
 
 
@@ -1544,20 +1592,9 @@
     chips = D // depth
     devices = 2 * chips
     share = D // devices
+    count = 13 * share + 2 * units // devices
     wide = 3 * cols
     down = mlp_out[0].T
-    owns = []
-    for s in range(2):
-        owns += [attn_qkv[0, s].reshape(depth, wide), attn_out[0, s].T]
-    owns += [mlp_in[0, :, :wide], mlp_in[0, :, wide:], down[:, :wide], down[:, wide:]]
-    small = jnp.concatenate(
-        [biases[0].reshape(-1), norm_gains[0].reshape(-1), hidden_bias[0].reshape(-1)]
-    )
-    count = small.shape[0]
-
-    def vectors(small):
-        vec = small[:, : 13 * share].reshape(devices, 13, share).transpose(1, 0, 2).reshape(13, D)
-        return vec, small[:, 13 * share :].reshape(2, units)
 
     def spread(gv_s, gv_t, gv_m, g_hidden):
         vec_grad = jnp.concatenate(
@@ -1571,14 +1608,16 @@
     if depth % 16 == 0 and chips % 4 == 0:
         lines = chips // 4
         cut = lambda g: g.reshape(full_shape(lines, depth, g.shape[2]))
-        tile = jnp.pad(small, (0, 1024 - count)).reshape(8, 128)
-        x, cot, full_tile, *w0, col_q1, block_o1 = first_call(tokens, cotangent, tile, *owns[:4], lines, 1)
-        vec, hidden = vectors(
-            full_tile.reshape(2, chips, 1024).transpose(1, 0, 2).reshape(devices, 1024)[:, :count]
+        x, cot, tiles, *w0, col_q1, block_o1 = first_call(
+            tokens, cotangent, norm_gains[0], biases[0], hidden_bias,
+            attn_qkv[0].transpose(0, 2, 1, 3), attn_out[0].transpose(0, 2, 1), lines, 1,
         )
+        tiles = tiles.reshape((2, chips) + TILE)
+        vec = tiles[:, :, :13, :share].transpose(2, 1, 0, 3).reshape(13, D)
+        hidden = tiles[:, :, 16, : 2 * units // devices].transpose(1, 0, 2).reshape(2, units)
         w0 = [flat(w) for w in w0]
         x1, *kept_s, q1, o1, col_q2, col_q3, block_o2, block_o3 = spatial_fwd(
-            x, *w0, vec, (col_q1, block_o1, *owns[4:], lines, 2)
+            x, *w0, vec, (col_q1, block_o1, mlp_in[0], down, lines, 2)
         )
         w1 = [flat(q1), flat(o1)]
         x2, *kept_t, q2, q3, o2, o3 = temporal_fwd(
@@ -1600,8 +1639,16 @@
         small_grad = small_grad.reshape(-1)[:count]
         go0, go1, go2, go3 = [g[0] for g in (go0, go1, go2, go3)]
     else:
+        owns = []
+        for s in range(2):
+            owns += [attn_qkv[0, s].reshape(depth, wide), attn_out[0, s].T]
+        owns += [mlp_in[0, :, :wide], mlp_in[0, :, wide:], down[:, :wide], down[:, wide:]]
+        small = jnp.concatenate(
+            [biases[0].reshape(-1), norm_gains[0].reshape(-1), hidden_bias[0].reshape(-1)]
+        )
         small = lax.all_gather(small.reshape(1, -1), everyone, axis=0, tiled=True)
-        vec, hidden = vectors(small)
+        vec = small[:, : 13 * share].reshape(devices, 13, share).transpose(1, 0, 2).reshape(13, D)
+        hidden = small[:, 13 * share :].reshape(2, units)
         weights = [flat(lax.all_gather(w, ("tensor", "dp"), axis=0, tiled=True).reshape(2, D, -1)) for w in owns]
         x = pad_frames(tokens)
         fold = lambda v: v.reshape(frames, PAD // 8, 8, D)
@@ -1613,6 +1660,7 @@
             rows_of(x2), rows_of(cot), *weights[4:], vec, hidden
         )
         output = swap_to_frames(out_b.reshape(x1.shape)).reshape(frames, PAD, D)[:, :PATCHES].astype(BF)
+        output = rows_of(output)
         up1, *grads1, gv_t = temporal_bwd(x1, up2.reshape(x1.shape), *kept_t, *weights[2:4], vec)
         up0, *grads0, gv_s = spatial_bwd(x, swap_to_frames(up1), *kept_s, *weights[0:2], vec)
         gq0, go0, gq1, go1, gq2, go2, gq3, go3 = [
@@ -1630,8 +1678,8 @@
     grad_gains = small_grad[10 * share : 13 * share].reshape(1, 3, share)
     grad_hidden = small_grad[13 * share :].reshape(1, -1)
     return (
-        rows_of(output),
-        rows_of(up0),
+        output,
+        up0,
         grad_qkv,
         grad_out,
         jnp.concatenate([gq2, go2], axis=1)[None],

time: 392 us -> 380 us (0.969)
  local copies, waits for them, and re-layouts: 31.1 us -> 21.3 us
    reshape x6 -> x1, local copies, waits for them, and re-layouts: 11.1 us -> 0.92 us  [shards(): vec = tiles[:, :, :13, :share].transpose(2, 1, 0, 3).reshape(13, D)]
    unnamed x17 -> x19, local copies, waits for them, and re-layouts: 2.14 us -> 7.18 us
where the time goes in v5:
time: 380 us; the launch traced here: 374 us
  Pallas kernels  346 us (91%)
  local copies, waits for them, and re-layouts  21.3 us (6%)
  other arithmetic  4.84 us (1%)
    pallas_call x1, Pallas kernels, mlp_both(): pl.pallas_call(mlp_kernel, grid=(rows // MLP_ROWS,), in_specs=[row_spec,...  70.7 us
    pallas_call x1, Pallas kernels, spatial_bwd(): pl.pallas_call(functools.partial(spatial_bwd_kernel, lines), grid=(frames...  61.1 us
    pallas_call x1, Pallas kernels, temporal_bwd(): pl.pallas_call(functools.partial(temporal_bwd_kernel, lines, groups), gri...  51.3 us
    pallas_call x1, Pallas kernels, last_call(): pl.pallas_call(functools.partial(last_kernel, lines), in_specs=[any_spec(...  42.8 us
    pallas_call x1, Pallas kernels, temporal_fwd(): pl.pallas_call(functools.partial(temporal_fwd_kernel, lines, groups), gri...  42.6 us
    pallas_call x1, Pallas kernels, first_call(): pl.pallas_call(functools.partial(first_kernel, lines), in_specs=[any_spec...  41.7 us
    pallas_call x1, Pallas kernels, spatial_fwd(): pl.pallas_call(functools.partial(spatial_fwd_kernel, lines), grid=(frames...  35.7 us

profile of v5, /device:TPU:0, one launch (start us, length us, event | category | flops | bytes accessed | tf_op | source)
XLA Modules:
  0.0 373.5 jit_solution(7156567361263843252)
XLA Ops:
  0.6 1.3 copy.50
  1.9 1.3 copy.49
  3.2 41.7 %first_gather.1 = (bf16[8,208,768]{2,1,0:T(8,128)(2,1)}, f32[16,13,8,768]{3,2,1,0:T(8,128)}, f32[2,4,2,2,24,128]{5,4,3,2,1,0:T(8,128)}, bf16[2,4,2,2,48,1152]{5,...) custom-call(bf16[1568,768]{1,0:T(8,128)(2,1)} %refs_0_.1, ...), custom_call_target="tpu_custom_call" | custom-call | tf_op jit(solution)/shard_map/first_gather/pallas_call | solution.py:766
  44.9 0.9 slice.53
  45.8 1.0 slice.52
  46.8 0.2 copy.47
  47.0 0.9 reshape.111.refs_3_.vec_ref.refs_8_
  47.9 0.7 reshape_reshape.6.hid_ref
  48.6 35.7 %spatial_fwd.1 = (f32[16,13,8,768]{3,2,1,0:T(8,128)}, bf16[8,2,208,1152]{3,2,1,0:T(8,128)(2,1)}, bf16[8,2,208,384]{3,2,1,0:T(8,128)(2,1)}, bf16[8,6,416,208]{3,2...) custom-call(bf16[8,208,768]{2,1,0:T(8,128)(2,1)} %get-tuple-element., ...), custom_call_target="tpu_custom_call" | custom-call | tf_op jit(solution)/shard_map/spatial_fwd/pallas_call | solution.py:946
  84.3 42.6 %temporal_fwd.1 = (f32[16,13,8,768]{3,2,1,0:T(8,128)}, bf16[2,1792,1152]{2,1,0:T(8,128)(2,1)}, bf16[2,1792,384]{2,1,0:T(8,128)(2,1)}, bf16[6,3584,128]{2,1,0:T(8...) custom-call(f32[16,13,8,768]{3,2,1,0:T(8,128)} %get-tuple-element.75, ...), custom_call_target="tpu_custom_call" | custom-call | tf_op jit(solution)/shard_map/temporal_fwd/pallas_call | solution.py:1189
  127.0 70.7 %mlp_both.1 = (f32[1664,768]{1,0:T(8,128)}, f32[1664,768]{1,0:T(8,128)}, bf16[2,768,1152]{2,1,0:T(8,128)(2,1)}, bf16[2,768,384]{2,1,0:T(8,128)(2,1)}, bf16[2,768...) custom-call(f32[1664,768]{1,0:T(8,128)} %bitcast.82, ...), custom_call_target="tpu_custom_call" | custom-call | tf_op jit(solution)/shard_map/mlp_both/pallas_call | solution.py:1555
  197.7 51.3 %temporal_bwd.1 = (f32[8,26,8,768]{3,2,1,0:T(8,128)}, bf16[2,768,1152]{2,1,0:T(8,128)(2,1)}, bf16[2,768,384]{2,1,0:T(8,128)(2,1)}, f32[8,768]{1,0:T(8,128)}, f32...) custom-call(f32[16,13,8,768]{3,2,1,0:T(8,128)} %get-tuple-element.75, ...), custom_call_target="tpu_custom_call" | custom-call | tf_op jit(solution)/shard_map/temporal_bwd/pallas_call | solution.py:1355
  249.1 61.1 %spatial_bwd.1 = (f32[1568,768]{1,0:T(8,128)}, bf16[2,768,1152]{2,1,0:T(8,128)(2,1)}, bf16[2,768,384]{2,1,0:T(8,128)(2,1)}, f32[8,768]{1,0:T(8,128)}, bf16[1568,...) custom-call(bf16[8,208,768]{2,1,0:T(8,128)(2,1)} %get-tuple-element., ...), custom_call_target="tpu_custom_call" | custom-call | tf_op jit(solution)/shard_map/spatial_bwd/pallas_call | solution.py:1069
  310.2 0.7 slice.46
  311.0 0.7 slice.42
  311.7 0.9 fusion
  312.8 0.2 reshape.130
  313.5 0.7 copy.38.refs_2_
  314.1 42.8 %last_reduce.1 = (f32[48,1152]{1,0:T(8,128)}, f32[1,48,384]{2,1,0:T(8,128)}, f32[8,128]{1,0:T(8,128)}, f32[48,1152]{1,0:T(8,128)}, f32[1,48,384]{2,1,0:T(8,128)}) custom-call(bf16[2,4,2,2,48,1152]{5,4,3,2,1,0:T(8,128)(2,1)} %bitcast.92, bf16[2,4,2,2,48,384]{5,4,3,2,1,0:T(8,128)(2,1)} %bitcast.100, f32[2,4,2,2,8,128]{5,4,3,2,1,0:T(8,128)} %copy.38.refs_2_, ...), custom_call_target="tpu_custom_call" | custom-call | tf_op jit(solution)/shard_map/last_reduce/pallas_call | solution.py:1435
  357.0 1.4 slice_bitcast_fusion
  358.4 0.8 slice.49
  359.1 0.7 slice.50
  359.8 0.6 reshape.139
  360.5 0.7 reshape.136
  361.1 1.0 stack_reshape.6
  362.2 1.6 maximum_bitcast_fusion.3
  363.8 1.7 stack_reshape.7
  365.5 1.2 maximum_bitcast_fusion
  366.7 0.8 copy.36
  367.5 1.9 maximum_bitcast_fusion.1
  369.4 1.4 copy.53
  370.8 2.2 copy.54
  (24 shorter events, 0.7 us)
Async XLA Ops:
  249.1 62.7 %copy-start.3 = (f32[8,768]{1,0:T(8,128)S(1)}, f32[8,768]{1,0:T(8,128)}, u32[]{:S(2)}) copy-start(f32[8,768]{1,0:T(8,128)} %get-tuple-element.115) | copy-start | bytes 73732
  249.1 63.6 %copy-start.2 = (f32[2,1,1536]{2,1,0:T(1,128)S(1)}, f32[2,1,1536]{2,1,0:T(1,128)}, u32[]{:S(2)}) copy-start(f32[2,1,1536]{2,1,0:T(1,128)} %get-tuple-element.117) | copy-start | bytes 36868
  314.1 53.4 %copy-start.1 = (f32[48,1152]{1,0:T(8,128)S(1)}, f32[48,1152]{1,0:T(8,128)}, u32[]{:S(2)}) copy-start(f32[48,1152]{1,0:T(8,128)} %get-tuple-element.124) | copy-start | bytes 663556
  314.1 56.7 %slice-start = ((s8[4816896]{0:T(1024)(128)(4,1)}), s8[622592]{0:T(1024)(128)(4,1)S(1)}, s32[]{:S(2)}) async-start(s8[4816896]{0:T(1024)(128)(4,1)} %bitcast.83), calls=%async_computation | async-start | bytes 1245184
  357.0 12.5 %copy-start = (bf16[1568,768]{1,0:T(8,128)(2,1)S(1)}, bf16[1568,768]{1,0:T(8,128)(2,1)}, u32[]{:S(2)}) copy-start(bf16[1568,768]{1,0:T(8,128)(2,1)} %get-tuple-element.170) | copy-start | bytes 7225348
  365.5 5.4 %slice-start.1 = ((s8[4816896]{0:T(1024)(128)(4,1)}), s8[4194304]{0:T(1024)(128)(4,1)S(1)}, s32[]{:S(2)}) async-start(s8[4816896]{0:T(1024)(128)(4,1)} %bitcast.83), calls=%async_computation.1 | async-start | bytes 8388608

commit v6 on v5

--- a/solution.py
+++ b/solution.py
@@ -614,14 +614,14 @@
 TILE = (24, 128)
 
 
-def padded_frames(rows, put):
-    frames = rows.shape[0] // PATCHES
+def padded_frame(rows, f, frames):
     half = frames // 2
-    zeros = jnp.zeros((PAD - PATCHES, rows.shape[1]), F32)
-    for part in range(2):
-        block = rows[half * PATCHES * part : half * PATCHES * (part + 1)].astype(F32)
-        for f in range(half):
-            put(half * part + f, jnp.concatenate([block[PATCHES * f : PATCHES * (f + 1)], zeros], axis=0))
+    start = half * PATCHES * (f // half)
+    inside = PATCHES * (f % half)
+    low = inside // 16 * 16
+    high = -(-(inside + PATCHES) // 16) * 16
+    block = rows[start + low : start + high].astype(F32)[inside - low : inside - low + PATCHES]
+    return jnp.concatenate([block, jnp.zeros((PAD - PATCHES, rows.shape[1]), F32)], axis=0)
 
 
 def first_kernel(lines, *refs):
@@ -686,14 +686,20 @@
     own_slab.stage(0)
     o0_plane.stage(0)
     tile_line.stage(0)
-    load_cot.wait()
     D = tok.shape[1]
     frames = x_out.shape[0]
-
-    def put_cot(f, rows):
-        frames_v[f] = rows.reshape(PAD // 8, 8, D)
-
-    padded_frames(cot_v, put_cot)
+    pieces = [("cot", f) for f in range(frames)] + [("tok", f) for f in range(frames)]
+
+    def work(count=1):
+        for kind, f in [pieces.pop(0) for _ in range(min(count, len(pieces)))]:
+            if f == 0:
+                (load_cot if kind == "cot" else load_tok).wait()
+            if kind == "cot":
+                frames_v[f] = padded_frame(cot_v, f, frames).reshape(PAD // 8, 8, D)
+            else:
+                x_out[f] = padded_frame(tok_v, f, frames).astype(BF)
+
+    work(5)
     own_slab.stage(1)
     q0_line.stage(1)
     pair(1, 0)
@@ -709,32 +715,32 @@
         frames_v.at[:, pl.ds(groups * (1 - t), groups)], cot_b.at[pl.ds(frames * t, frames)],
         (ex_send, ex_recv), 0, place.core,
     )
+    work(frames - 5)
     mine.start()
     theirs.start()
-    load_tok.wait()
-
-    def put_tok(f, rows):
-        x_out[f] = rows.astype(BF)
-
-    padded_frames(tok_v, put_tok)
     o0_plane.stage(2)
     o0_plane.stage(3)
     o0_line.stage(0)
     pair(1, 1)
     own_slab.stage(2)
+    work(2)
     for k in range(2, lines):
         q0_line.stage(k)
         pair(k, 0)
         tile_line.stage(k)
         q1_line.stage(k - 1)
+        work()
         pair(k, 1)
         pair(k - 1, 2)
+        work()
         o0_line.stage(k - 1)
     tile_plane.stage(0)
     o1_plane.stage(1)
+    work()
     tile_plane.stage(1)
     o1_plane.stage(2)
     pair(hops, 2)
+    work(frames)
     o0_line.stage(hops)
     tile_plane.stage(2)
     q1_line.stage(hops)
@@ -983,9 +989,10 @@
 
     if linked:
         out_a, gw1, go1, col2, col3, block2, block3 = joins
-        out_ref, col1, block1, sum_q2, sum_q3, sum_o2, sum_o3 = results
+        out_ref, sum_q1, sum_o1, sum_q2, sum_q3, sum_o2, sum_o3 = results
+        (col1, block1), rest = rest[:2], rest[2:]
         place = Place(lines)
-        parts = take(rest, PlaneReduce.n_scratch, LineReduce.n_scratch, 4, 4, 4, 4)
+        parts = take(rest, PlaneReduce.n_scratch, LineReduce.n_scratch, 4, 4, 4, 4, 4, 4)
         q1 = PlaneReduce(place, gw1, col1, parts[0])
         o1 = LineReduce(place, go1, block1.at[0], parts[1])
         l2 = LineSum(place, col2, sum_q2, parts[2])
@@ -997,14 +1004,16 @@
         def _():
             place.greet()
 
+        l1 = LineSum(place, col1, sum_q1, parts[6])
+        p1 = PlaneSum(place, block1, sum_o1, parts[7])
         at_step(0, (q1, 0), (o1, 0), (l2, 0), (l3, 0), (p2, 0), (p3, 0))
-        at_step(1, (q1, 1))
-        at_step(2, (o1, 1), (l2, 1), (l3, 1), (p2, 1), (p3, 1))
-        at_step(3, (p2, 2), (p3, 2))
-        at_step(4, (q1, 2), (o1, 2), *[(job, k) for k in range(2, lines - 1) for job in (l2, l3)])
-        at_step(5, (l2, lines - 1), (l3, lines - 1))
-        at_step(6, (q1, 3), *[(o1, k) for k in range(3, lines)])
-        at_step(7, (o1, lines))
+        at_step(1, (q1, 1), (o1, 1), (l2, 1), (l3, 1))
+        at_step(2, (p2, 1), (p3, 1), (o1, 2), *[(job, k) for k in range(2, lines - 1) for job in (l2, l3)])
+        at_step(3, (q1, 2), (p2, 2), (p3, 2), (l2, lines - 1), (l3, lines - 1), *[(o1, k) for k in range(3, lines)])
+        at_step(4, (q1, 3), (l1, 0), (o1, lines), (p1, 0))
+        at_step(5, (l1, 1), (p1, 1))
+        at_step(6, (p1, 2), *[(l1, k) for k in range(2, lines - 1)])
+        at_step(7, (l1, lines - 1))
         place_frame(i, rest[-1], out_a[0].reshape(PAD, out_a.shape[3])[:PATCHES])
 
         @pl.when(i % SHARED == SHARED - 1)
@@ -1058,13 +1067,15 @@
         q_block, o_block = gw1.shape[4:], go1.shape[4:]
         in_specs += [frame_spec] + [any_spec()] * 2 + [whole_spec(v.shape) for v in args[-4:]]
         more = [
-            struct(col2.shape, BF), struct(block2.shape, BF), struct(q_block, F32), struct(q_block, F32),
+            struct(q_block, F32), struct((1,) + o_block, F32), struct(q_block, F32), struct(q_block, F32),
             struct((1,) + o_block, F32), struct((1,) + o_block, F32),
         ]
         out_specs += [live_spec] + [whole_spec(s.shape) for s in more]
         out_shape += [struct((frames * PATCHES, D), BF)] + more
+        scratch += [pltpu.VMEM(col2.shape, BF), pltpu.VMEM(block2.shape, BF)]
         scratch += PlaneReduce.scratch(lines, q_block, BF) + LineReduce.scratch(lines, o_block, BF)
         scratch += LineSum.scratch(lines, q_block, BF) * 2 + PlaneSum.scratch(1, o_block, BF) * 2
+        scratch += LineSum.scratch(lines, q_block, BF) + PlaneSum.scratch(1, o_block, BF)
         scratch += [pltpu.VMEM((SHARED * PATCHES, D), F32)]
     return pl.pallas_call(
         functools.partial(spatial_bwd_kernel, lines),
@@ -1368,9 +1379,15 @@
 
 
 def last_kernel(lines, *refs):
-    (gq0, go0, tiles, col1, block1), (sum_q0, sum_o0, sum_tile, sum_q1, sum_o1), (
-        col_a, col_b, col_tile, block0), *parts = take(
-        refs, 5, 5, 4, 9, 9, 9, 9, 4, 4, 4, 4, 4, 4)
+    (gq0, go0, tiles, sum_q1, sum_o1), mlp_parts, (grad_qkv, grad_out), mlp_grads, (grad_bias, grad_gain, grad_hidden), (
+        sum_q0, sum_tile, col_a, col_b, col_tile, block0), *parts = take(
+        refs, 5, 4, 2, 2, 3, 6, 9, 9, 9, 9, 4, 4, 4, 4)
+    for n, grad in enumerate(mlp_grads):
+        first, second = mlp_parts[2 * n : 2 * n + 2]
+        grad[:, : first.shape[1]] = first[...]
+        grad[:, first.shape[1] :] = second[0]
+    sum_o0 = grad_out.at[pl.ds(0, 1)]
+    grad_out[1] = sum_o1[0]
     place = Place(lines)
     place.greet()
     width = sum_q0.shape[1]
@@ -1381,33 +1398,25 @@
     qa_line = LineSum(place, col_a, sum_q0.at[:, 0:LAST_CUT], parts[4])
     qb_line = LineSum(place, col_b, sum_q0.at[:, LAST_CUT:width], parts[5])
     small_line = LineSum(place, col_tile, sum_tile, parts[6])
-    q1_line = LineSum(place, col1, sum_q1, parts[7])
-    o1_plane = PlaneSum(place, block1, sum_o1, parts[8])
-    o0_plane = PlaneSum(place, block0, sum_o0, parts[9])
+    o0_plane = PlaneSum(place, block0, sum_o0, parts[7])
     n = lines
     o0.stage(0)
     qa.stage(0)
     qb.stage(0)
     small.stage(0)
-    o1_plane.stage(0)
     o0.stage(1)
     qa.stage(1)
-    q1_line.stage(0)
     qb.stage(1)
     small.stage(1)
     o0.stage(2)
     qa.stage(2)
     small.stage(2)
-    o1_plane.stage(1)
-    q1_line.stage(1)
     qb.stage(2)
     qa.stage(3)
     qa_line.stage(0)
     small.stage(3)
     small_line.stage(0)
     o0.stage(3)
-    for k in range(2, n - 1):
-        q1_line.stage(k)
     qb.stage(3)
     qb_line.stage(0)
     qa_line.stage(1)
@@ -1416,8 +1425,6 @@
         o0.stage(k)
     o0_plane.stage(0)
     qb_line.stage(1)
-    q1_line.stage(n - 1)
-    o1_plane.stage(2)
     for k in range(2, n):
         qa_line.stage(k)
         small_line.stage(k)
@@ -1425,22 +1432,32 @@
             o0_plane.stage(1)
         qb_line.stage(k)
     o0_plane.stage(2)
-
-
-def last_call(gq0, go0, tiles, col1, block1, lines, collective_id):
+    part = grad_qkv.shape[3]
+    for n, total in enumerate((sum_q0, sum_q1)):
+        for k in range(3):
+            grad_qkv[n, k] = total[:, part * k : part * (k + 1)]
+    grad_bias[...] = sum_tile[0:10, : grad_bias.shape[1]]
+    grad_gain[...] = sum_tile[10:13, : grad_gain.shape[1]]
+    grad_hidden[...] = sum_tile[16:17, : grad_hidden.shape[1]]
+
+
+def last_call(gq0, go0, tiles, sum_q1, sum_o1, mlp_parts, share, lines, collective_id):
     q_block, o_block, tile = gq0.shape[4:], go0.shape[4:], tiles.shape[4:]
     rows, width = q_block
     cut_a, cut_b = (rows, LAST_CUT), (rows, width - LAST_CUT)
+    whole_row = (rows, width + o_block[1])
     vmem = pl.BlockSpec(memory_space=pltpu.VMEM)
     return pl.pallas_call(
         functools.partial(last_kernel, lines),
-        in_specs=[any_spec()] * 3 + [vmem] * 2,
-        out_specs=[vmem] * 5,
+        in_specs=[any_spec()] * 3 + [vmem] * 6,
+        out_specs=[vmem] * 7,
         out_shape=[
-            struct(q_block, F32), struct((1,) + o_block, F32), struct(tile, F32), struct(q_block, F32),
-            struct((1,) + o_block, F32),
+            struct((2, 3, rows, width // 3), F32), struct((2,) + o_block, F32), struct(whole_row, F32),
+            struct(whole_row, F32), struct((10, share), F32), struct((3, share), F32), struct((1, 4 * share), F32),
         ],
         scratch_shapes=[
+            pltpu.VMEM(q_block, F32),
+            pltpu.VMEM(tile, F32),
             pltpu.VMEM((lines,) + cut_a, BF),
             pltpu.VMEM((lines,) + cut_b, BF),
             pltpu.VMEM((lines,) + tile, F32),
@@ -1453,11 +1470,10 @@
         + LineSum.scratch(lines, cut_a, BF)
         + LineSum.scratch(lines, cut_b, BF)
         + LineSum.scratch(lines, tile, F32)
-        + LineSum.scratch(lines, q_block, BF)
-        + PlaneSum.scratch(1, o_block, BF) * 2,
+        + PlaneSum.scratch(1, o_block, BF),
         name="last_reduce",
         compiler_params=kernel_params(collective_id),
-    )(gq0, go0, tiles, col1, block1)
+    )(gq0, go0, tiles, sum_q1, sum_o1, *mlp_parts)
 
 
 MLP_ROWS = 416
@@ -1592,7 +1608,6 @@
     chips = D // depth
     devices = 2 * chips
     share = D // devices
-    count = 13 * share + 2 * units // devices
     wide = 3 * cols
     down = mlp_out[0].T
 
@@ -1600,8 +1615,7 @@
         vec_grad = jnp.concatenate(
             [gv_s[0:4], gv_t[0:4], gv_m[0:1], gv_m[3:4], gv_s[4:5], gv_t[4:5], gv_m[4:5]]
         )
-        vec_grad = vec_grad.reshape(13, devices, share).transpose(1, 0, 2).reshape(devices, 13 * share)
-        return jnp.concatenate([vec_grad, g_hidden.reshape(devices, -1)], axis=1)
+        return vec_grad.reshape(13, devices, share).transpose(1, 0, 2), g_hidden.reshape(devices, -1)
 
     flat = lambda w: w.reshape(2, D, w.shape[-1])
     rows_of = lambda v: v.reshape(-1, D)
@@ -1630,14 +1644,19 @@
             x1, up2.reshape(x1.shape), *kept_t, *w1, vec,
             (out_b.reshape(x1.shape), cut(gq2), cut(gq3), cut(go2), cut(go3), lines, 4),
         )
-        up0, gq0, go0, gv_s, output, col1, block1, gq2, gq3, go2, go3 = spatial_bwd(
+        up0, gq0, go0, gv_s, output, gq1, go1, gq2, gq3, go2, go3 = spatial_bwd(
             x, up1, *kept_s, *w0, vec, (out_a, cut(gq1), cut(go1), col2, col3, block2, block3, lines, 5)
         )
-        tiles = jnp.pad(spread(gv_s, gv_t, gv_m, g_hidden), ((0, 0), (0, 1024 - count)))
-        tiles = tiles.reshape(chips, 2, 1024).transpose(1, 0, 2).reshape(full_shape(lines, 8, 128))
-        gq0, go0, small_grad, gq1, go1 = last_call(cut(gq0), cut(go0), tiles, col1, block1, lines, 6)
-        small_grad = small_grad.reshape(-1)[:count]
-        go0, go1, go2, go3 = [g[0] for g in (go0, go1, go2, go3)]
+        vec_grad, hidden_grad = spread(gv_s, gv_t, gv_m, g_hidden)
+        place = lambda v, rows: jnp.pad(v, ((0, 0), (0, rows - v.shape[1]), (0, TILE[1] - v.shape[2])))
+        tiles = jnp.concatenate([place(vec_grad, 16), place(hidden_grad[:, None], 8)], axis=1)
+        tiles = tiles.reshape((chips, 2) + TILE).swapaxes(0, 1).reshape(full_shape(lines, *TILE))
+        grad_qkv, grad_out, grad_in, grad_down, grad_biases, grad_gains, grad_hidden = last_call(
+            cut(gq0), cut(go0), tiles, gq1, go1, (gq2, go2, gq3, go3), share, lines, 6
+        )
+        grad_qkv = grad_qkv.transpose(0, 2, 1, 3)
+        grad_out = grad_out.transpose(0, 2, 1)
+        grad_down = grad_down.T
     else:
         owns = []
         for s in range(2):
@@ -1669,23 +1688,25 @@
             ).astype(F32)
             for g in grads0 + grads1 + mlp_grads
         ]
-        small_grad = lax.psum_scatter(
-            spread(gv_s, gv_t, gv_m, g_hidden), everyone, scatter_dimension=0, tiled=True
-        )[0]
-    grad_qkv = jnp.stack([gq0.reshape(depth, 3, cols), gq1.reshape(depth, 3, cols)])[None]
-    grad_out = jnp.stack([go0.T, go1.T])[None]
-    grad_biases = small_grad[: 10 * share].reshape(1, 10, share)
-    grad_gains = small_grad[10 * share : 13 * share].reshape(1, 3, share)
-    grad_hidden = small_grad[13 * share :].reshape(1, -1)
+        vec_grad, hidden_grad = spread(gv_s, gv_t, gv_m, g_hidden)
+        small_grad = jnp.concatenate([vec_grad.reshape(devices, 13 * share), hidden_grad], axis=1)
+        small_grad = lax.psum_scatter(small_grad, everyone, scatter_dimension=0, tiled=True)[0]
+        grad_qkv = jnp.stack([gq0.reshape(depth, 3, cols), gq1.reshape(depth, 3, cols)])
+        grad_out = jnp.stack([go0.T, go1.T])
+        grad_in = jnp.concatenate([gq2, go2], axis=1)
+        grad_down = jnp.concatenate([gq3, go3], axis=1).T
+        grad_biases = small_grad[: 10 * share].reshape(10, share)
+        grad_gains = small_grad[10 * share : 13 * share].reshape(3, share)
+        grad_hidden = small_grad[13 * share :].reshape(1, -1)
     return (
         output,
         up0,
-        grad_qkv,
-        grad_out,
-        jnp.concatenate([gq2, go2], axis=1)[None],
-        jnp.concatenate([gq3, go3], axis=1).T[None],
-        grad_gains,
-        grad_biases,
+        grad_qkv[None],
+        grad_out[None],
+        grad_in[None],
+        grad_down[None],
+        grad_gains[None],
+        grad_biases[None],
         grad_hidden,
     )
 

time: 380 us -> 377 us (level)
  other arithmetic: 4.84 us -> 0.07 us
    unnamed x19 -> x29, local copies, waits for them, and re-layouts: 7.18 us -> 15.1 us
    broadcast_in_dim x3 -> x0, other arithmetic: 4.71 us -> none  [the longest x1 1.87 us: shards(): jnp.concatenate([gq2, go2], axis=1)[None]]
where the time goes in v6:
time: 377 us; the launch traced here: 370 us
  Pallas kernels  346 us (92%)
  local copies, waits for them, and re-layouts  22.2 us (6%)
    pallas_call x1, Pallas kernels, mlp_both(): pl.pallas_call(mlp_kernel, grid=(rows // MLP_ROWS,), in_specs=[row_spec,...  70.8 us
    pallas_call x1, Pallas kernels, spatial_bwd(): pl.pallas_call(functools.partial(spatial_bwd_kernel, lines), grid=(frames...  63 us
    pallas_call x1, Pallas kernels, temporal_bwd(): pl.pallas_call(functools.partial(temporal_bwd_kernel, lines, groups), gri...  51.3 us
    pallas_call x1, Pallas kernels, temporal_fwd(): pl.pallas_call(functools.partial(temporal_fwd_kernel, lines, groups), gri...  42.7 us
    pallas_call x1, Pallas kernels, first_call(): pl.pallas_call(functools.partial(first_kernel, lines), in_specs=[any_spec...  41.8 us
    pallas_call x1, Pallas kernels, last_call(): pl.pallas_call(functools.partial(last_kernel, lines), in_specs=[any_spec(...  41.2 us
    pallas_call x1, Pallas kernels, spatial_fwd(): pl.pallas_call(functools.partial(spatial_fwd_kernel, lines), grid=(frames...  35.6 us
    unnamed x29, local copies, waits for them, and re-layouts  15.1 us

profile of v6, /device:TPU:0, one launch (start us, length us, event | category | flops | bytes accessed | tf_op | source)
XLA Modules:
  0.0 369.9 jit_solution(2921390730438254886)
XLA Ops:
  0.6 1.3 copy.39
  1.9 1.3 copy.38
  3.2 41.8 %first_gather.1 = (bf16[8,208,768]{2,1,0:T(8,128)(2,1)}, f32[16,13,8,768]{3,2,1,0:T(8,128)}, f32[2,4,2,2,24,128]{5,4,3,2,1,0:T(8,128)}, bf16[2,4,2,2,48,1152]{5,...) custom-call(bf16[1568,768]{1,0:T(8,128)(2,1)} %refs_0_.1, ...), custom_call_target="tpu_custom_call" | custom-call | tf_op jit(solution)/shard_map/first_gather/pallas_call | solution.py:772
  45.0 0.9 slice.37
  45.9 1.0 slice.36
  46.9 0.2 copy.36
  47.0 0.9 reshape.96.refs_3_.vec_ref.refs_8_
  48.0 0.7 reshape_reshape.3.hid_ref
  48.7 35.6 %spatial_fwd.1 = (f32[16,13,8,768]{3,2,1,0:T(8,128)}, bf16[8,2,208,1152]{3,2,1,0:T(8,128)(2,1)}, bf16[8,2,208,384]{3,2,1,0:T(8,128)(2,1)}, bf16[8,6,416,208]{3,2...) custom-call(bf16[8,208,768]{2,1,0:T(8,128)(2,1)} %get-tuple-element., ...), custom_call_target="tpu_custom_call" | custom-call | tf_op jit(solution)/shard_map/spatial_fwd/pallas_call | solution.py:952
  84.3 42.7 %temporal_fwd.1 = (f32[16,13,8,768]{3,2,1,0:T(8,128)}, bf16[2,1792,1152]{2,1,0:T(8,128)(2,1)}, bf16[2,1792,384]{2,1,0:T(8,128)(2,1)}, bf16[6,3584,128]{2,1,0:T(8...) custom-call(f32[16,13,8,768]{3,2,1,0:T(8,128)} %get-tuple-element.77, ...), custom_call_target="tpu_custom_call" | custom-call | tf_op jit(solution)/shard_map/temporal_fwd/pallas_call | solution.py:1200
  127.0 70.8 %mlp_both.1 = (f32[1664,768]{1,0:T(8,128)}, f32[1664,768]{1,0:T(8,128)}, bf16[2,768,1152]{2,1,0:T(8,128)(2,1)}, bf16[2,768,384]{2,1,0:T(8,128)(2,1)}, bf16[2,768...) custom-call(f32[1664,768]{1,0:T(8,128)} %bitcast.69, ...), custom_call_target="tpu_custom_call" | custom-call | tf_op jit(solution)/shard_map/mlp_both/pallas_call | solution.py:1571
  197.8 51.3 %temporal_bwd.1 = (f32[8,26,8,768]{3,2,1,0:T(8,128)}, bf16[2,768,1152]{2,1,0:T(8,128)(2,1)}, bf16[2,768,384]{2,1,0:T(8,128)(2,1)}, f32[8,768]{1,0:T(8,128)}, f32...) custom-call(f32[16,13,8,768]{3,2,1,0:T(8,128)} %get-tuple-element.77, ...), custom_call_target="tpu_custom_call" | custom-call | tf_op jit(solution)/shard_map/temporal_bwd/pallas_call | solution.py:1366
  249.1 0.0 copy-start.5
  249.1 63.0 %spatial_bwd.1 = (f32[1568,768]{1,0:T(8,128)}, bf16[2,768,1152]{2,1,0:T(8,128)(2,1)}, bf16[2,768,384]{2,1,0:T(8,128)(2,1)}, f32[8,768]{1,0:T(8,128)}, bf16[1568,...) custom-call(bf16[8,208,768]{2,1,0:T(8,128)(2,1)} %get-tuple-element., ...), custom_call_target="tpu_custom_call" | custom-call | tf_op jit(solution)/shard_map/spatial_bwd/pallas_call | solution.py:1080
  312.2 0.7 slice.33
  312.9 0.7 slice.29
  313.7 0.9 fusion
  314.5 0.1 concatenate.6
  314.6 0.1 broadcast_in_dim_reshape_reshape.3
  314.7 0.2 reshape.115
  314.9 0.2 copy.24
  315.2 0.8 copy.25
  315.9 41.2 %last_reduce.1 = (f32[2,3,48,384]{3,2,1,0:T(8,128)}, f32[2,48,384]{2,1,0:T(8,128)}, f32[48,1536]{1,0:T(8,128)}, f32[48,1536]{1,0:T(8,128)}, f32[10,24]{1,0:T(8,128)}, /*index=5*/f32[3,24]{1,0:T(4,128)}, f32[1,96]{1,0:T(1,128)}) custom-call(bf16[2,4,2,2,48,1152]{5,4,3,2,1,0:T(8,128)(2,1)} %bitcast.77, bf16[2,4,2,2,48,384]{5,4,3,2,1,0:T(8,128)(2,1)} %bitcast.87, ...), custom_call_target="tpu_custom_call" | custom-call | tf_op jit(solution)/shard_map/last_reduce/pallas_call | solution.py:1450
  357.1 1.2 copy.26
  358.3 1.3 copy.27
  359.6 1.4 copy.47
  361.1 5.0 %copy.48 = f32[1568,768]{1,0:T(8,128)} copy(f32[1568,768]{1,0:T(8,128)} %get-tuple-element.164) | data formatting | bytes 9633792
  366.1 0.8 copy.49
  366.8 0.7 copy.50
  367.5 0.7 copy.51
  368.2 0.7 copy.52
  368.9 0.5 copy.53
  (20 shorter events, 0.1 us)
Async XLA Ops:
  249.1 64.5 %copy-start.6 = (f32[8,768]{1,0:T(8,128)S(1)}, f32[8,768]{1,0:T(8,128)}, u32[]{:S(2)}) copy-start(f32[8,768]{1,0:T(8,128)} %get-tuple-element.117) | copy-start | bytes 73732
  249.1 65.5 %copy-start.5 = (f32[2,1,1536]{2,1,0:T(1,128)S(1)}, f32[2,1,1536]{2,1,0:T(1,128)}, u32[]{:S(2)}) copy-start(f32[2,1,1536]{2,1,0:T(1,128)} %get-tuple-element.119) | copy-start | bytes 36868
  315.2 44.5 %copy-start = (bf16[1568,768]{1,0:T(8,128)(2,1)S(1)}, bf16[1568,768]{1,0:T(8,128)(2,1)}, u32[]{:S(2)}) copy-start(bf16[1568,768]{1,0:T(8,128)(2,1)} %get-tuple-element.163) | copy-start | bytes 7225348
  361.1 5.0 %copy-start.1 = (f32[2,3,48,384]{3,2,1,0:T(8,128)S(1)}, f32[2,3,48,384]{3,2,1,0:T(8,128)}, u32[]{:S(2)}) copy-start(f32[2,3,48,384]{3,2,1,0:T(8,128)} %get-tuple-element.126) | copy-start | bytes 1327108
  361.1 5.8 %copy-start.4 = (f32[2,48,384]{2,1,0:T(8,128)S(1)}, f32[2,48,384]{2,1,0:T(8,128)}, u32[]{:S(2)}) copy-start(f32[2,48,384]{2,1,0:T(8,128)} %get-tuple-element.127) | copy-start | bytes 442372
  361.1 6.4 %copy-start.3 = (f32[48,1536]{1,0:T(8,128)S(1)}, f32[48,1536]{1,0:T(8,128)}, u32[]{:S(2)}) copy-start(f32[48,1536]{1,0:T(8,128)} %get-tuple-element.128) | copy-start | bytes 884740
  361.1 7.1 %copy-start.2 = (f32[48,1536]{1,0:T(8,128)S(1)}, f32[48,1536]{1,0:T(8,128)}, u32[]{:S(2)}) copy-start(f32[48,1536]{1,0:T(8,128)} %get-tuple-element.129) | copy-start | bytes 884740
  361.1 7.9 %copy-start.7 = (f32[1,96]{1,0:T(1,128)S(1)}, f32[1,96]{1,0:T(1,128)}, u32[]{:S(2)}) copy-start(f32[1,96]{1,0:T(1,128)} %get-tuple-element.171) | copy-start | bytes 1156

commit v7 on v6

--- a/solution.py
+++ b/solution.py
@@ -1150,8 +1150,7 @@
         at_step(0, (q2, 0), (o2, 0), (o3, 0))
         at_step(2, (q2, 1), (q3, 0))
         at_step(3, (o2, 1), (o3, 1))
-        at_step(5, *[(job, k) for k in range(2, hops) for job in (o2, o3)])
-        at_step(6, (q3, 1))
+        at_step(5, (q3, 1), *[(job, k) for k in range(2, hops) for job in (o2, o3)])
     x = group_rows(x_ref[...], lambda b: STEP_GROUPS * i + b < groups)
     s = temporal_forward(x, w_ref, wo_ref, vec_ref, qkv_ref, mix_ref, p_ref, r_ref)
     for b in range(STEP_GROUPS):
@@ -1375,7 +1374,7 @@
     )(*args)
 
 
-LAST_CUT = 640
+LAST_CUT = 768
 
 
 def last_kernel(lines, *refs):

time: 377 us -> 375 us (level)
  no operation moved by 1% of the time
where the time goes in v7:
time: 375 us; the launch traced here: 368 us
  Pallas kernels  345 us (92%)
  local copies, waits for them, and re-layouts  22.2 us (6%)
    pallas_call x1, Pallas kernels, mlp_both(): pl.pallas_call(mlp_kernel, grid=(rows // MLP_ROWS,), in_specs=[row_spec,...  70.8 us
    pallas_call x1, Pallas kernels, spatial_bwd(): pl.pallas_call(functools.partial(spatial_bwd_kernel, lines), grid=(frames...  63.2 us
    pallas_call x1, Pallas kernels, temporal_bwd(): pl.pallas_call(functools.partial(temporal_bwd_kernel, lines, groups), gri...  51.4 us
    pallas_call x1, Pallas kernels, first_call(): pl.pallas_call(functools.partial(first_kernel, lines), in_specs=[any_spec...  41.8 us
    pallas_call x1, Pallas kernels, temporal_fwd(): pl.pallas_call(functools.partial(temporal_fwd_kernel, lines, groups), gri...  41.2 us
    pallas_call x1, Pallas kernels, last_call(): pl.pallas_call(functools.partial(last_kernel, lines), in_specs=[any_spec(...  40.9 us
    pallas_call x1, Pallas kernels, spatial_fwd(): pl.pallas_call(functools.partial(spatial_fwd_kernel, lines), grid=(frames...  35.6 us
    unnamed x29, local copies, waits for them, and re-layouts  15.1 us

profile of v7, /device:TPU:0, one launch (start us, length us, event | category | flops | bytes accessed | tf_op | source)
XLA Modules:
  0.0 368.4 jit_solution(6042223589735596870)
XLA Ops:
  0.6 1.3 copy.39
  1.9 1.3 copy.38
  3.2 41.8 %first_gather.1 = (bf16[8,208,768]{2,1,0:T(8,128)(2,1)}, f32[16,13,8,768]{3,2,1,0:T(8,128)}, f32[2,4,2,2,24,128]{5,4,3,2,1,0:T(8,128)}, bf16[2,4,2,2,48,1152]{5,...) custom-call(bf16[1568,768]{1,0:T(8,128)(2,1)} %refs_0_.1, ...), custom_call_target="tpu_custom_call" | custom-call | tf_op jit(solution)/shard_map/first_gather/pallas_call | solution.py:772
  45.0 0.9 slice.37
  45.9 1.0 slice.36
  46.9 0.2 copy.36
  47.0 0.9 reshape.96.refs_3_.vec_ref.refs_8_
  48.0 0.7 reshape_reshape.3.hid_ref
  48.7 35.6 %spatial_fwd.1 = (f32[16,13,8,768]{3,2,1,0:T(8,128)}, bf16[8,2,208,1152]{3,2,1,0:T(8,128)(2,1)}, bf16[8,2,208,384]{3,2,1,0:T(8,128)(2,1)}, bf16[8,6,416,208]{3,2...) custom-call(bf16[8,208,768]{2,1,0:T(8,128)(2,1)} %get-tuple-element., ...), custom_call_target="tpu_custom_call" | custom-call | tf_op jit(solution)/shard_map/spatial_fwd/pallas_call | solution.py:952
  84.3 41.2 %temporal_fwd.1 = (f32[16,13,8,768]{3,2,1,0:T(8,128)}, bf16[2,1792,1152]{2,1,0:T(8,128)(2,1)}, bf16[2,1792,384]{2,1,0:T(8,128)(2,1)}, bf16[6,3584,128]{2,1,0:T(8...) custom-call(f32[16,13,8,768]{3,2,1,0:T(8,128)} %get-tuple-element.77, ...), custom_call_target="tpu_custom_call" | custom-call | tf_op jit(solution)/shard_map/temporal_fwd/pallas_call | solution.py:1199
  125.5 70.8 %mlp_both.1 = (f32[1664,768]{1,0:T(8,128)}, f32[1664,768]{1,0:T(8,128)}, bf16[2,768,1152]{2,1,0:T(8,128)(2,1)}, bf16[2,768,384]{2,1,0:T(8,128)(2,1)}, bf16[2,768...) custom-call(f32[1664,768]{1,0:T(8,128)} %bitcast.69, ...), custom_call_target="tpu_custom_call" | custom-call | tf_op jit(solution)/shard_map/mlp_both/pallas_call | solution.py:1570
  196.3 51.4 %temporal_bwd.1 = (f32[8,26,8,768]{3,2,1,0:T(8,128)}, bf16[2,768,1152]{2,1,0:T(8,128)(2,1)}, bf16[2,768,384]{2,1,0:T(8,128)(2,1)}, f32[8,768]{1,0:T(8,128)}, f32...) custom-call(f32[16,13,8,768]{3,2,1,0:T(8,128)} %get-tuple-element.77, ...), custom_call_target="tpu_custom_call" | custom-call | tf_op jit(solution)/shard_map/temporal_bwd/pallas_call | solution.py:1365
  247.6 0.0 copy-start.5
  247.7 63.2 %spatial_bwd.1 = (f32[1568,768]{1,0:T(8,128)}, bf16[2,768,1152]{2,1,0:T(8,128)(2,1)}, bf16[2,768,384]{2,1,0:T(8,128)(2,1)}, f32[8,768]{1,0:T(8,128)}, bf16[1568,...) custom-call(bf16[8,208,768]{2,1,0:T(8,128)(2,1)} %get-tuple-element., ...), custom_call_target="tpu_custom_call" | custom-call | tf_op jit(solution)/shard_map/spatial_bwd/pallas_call | solution.py:1080
  310.9 0.7 slice.33
  311.6 0.7 slice.29
  312.4 0.9 fusion
  313.3 0.1 concatenate.6
  313.4 0.1 broadcast_in_dim_reshape_reshape.3
  313.5 0.2 reshape.115
  313.7 0.2 copy.24
  313.9 0.8 copy.25
  314.7 40.9 %last_reduce.1 = (f32[2,3,48,384]{3,2,1,0:T(8,128)}, f32[2,48,384]{2,1,0:T(8,128)}, f32[48,1536]{1,0:T(8,128)}, f32[48,1536]{1,0:T(8,128)}, f32[10,24]{1,0:T(8,128)}, /*index=5*/f32[3,24]{1,0:T(4,128)}, f32[1,96]{1,0:T(1,128)}) custom-call(bf16[2,4,2,2,48,1152]{5,4,3,2,1,0:T(8,128)(2,1)} %bitcast.77, bf16[2,4,2,2,48,384]{5,4,3,2,1,0:T(8,128)(2,1)} %bitcast.87, ...), custom_call_target="tpu_custom_call" | custom-call | tf_op jit(solution)/shard_map/last_reduce/pallas_call | solution.py:1449
  355.6 1.2 copy.26
  356.8 1.3 copy.27
  358.1 1.4 copy.47
  359.6 5.0 %copy.48 = f32[1568,768]{1,0:T(8,128)} copy(f32[1568,768]{1,0:T(8,128)} %get-tuple-element.164) | data formatting | bytes 9633792
  364.6 0.8 copy.49
  365.3 0.7 copy.50
  366.0 0.7 copy.51
  366.7 0.7 copy.52
  367.4 0.5 copy.53
  (20 shorter events, 0.1 us)
Async XLA Ops:
  247.6 64.8 %copy-start.6 = (f32[8,768]{1,0:T(8,128)S(1)}, f32[8,768]{1,0:T(8,128)}, u32[]{:S(2)}) copy-start(f32[8,768]{1,0:T(8,128)} %get-tuple-element.117) | copy-start | bytes 73732
  247.6 65.7 %copy-start.5 = (f32[2,1,1536]{2,1,0:T(1,128)S(1)}, f32[2,1,1536]{2,1,0:T(1,128)}, u32[]{:S(2)}) copy-start(f32[2,1,1536]{2,1,0:T(1,128)} %get-tuple-element.119) | copy-start | bytes 36868
  313.9 44.2 %copy-start = (bf16[1568,768]{1,0:T(8,128)(2,1)S(1)}, bf16[1568,768]{1,0:T(8,128)(2,1)}, u32[]{:S(2)}) copy-start(bf16[1568,768]{1,0:T(8,128)(2,1)} %get-tuple-element.163) | copy-start | bytes 7225348
  359.5 5.0 %copy-start.1 = (f32[2,3,48,384]{3,2,1,0:T(8,128)S(1)}, f32[2,3,48,384]{3,2,1,0:T(8,128)}, u32[]{:S(2)}) copy-start(f32[2,3,48,384]{3,2,1,0:T(8,128)} %get-tuple-element.126) | copy-start | bytes 1327108
  359.6 5.8 %copy-start.4 = (f32[2,48,384]{2,1,0:T(8,128)S(1)}, f32[2,48,384]{2,1,0:T(8,128)}, u32[]{:S(2)}) copy-start(f32[2,48,384]{2,1,0:T(8,128)} %get-tuple-element.127) | copy-start | bytes 442372
  359.6 6.4 %copy-start.3 = (f32[48,1536]{1,0:T(8,128)S(1)}, f32[48,1536]{1,0:T(8,128)}, u32[]{:S(2)}) copy-start(f32[48,1536]{1,0:T(8,128)} %get-tuple-element.128) | copy-start | bytes 884740
  359.6 7.1 %copy-start.2 = (f32[48,1536]{1,0:T(8,128)S(1)}, f32[48,1536]{1,0:T(8,128)}, u32[]{:S(2)}) copy-start(f32[48,1536]{1,0:T(8,128)} %get-tuple-element.129) | copy-start | bytes 884740
  359.6 7.9 %copy-start.7 = (f32[1,96]{1,0:T(1,128)S(1)}, f32[1,96]{1,0:T(1,128)}, u32[]{:S(2)}) copy-start(f32[1,96]{1,0:T(1,128)} %get-tuple-element.171) | copy-start | bytes 1156

commit v8 on v7

--- a/solution.py
+++ b/solution.py
@@ -862,10 +862,11 @@
 
     at_step(0, (q1, 0), (o1, 0), (l2, 0), (l3, 0), (p2, 0), (p3, 0))
     at_step(2, (p2, 1), (p3, 1))
-    at_step(3, (q1, 1), (o1, 1), (l2, 1), (l3, 1))
-    at_step(5, (p2, 2), (p2, 3), (p3, 2), (p3, 3))
-    at_step(6, *[(job, k) for k in range(2, hops) for job in (o1, l2, l3)])
-    at_step(7, (q1, 2))
+    at_step(3, (q1, 1), (o1, 1))
+    at_step(4, (l2, 1), (l3, 1))
+    at_step(5, *[(o1, k) for k in range(2, hops)], (p2, 2), (p2, 3), (p3, 2), (p3, 3))
+    at_step(6, *[(job, k) for k in range(2, hops) for job in (l2, l3)])
+    at_step(7, (o1, hops), (q1, 2))
 
     def here(f):
         return pltpu.make_async_copy(
@@ -893,7 +894,6 @@
 
     @pl.when(i == frames - 1)
     def _():
-        o1.stage(hops)
         l2.stage(hops)
         l3.stage(hops)
         q1.stage(3)

time: 375 us -> 375 us (level)
  no operation moved by 1% of the time
where the time goes in v8:
time: 375 us; the launch traced here: 368 us
  Pallas kernels  345 us (92%)
  local copies, waits for them, and re-layouts  22.2 us (6%)
    pallas_call x1, Pallas kernels, mlp_both(): pl.pallas_call(mlp_kernel, grid=(rows // MLP_ROWS,), in_specs=[row_spec,...  70.8 us
    pallas_call x1, Pallas kernels, spatial_bwd(): pl.pallas_call(functools.partial(spatial_bwd_kernel, lines), grid=(frames...  63.4 us
    pallas_call x1, Pallas kernels, temporal_bwd(): pl.pallas_call(functools.partial(temporal_bwd_kernel, lines, groups), gri...  52.1 us
    pallas_call x1, Pallas kernels, first_call(): pl.pallas_call(functools.partial(first_kernel, lines), in_specs=[any_spec...  41.8 us
    pallas_call x1, Pallas kernels, temporal_fwd(): pl.pallas_call(functools.partial(temporal_fwd_kernel, lines, groups), gri...  40.8 us
    pallas_call x1, Pallas kernels, last_call(): pl.pallas_call(functools.partial(last_kernel, lines), in_specs=[any_spec(...  40.7 us
    pallas_call x1, Pallas kernels, spatial_fwd(): pl.pallas_call(functools.partial(spatial_fwd_kernel, lines), grid=(frames...  35.1 us
    unnamed x29, local copies, waits for them, and re-layouts  15.1 us

profile of v8, /device:TPU:0, one launch (start us, length us, event | category | flops | bytes accessed | tf_op | source)
XLA Modules:
  0.0 368.2 jit_solution(17721268850892911281)
XLA Ops:
  0.6 1.3 copy.39
  1.9 1.3 copy.38
  3.2 41.8 %first_gather.1 = (bf16[8,208,768]{2,1,0:T(8,128)(2,1)}, f32[16,13,8,768]{3,2,1,0:T(8,128)}, f32[2,4,2,2,24,128]{5,4,3,2,1,0:T(8,128)}, bf16[2,4,2,2,48,1152]{5,...) custom-call(bf16[1568,768]{1,0:T(8,128)(2,1)} %refs_0_.1, ...), custom_call_target="tpu_custom_call" | custom-call | tf_op jit(solution)/shard_map/first_gather/pallas_call | solution.py:772
  45.0 0.9 slice.37
  45.9 1.0 slice.36
  46.9 0.2 copy.36
  47.0 0.9 reshape.96.refs_3_.vec_ref.refs_8_
  48.0 0.7 reshape_reshape.3.hid_ref
  48.7 35.1 %spatial_fwd.1 = (f32[16,13,8,768]{3,2,1,0:T(8,128)}, bf16[8,2,208,1152]{3,2,1,0:T(8,128)(2,1)}, bf16[8,2,208,384]{3,2,1,0:T(8,128)(2,1)}, bf16[8,6,416,208]{3,2...) custom-call(bf16[8,208,768]{2,1,0:T(8,128)(2,1)} %get-tuple-element., ...), custom_call_target="tpu_custom_call" | custom-call | tf_op jit(solution)/shard_map/spatial_fwd/pallas_call | solution.py:952
  83.8 40.8 %temporal_fwd.1 = (f32[16,13,8,768]{3,2,1,0:T(8,128)}, bf16[2,1792,1152]{2,1,0:T(8,128)(2,1)}, bf16[2,1792,384]{2,1,0:T(8,128)(2,1)}, bf16[6,3584,128]{2,1,0:T(8...) custom-call(f32[16,13,8,768]{3,2,1,0:T(8,128)} %get-tuple-element.77, ...), custom_call_target="tpu_custom_call" | custom-call | tf_op jit(solution)/shard_map/temporal_fwd/pallas_call | solution.py:1199
  124.6 70.8 %mlp_both.1 = (f32[1664,768]{1,0:T(8,128)}, f32[1664,768]{1,0:T(8,128)}, bf16[2,768,1152]{2,1,0:T(8,128)(2,1)}, bf16[2,768,384]{2,1,0:T(8,128)(2,1)}, bf16[2,768...) custom-call(f32[1664,768]{1,0:T(8,128)} %bitcast.69, ...), custom_call_target="tpu_custom_call" | custom-call | tf_op jit(solution)/shard_map/mlp_both/pallas_call | solution.py:1570
  195.4 52.1 %temporal_bwd.1 = (f32[8,26,8,768]{3,2,1,0:T(8,128)}, bf16[2,768,1152]{2,1,0:T(8,128)(2,1)}, bf16[2,768,384]{2,1,0:T(8,128)(2,1)}, f32[8,768]{1,0:T(8,128)}, f32...) custom-call(f32[16,13,8,768]{3,2,1,0:T(8,128)} %get-tuple-element.77, ...), custom_call_target="tpu_custom_call" | custom-call | tf_op jit(solution)/shard_map/temporal_bwd/pallas_call | solution.py:1365
  247.5 0.0 copy-start.5
  247.5 63.4 %spatial_bwd.1 = (f32[1568,768]{1,0:T(8,128)}, bf16[2,768,1152]{2,1,0:T(8,128)(2,1)}, bf16[2,768,384]{2,1,0:T(8,128)(2,1)}, f32[8,768]{1,0:T(8,128)}, bf16[1568,...) custom-call(bf16[8,208,768]{2,1,0:T(8,128)(2,1)} %get-tuple-element., ...), custom_call_target="tpu_custom_call" | custom-call | tf_op jit(solution)/shard_map/spatial_bwd/pallas_call | solution.py:1080
  310.9 0.7 slice.33
  311.6 0.7 slice.29
  312.4 0.9 fusion
  313.2 0.1 concatenate.6
  313.4 0.1 broadcast_in_dim_reshape_reshape.3
  313.4 0.2 reshape.115
  313.6 0.2 copy.24
  313.9 0.8 copy.25
  314.7 40.7 %last_reduce.1 = (f32[2,3,48,384]{3,2,1,0:T(8,128)}, f32[2,48,384]{2,1,0:T(8,128)}, f32[48,1536]{1,0:T(8,128)}, f32[48,1536]{1,0:T(8,128)}, f32[10,24]{1,0:T(8,128)}, /*index=5*/f32[3,24]{1,0:T(4,128)}, f32[1,96]{1,0:T(1,128)}) custom-call(bf16[2,4,2,2,48,1152]{5,4,3,2,1,0:T(8,128)(2,1)} %bitcast.77, bf16[2,4,2,2,48,384]{5,4,3,2,1,0:T(8,128)(2,1)} %bitcast.87, ...), custom_call_target="tpu_custom_call" | custom-call | tf_op jit(solution)/shard_map/last_reduce/pallas_call | solution.py:1449
  355.4 1.2 copy.26
  356.6 1.3 copy.27
  357.9 1.4 copy.47
  359.3 5.0 %copy.48 = f32[1568,768]{1,0:T(8,128)} copy(f32[1568,768]{1,0:T(8,128)} %get-tuple-element.164) | data formatting | bytes 9633792
  364.3 0.8 copy.49
  365.1 0.7 copy.50
  365.8 0.7 copy.51
  366.5 0.7 copy.52
  367.2 0.5 copy.53
  (20 shorter events, 0.1 us)
Async XLA Ops:
  247.5 64.9 %copy-start.6 = (f32[8,768]{1,0:T(8,128)S(1)}, f32[8,768]{1,0:T(8,128)}, u32[]{:S(2)}) copy-start(f32[8,768]{1,0:T(8,128)} %get-tuple-element.117) | copy-start | bytes 73732
  247.5 65.8 %copy-start.5 = (f32[2,1,1536]{2,1,0:T(1,128)S(1)}, f32[2,1,1536]{2,1,0:T(1,128)}, u32[]{:S(2)}) copy-start(f32[2,1,1536]{2,1,0:T(1,128)} %get-tuple-element.119) | copy-start | bytes 36868
  313.9 44.0 %copy-start = (bf16[1568,768]{1,0:T(8,128)(2,1)S(1)}, bf16[1568,768]{1,0:T(8,128)(2,1)}, u32[]{:S(2)}) copy-start(bf16[1568,768]{1,0:T(8,128)(2,1)} %get-tuple-element.163) | copy-start | bytes 7225348
  359.3 5.0 %copy-start.1 = (f32[2,3,48,384]{3,2,1,0:T(8,128)S(1)}, f32[2,3,48,384]{3,2,1,0:T(8,128)}, u32[]{:S(2)}) copy-start(f32[2,3,48,384]{3,2,1,0:T(8,128)} %get-tuple-element.126) | copy-start | bytes 1327108
  359.3 5.8 %copy-start.4 = (f32[2,48,384]{2,1,0:T(8,128)S(1)}, f32[2,48,384]{2,1,0:T(8,128)}, u32[]{:S(2)}) copy-start(f32[2,48,384]{2,1,0:T(8,128)} %get-tuple-element.127) | copy-start | bytes 442372
  359.3 6.4 %copy-start.3 = (f32[48,1536]{1,0:T(8,128)S(1)}, f32[48,1536]{1,0:T(8,128)}, u32[]{:S(2)}) copy-start(f32[48,1536]{1,0:T(8,128)} %get-tuple-element.128) | copy-start | bytes 884740
  359.3 7.1 %copy-start.2 = (f32[48,1536]{1,0:T(8,128)S(1)}, f32[48,1536]{1,0:T(8,128)}, u32[]{:S(2)}) copy-start(f32[48,1536]{1,0:T(8,128)} %get-tuple-element.129) | copy-start | bytes 884740
  359.3 7.9 %copy-start.7 = (f32[1,96]{1,0:T(1,128)S(1)}, f32[1,96]{1,0:T(1,128)}, u32[]{:S(2)}) copy-start(f32[1,96]{1,0:T(1,128)} %get-tuple-element.171) | copy-start | bytes 1156
